TPU v7x, 512 devices: a whole 4x4x16 slice. The times are simulated.
512 devices in a mesh: dp: 16 (over z_lo, x), fsdp: 32 (over y, z_hi, core).
Axes of the slice: x: 4, y: 4, z: 16 (z_hi: 4, z_lo: 4; z = z_hi * 4 + z_lo), core: 2. Of those that a mesh axis runs over, the one named last changes fastest.
Arguments:
- normed_input: bfloat16 [65536, 8192], P(('dp', 'fsdp')), may hold values from -6 to 6
- value_cotangent: bfloat16 [65536, 1024], P(('dp', 'fsdp')), may hold values from -6 to 6
- basis: bfloat16 [8192, 512], P('fsdp'), may hold values from -0.25 to 0.25
- first_moment: float32 [512, 1024], P(('dp', 'fsdp')), may hold values from -6 to 6
- second_moment: float32 [512, 1024], P(('dp', 'fsdp')), may hold values from 1 to 30
Outputs:
- new_first_moment: float32 [512, 1024], P(('dp', 'fsdp'))
- new_second_moment: float32 [512, 1024], P(('dp', 'fsdp'))
- value_update: bfloat16 [8192, 1024], P('fsdp')
All inputs are finite; a program needn't handle non-finite values.
Results may differ from a plain program's by a relative error of at most 0.0049.
The roundings to bfloat16 on the way count: a program that leaves them out, or rounds other values in their place, can miss the bound.
Values may be sent and summed in bfloat16 or wider, within the bound.
No kernel may reach another device: no remote copies, remote signals or barrier semaphores. Data moves between devices by JAX's collectives and lax.ppermute only.
A program may use at most 64 MiB of HBM per device.

v0:
```python
import math

import jax
import jax.numpy as jnp
from jax import lax
from jax.sharding import PartitionSpec as P

STEP = 1000


beta_first = 0.9
beta_second = 0.999
adam_epsilon = 1e-08


def contract_lead(left, right):
    return lax.dot_general(left, right, (((0,), (0,)), ((), ())), precision=lax.Precision.HIGHEST)


def local(normed_input, value_cotangent, basis, first_moment, second_moment):
    group_devices = lax.axis_size("dp") * lax.axis_size("fsdp")
    tokens_all = normed_input.shape[0] * group_devices
    scale_factor = 1.0 / math.sqrt(tokens_all)
    reduced = jnp.dot(
        normed_input,
        lax.all_gather(basis, "fsdp", axis=0, tiled=True),
        preferred_element_type=jnp.float32,
    )
    cotangent_float = value_cotangent.astype(jnp.float32)
    share = lax.psum_scatter(
        contract_lead(reduced, cotangent_float) * scale_factor,
        ("dp", "fsdp"),
        scatter_dimension=0,
        tiled=True,
    )
    new_first = beta_first * first_moment + (1.0 - beta_first) * share
    new_second = beta_second * second_moment + (1.0 - beta_second) * share * share
    corr_first = 1.0 - beta_first**STEP
    corr_second = 1.0 - beta_second**STEP
    normalized = (
        new_first / corr_first / (jnp.sqrt(new_second / corr_second) + adam_epsilon)
    ).astype(jnp.bfloat16)
    all_normalized = lax.all_gather(normalized, ("dp", "fsdp"), axis=0, tiled=True)
    value_update = jnp.dot(basis, all_normalized, preferred_element_type=jnp.float32).astype(
        jnp.bfloat16
    )
    return (new_first, new_second, value_update)


def solution(mesh):
    return jax.shard_map(
        local,
        mesh=mesh,
        in_specs=(
            P(("dp", "fsdp"), None),
            P(("dp", "fsdp"), None),
            P("fsdp", None),
            P(("dp", "fsdp"), None),
            P(("dp", "fsdp"), None),
        ),
        out_specs=(P(("dp", "fsdp"), None), P(("dp", "fsdp"), None), P("fsdp", None)),
        check_vma=False,
    )
```

profile of v0, /device:TPU:1, one launch (start us, length us, event | category | flops | bytes accessed | tf_op | source)
XLA Modules:
  0.0 1403.3 jit_solution(6200577338157344408)
XLA Ops:
  7.2 0.0 copy-start
  7.2 0.0 all-gather.4.cloned.1.call-start
  7.2 0.7 all-gather.4.cloned.1.call-update
  7.9 0.0 copy-start.1
  7.9 0.0 all-reduce.3.cloned.1.call-start
  8.0 144.1 %all-gather.4.cloned.1.call-done = bf16[8192,512]{1,0:T(8,128)(2,1)} async-done(((bf16[256,512]{1,0:T(8,128)(2,1)}), bf16[8192,512]{1,0:T(8,128)(2,1)}) %all-gather.4.cloned.1.call-update) | async-done | bytes 8388624 | tf_op jit(solution)/shard_map/all_gather | solution.py:26
  152.1 0.0 copy-done
  152.1 4.6 fusion.5
  156.8 0.0 copy-done.1
  156.8 0.0 copy-start.3
  156.8 0.0 copy-start.4
  156.8 0.0 copy-start.2
  156.8 2.3 convolution_multiply_fusion
  159.1 0.0 all-reduce.3.cloned.1.call-update
  159.2 0.0 all-gather.6.cloned.1.call-start
  159.2 471.3 %all-reduce.3.cloned.1.call-done = f32[512,1024]{1,0:T(8,128)} async-done(((f32[512,1024]{1,0:T(8,128)}), f32[512,1024]{1,0:T(8,128)}) %all-reduce.3.cloned.1.call-update) | async-done | bytes 2097168
  630.5 0.0 copy-done.3
  630.5 0.0 copy-done.4
  630.5 1.4 convert_bitcast_fusion
  631.9 0.0 all-gather.6.cloned.1.call-update
  631.9 761.5 %all-gather.6.cloned.1.call-done = bf16[512,1,1024]{2,1,0:T(2,128)(2,1)} async-done(((bf16[1,1,1024]{2,1,0:T(2,128)(2,1)}), bf16[512,1,1024]{2,1,0:T(2,128)(2,1)}) %all-gather.6.cloned.1.call-update) | async-done | bytes 1048592 | tf_op jit(solution)/shard_map/all_gather | solution.py:43
  1393.4 0.0 copy-done.2
  1393.4 2.4 fusion
  1395.8 1.0 copy.10
Async XLA Ops:
  7.2 144.9 %copy-start = (bf16[128,8192]{1,0:T(8,128)(2,1)S(1)}, bf16[128,8192]{1,0:T(8,128)(2,1)}, u32[]{:S(2)}) copy-start(bf16[128,8192]{1,0:T(8,128)(2,1)} %param.5) | copy-start | bytes 6291460
  7.2 144.9 %all-gather.4.cloned.1.call-start = ((), (), s32[]{:S(2)}) async-start(), calls=%async_computation | async-start | bytes 8650752 | tf_op jit(solution)/shard_map/all_gather | solution.py:26
  7.9 148.8 %copy-start.1 = (bf16[128,1024]{1,0:T(8,128)(2,1)S(1)}, bf16[128,1024]{1,0:T(8,128)(2,1)}, u32[]{:S(2)}) copy-start(bf16[128,1024]{1,0:T(8,128)(2,1)} %param.6) | copy-start | bytes 786436
  7.9 622.6 %all-reduce.3.cloned.1.call-start = ((), (), s32[]{:S(2)}) async-start(), calls=%async_computation.2 | async-start | bytes 4194304
  156.8 473.7 %copy-start.3 = (f32[1,1024]{1,0:T(1,128)S(1)}, f32[1,1024]{1,0:T(1,128)}, u32[]{:S(2)}) copy-start(f32[1,1024]{1,0:T(1,128)} %param.9) | copy-start | bytes 12292
  156.8 473.7 %copy-start.4 = (f32[1,1024]{1,0:T(1,128)S(1)}, f32[1,1024]{1,0:T(1,128)}, u32[]{:S(2)}) copy-start(f32[1,1024]{1,0:T(1,128)} %param.8) | copy-start | bytes 12292
  156.8 1236.6 %copy-start.2 = (bf16[256,512]{1,0:T(8,128)(2,1)S(1)}, bf16[256,512]{1,0:T(8,128)(2,1)}, u32[]{:S(2)}) copy-start(bf16[256,512]{1,0:T(8,128)(2,1)} %param.7) | copy-start | bytes 786436
  159.2 1234.2 %all-gather.6.cloned.1.call-start = ((), (), s32[]{:S(2)}) async-start(), calls=%async_computation.1 | async-start | bytes 2101248 | tf_op jit(solution)/shard_map/all_gather | solution.py:43
Sparse Core Ops, SparseCore 0:
  11.1 140.9 all-gather.3
  159.3 471.1 all-reduce.2
  633.2 760.1 all-gather.5
where the time goes:
time: 1400 us
  waiting for transfers between devices  1380 us (99%)
    all_gather x1, waiting for transfers between devices, local(): lax.all_gather(normalized, ('dp', 'fsdp'), axis=0, tiled=True)  761 us
    unnamed x4, waiting for transfers between devices  472 us
    all_gather x1, waiting for transfers between devices, local(): lax.all_gather(basis, 'fsdp', axis=0, tiled=True)  144 us
  transfers between devices with their start and end apart: 3, of which 3 were waited for; matrix products, arithmetic and copies ran while one was open for 0% of the time, Pallas kernels for 0%

commit v1 on v0

v1 whole, which is shorter than its diff:
```python
import math

import jax
import jax.numpy as jnp
from jax import lax
from jax.sharding import Mesh
from jax.sharding import PartitionSpec as P

STEP = 1000

beta_first = 0.9
beta_second = 0.999
adam_epsilon = 1e-08

AXES = ("z_lo", "x", "y", "z_hi", "core")
Z = ("z_hi", "z_lo")
RANK = 512
TOKENS = 65536


def owner_row(core, xy, z):
    x, y = xy // 4, xy % 4
    z_hi, z_lo = z // 4, z % 4
    return (((z_lo * 4 + x) * 4 + y) * 4 + z_hi) * 2 + core


def reorder(basis, rows):
    pick = (lax.broadcasted_iota(jnp.int32, (RANK, RANK), 0) == rows[None, :]).astype(jnp.bfloat16)
    return jnp.dot(basis, pick, preferred_element_type=jnp.float32).astype(jnp.bfloat16)


def shifts(block, axis):
    return [block] + [
        lax.ppermute(block, axis, [(i, (i + k) % 4) for i in range(4)]) for k in (1, 2, 3)
    ]


def ordered(parts, index):
    stacked = jnp.stack(parts)
    return jnp.take(stacked, (index - jnp.arange(4)) % 4, axis=0)


def local(normed_input, value_cotangent, basis, first_moment, second_moment):
    x_at, y_at, z_lo_at = lax.axis_index("x"), lax.axis_index("y"), lax.axis_index("z_lo")
    place = jnp.arange(RANK)
    with jax.named_scope("order"):
        ranked = reorder(basis, owner_row(place // 256, place // 16 % 16, place % 16))
        decoder = reorder(basis, owner_row(place // 16 % 2, place // 32, place % 16))
    with jax.named_scope("swap_tokens"):
        swap = [(0, 1), (1, 0)]
        other_input = lax.ppermute(normed_input, "core", swap)
        other_cotangent = lax.ppermute(value_cotangent, "core", swap)
    with jax.named_scope("gather_z"):
        mine = lax.dynamic_slice_in_dim(ranked, (x_at * 4 + z_lo_at) * 16, 16, 0)
        halves = jnp.stack([mine[:, :256], mine[:, 256:]])
        line = lax.all_to_all(
            jnp.broadcast_to(halves[None], (16, 2, 16, 256)).reshape(32, 16, 256),
            ("z_hi", "z_lo", "core"), 0, 0, tiled=True,
        ).reshape(4, 4, 2, 16, 256)
        lower, upper = line[:, :, 0], line[:, :, 1]
    with jax.named_scope("gather_xy"):
        lower_x = shifts(lower, "x")
        upper_y = shifts(upper, "y")
        lower_x = ordered(lower_x, x_at)
        upper_y = ordered(upper_y, y_at)
    with jax.named_scope("gather_yx"):
        lower_xy = shifts(lower_x, "y")
        upper_xy = shifts(upper_y, "x")
        lower_all = ordered(lower_xy, y_at).transpose(0, 2, 1, 3, 4, 5).reshape(4, 4, 256, 256)
        upper_all = ordered(upper_xy, x_at).transpose(1, 2, 0, 3, 4, 5).reshape(4, 4, 256, 256)
    with jax.named_scope("project"):
        whole = jnp.stack([lower_all, upper_all], axis=2).reshape(8192, 256)

        def term(tokens, cotangent):
            reduced = jnp.dot(tokens, whole, preferred_element_type=jnp.float32)
            high = lax.reduce_precision(reduced, 8, 7)
            low = (reduced - high).astype(jnp.bfloat16)
            both = jnp.concatenate([high.astype(jnp.bfloat16), low], axis=0)
            twice = jnp.concatenate([cotangent, cotangent], axis=0)
            return lax.dot_general(
                both, twice, (((0,), (0,)), ((), ())), preferred_element_type=jnp.float32
            )

        partial = term(normed_input, value_cotangent) + term(other_input, other_cotangent)
    with jax.named_scope("reduce_xy"):
        parts = lax.all_to_all(partial.reshape(16, 16, 1024), ("x", "y"), 0, 0, tiled=True)
        summed = jnp.sum(parts, axis=0)
    with jax.named_scope("reduce_z"):
        parts = lax.all_to_all(summed.reshape(16, 8, 128), Z, 0, 0, tiled=True)
        share = jnp.sum(parts, axis=0) * (1.0 / math.sqrt(TOKENS))
    with jax.named_scope("adam"):
        first, second = first_moment.reshape(8, 128), second_moment.reshape(8, 128)
        new_first = beta_first * first + (1.0 - beta_first) * share
        new_second = beta_second * second + (1.0 - beta_second) * share * share
        corr_first = 1.0 - beta_first**STEP
        corr_second = 1.0 - beta_second**STEP
        normalized = (
            new_first / corr_first / (jnp.sqrt(new_second / corr_second) + adam_epsilon)
        ).astype(jnp.bfloat16)
    with jax.named_scope("spread_z"):
        column = lax.all_gather(normalized, Z, axis=0, tiled=False).reshape(16, 1024)
    with jax.named_scope("spread_xy"):
        step = lax.all_to_all(
            jnp.broadcast_to(column[None], (32, 16, 1024)), ("x", "y", "core"), 0, 0, tiled=True
        ).reshape(RANK, 1024)
    with jax.named_scope("decode"):
        update = jnp.dot(decoder, step, preferred_element_type=jnp.float32).astype(jnp.bfloat16)
    return new_first.reshape(1, 1024), new_second.reshape(1, 1024), update


def solution(mesh):
    fine = Mesh(mesh.devices.reshape(4, 4, 4, 4, 2), AXES)
    weights = P(("y", "z_hi", "core"), None)
    return jax.shard_map(
        local,
        mesh=fine,
        in_specs=(P(AXES, None), P(AXES, None), weights, P(AXES, None), P(AXES, None)),
        out_specs=(P(AXES, None), P(AXES, None), weights),
        check_vma=False,
    )
```

time: 1400 us -> 222 us (0.16)
  waiting for transfers between devices: 1380 us -> 46.3 us
  starting transfers between devices: 0.12 us -> 80.6 us
  blocking collectives: 0 us -> 62.4 us
    all_gather x2 -> x0, waiting for transfers between devices: 906 us -> none  [the longest x1 761 us: local(): lax.all_gather(normalized, ('dp', 'fsdp'), axis=0, tiled=True)]
    unnamed x4 -> x0, waiting for transfers between devices: 472 us -> none
    ppermute x0 -> x14, starting transfers between devices: none -> 49.8 us  [the longest x12 36.7 us: shifts(): lax.ppermute(block, axis, [(i, (i + k) % 4) for i in range(4)])]
    all_to_all x0 -> x2, blocking collectives: none -> 41.7 us  [the longest x1 22.9 us: local(): lax.all_to_all(partial.reshape(16, 16, 1024), ('x', 'y'), 0, 0, tiled=True)]
    all_to_all x0 -> x2, waiting for transfers between devices: none -> 38.8 us  [the longest x1 21.9 us: local(): lax.all_to_all(jnp.broadcast_to(halves[None], (16, 2, 16, 256)).reshape(3...]
    all_to_all x0 -> x2, starting transfers between devices: none -> 30.9 us  [the longest x1 16.8 us: local(): lax.all_to_all(jnp.broadcast_to(halves[None], (16, 2, 16, 256)).reshape(3...]
    all_gather x0 -> x1, blocking collectives: none -> 20.7 us  [local(): lax.all_gather(normalized, Z, axis=0, tiled=False).reshape(16, 1024)]
  transfers between devices with their start and end apart: 3 -> 16, of which waited for: 3 -> 4; matrix products, arithmetic and copies ran while one was open for 0% -> 10% of each run, Pallas kernels for 0% -> 0%
where the time goes in v1:
time: 222 us; the launch traced here: 221 us
  starting transfers between devices  80.6 us (36%)
  blocking collectives  62.4 us (28%)
  waiting for transfers between devices  46.3 us (21%)
  local copies, waits for them, and re-layouts  11.6 us (5%)
  matrix products  9.71 us (4%)
  other arithmetic  9.54 us (4%)
    ppermute x12, starting transfers between devices, shifts(): lax.ppermute(block, axis, [(i, (i + k) % 4) for i in range(4)])  36.7 us
    all_to_all x1, blocking collectives, local(): lax.all_to_all(partial.reshape(16, 16, 1024), ('x', 'y'), 0, 0, tiled=True)  22.9 us
    all_to_all x1, waiting for transfers between devices, local(): lax.all_to_all(jnp.broadcast_to(halves[None], (16, 2, 16, 256)).reshape(3...  21.9 us
    all_gather x1, blocking collectives, local(): lax.all_gather(normalized, Z, axis=0, tiled=False).reshape(16, 1024)  20.7 us
    all_to_all x1, blocking collectives, local(): parts = lax.all_to_all(summed.reshape(16, 8, 128), Z, 0, 0, tiled=True)  18.8 us
    all_to_all x1, waiting for transfers between devices, local(): lax.all_to_all(jnp.broadcast_to(column[None], (32, 16, 1024)), ('x', 'y',...  16.9 us
    all_to_all x1, starting transfers between devices, local(): lax.all_to_all(jnp.broadcast_to(halves[None], (16, 2, 16, 256)).reshape(3...  16.8 us
    all_to_all x1, starting transfers between devices, local(): lax.all_to_all(jnp.broadcast_to(column[None], (32, 16, 1024)), ('x', 'y',...  14.1 us
  transfers between devices with their start and end apart: 16, of which 4 were waited for; matrix products, arithmetic and copies ran while one was open for 10% of the time, Pallas kernels for 0%

profile of v1, /device:TPU:1, one launch (start us, length us, event | category | flops | bytes accessed | tf_op | source)
XLA Modules:
  0.0 221.3 jit_solution(7984424715170966024)
XLA Ops:
  2.7 16.8 %all-to-all-start = ((bf16[32,16,256]{2,1,0:T(8,128)(2,1)}), bf16[32,16,256]{2,1,0:T(8,128)(2,1)S(1)}, u32[]{:S(2)}, u32[]{:S(2)}) async-start(bf16[32,16,256]{2,1,0:T(8,128)(2,1)} %bitcast.3), calls=%async_computation | async-start | bytes 524288 | tf_op jit(solution)/shard_map/gather_z/all_to_all | solution.py:56
  19.6 21.9 %all-to-all-done = bf16[32,16,256]{2,1,0:T(8,128)(2,1)S(1)} async-done(((bf16[32,16,256]{2,1,0:T(8,128)(2,1)}), bf16[32,16,256]{2,1,0:T(8,128)(2,1)S(1)}, u32[]{:S(2)}, u32[]{:S(2)}) %all-to-all-start) | async-done | bytes 262176 | tf_op jit(solution)/shard_map/gather_z/all_to_all | solution.py:56
  41.5 3.1 %collective-permute-start = (bf16[4,4,16,256]{3,2,1,0:T(8,128)(2,1)S(1)}, bf16[4,4,16,256]{3,2,1,0:T(8,128)(2,1)S(1)}, u32[]{:S(2)}, u32[]{:S(2)}) collective-permute-start(bf16[4,4,16,256]{3,2,1,0:T(8,128)(2,1)S(1)} %get-tuple-element.6), channel_id=1, source_target_pairs={{0,32},{32,64},{64,96},{96,0},{1,33},{33,65},{65,97},{97,1},{2,34}... | collective-permute-start | bytes 393224 | tf_op jit(solution)/shard_map/gather_xy/ppermute | solution.py:34
  44.7 4.4 %collective-permute-start.1 = (bf16[4,4,16,256]{3,2,1,0:T(8,128)(2,1)S(1)}, bf16[4,4,16,256]{3,2,1,0:T(8,128)(2,1)S(1)}, u32[]{:S(2)}, u32[]{:S(2)}) collective-permute-start(bf16[4,4,16,256]{3,2,1,0:T(8,128)(2,1)S(1)} %get-tuple-element.6), channel_id=1, source_target_pairs={{0,64},{32,96},{64,0},{96,32},{1,65},{33,97},{65,1},{97,33},{2,66}... | collective-permute-start | bytes 393224 | tf_op jit(solution)/shard_map/gather_xy/ppermute | solution.py:34
  49.0 3.1 %collective-permute-start.2 = (bf16[4,4,16,256]{3,2,1,0:T(8,128)(2,1)S(1)}, bf16[4,4,16,256]{3,2,1,0:T(8,128)(2,1)S(1)}, u32[]{:S(2)}, u32[]{:S(2)}) collective-permute-start(bf16[4,4,16,256]{3,2,1,0:T(8,128)(2,1)S(1)} %get-tuple-element.6), channel_id=1, source_target_pairs={{0,96},{32,0},{64,32},{96,64},{1,97},{33,1},{65,33},{97,65},{2,98}... | collective-permute-start | bytes 393224 | tf_op jit(solution)/shard_map/gather_xy/ppermute | solution.py:34
  52.1 3.2 %collective-permute-start.6 = (bf16[4,4,16,256]{3,2,1,0:T(8,128)(2,1)S(1)}, bf16[4,4,16,256]{3,2,1,0:T(8,128)(2,1)S(1)}, u32[]{:S(2)}, u32[]{:S(2)}) collective-permute-start(bf16[4,4,16,256]{3,2,1,0:T(8,128)(2,1)S(1)} %get-tuple-element.7), channel_id=1, source_target_pairs={{0,8},{8,16},{16,24},{24,0},{1,9},{9,17},{17,25},{25,1},{2,10},{10... | collective-permute-start | bytes 393224 | tf_op jit(solution)/shard_map/gather_xy/ppermute | solution.py:34
  55.3 4.5 %collective-permute-start.7 = (bf16[4,4,16,256]{3,2,1,0:T(8,128)(2,1)S(1)}, bf16[4,4,16,256]{3,2,1,0:T(8,128)(2,1)S(1)}, u32[]{:S(2)}, u32[]{:S(2)}) collective-permute-start(bf16[4,4,16,256]{3,2,1,0:T(8,128)(2,1)S(1)} %get-tuple-element.7), channel_id=1, source_target_pairs={{0,16},{8,24},{16,0},{24,8},{1,17},{9,25},{17,1},{25,9},{2,18},{10... | collective-permute-start | bytes 393224 | tf_op jit(solution)/shard_map/gather_xy/ppermute | solution.py:34
  59.9 3.0 %collective-permute-start.8 = (bf16[4,4,16,256]{3,2,1,0:T(8,128)(2,1)S(1)}, bf16[4,4,16,256]{3,2,1,0:T(8,128)(2,1)S(1)}, u32[]{:S(2)}, u32[]{:S(2)}) collective-permute-start(bf16[4,4,16,256]{3,2,1,0:T(8,128)(2,1)S(1)} %get-tuple-element.7), channel_id=1, source_target_pairs={{0,24},{8,0},{16,8},{24,16},{1,25},{9,1},{17,9},{25,17},{2,26},{10... | collective-permute-start | bytes 393224 | tf_op jit(solution)/shard_map/gather_xy/ppermute | solution.py:34
  63.7 2.3 %collective-permute-start.3 = (bf16[4,4,4,16,256]{4,3,2,1,0:T(8,128)(2,1)S(1)}, bf16[4,4,4,16,256]{4,3,2,1,0:T(8,128)(2,1)}, u32[]{:S(2)}, u32[]{:S(2)}) collective-permute-start(bf16[4,4,4,16,256]{4,3,2,1,0:T(8,128)(2,1)S(1)} %broadcast_select_fusion.1), channel_id=1, source_target_pairs={{0,8},{8,16},{16,24},{24,0},{1,9},{9,17},{17,25},{25,1},{2,10},{10... | collective-permute-start | bytes 1572872 | tf_op jit(solution)/shard_map/gather_yx/ppermute | solution.py:34
  66.0 2.7 %collective-permute-start.4 = (bf16[4,4,4,16,256]{4,3,2,1,0:T(8,128)(2,1)S(1)}, bf16[4,4,4,16,256]{4,3,2,1,0:T(8,128)(2,1)}, u32[]{:S(2)}, u32[]{:S(2)}) collective-permute-start(bf16[4,4,4,16,256]{4,3,2,1,0:T(8,128)(2,1)S(1)} %broadcast_select_fusion.1), channel_id=1, source_target_pairs={{0,16},{8,24},{16,0},{24,8},{1,17},{9,25},{17,1},{25,9},{2,18},{10... | collective-permute-start | bytes 1572872 | tf_op jit(solution)/shard_map/gather_yx/ppermute | solution.py:34
  68.8 4.9 %collective-permute-start.12 = (bf16[128,8192]{1,0:T(8,128)(2,1)}, bf16[128,8192]{1,0:T(8,128)(2,1)}, u32[]{:S(2)}, u32[]{:S(2)}) collective-permute-start(bf16[128,8192]{1,0:T(8,128)(2,1)} %param.9), channel_id=1, source_target_pairs={{0,1},{1,0},{2,3},{3,2},{4,5},{5,4},{6,7},{7,6},{8,9},{9,8},{10,11... | collective-permute-start | bytes 6291464 | tf_op jit(solution)/shard_map/swap_tokens/ppermute | solution.py:51
  73.7 3.5 %collective-permute-start.5 = (bf16[4,4,4,16,256]{4,3,2,1,0:T(8,128)(2,1)S(1)}, bf16[4,4,4,16,256]{4,3,2,1,0:T(8,128)(2,1)}, u32[]{:S(2)}, u32[]{:S(2)}) collective-permute-start(bf16[4,4,4,16,256]{4,3,2,1,0:T(8,128)(2,1)S(1)} %broadcast_select_fusion.1), channel_id=1, source_target_pairs={{0,24},{8,0},{16,8},{24,16},{1,25},{9,1},{17,9},{25,17},{2,26},{10... | collective-permute-start | bytes 1572872 | tf_op jit(solution)/shard_map/gather_yx/ppermute | solution.py:34
  78.8 2.2 collective-permute-start.9
  81.1 2.5 %collective-permute-start.10 = (bf16[4,4,4,16,256]{4,3,2,1,0:T(8,128)(2,1)}, bf16[4,4,4,16,256]{4,3,2,1,0:T(8,128)(2,1)}, u32[]{:S(2)}, u32[]{:S(2)}) collective-permute-start(bf16[4,4,4,16,256]{4,3,2,1,0:T(8,128)(2,1)} %broadcast_select_fusion), channel_id=1, source_target_pairs={{0,64},{32,96},{64,0},{96,32},{1,65},{33,97},{65,1},{97,33},{2,66}... | collective-permute-start | bytes 1572872 | tf_op jit(solution)/shard_map/gather_yx/ppermute | solution.py:34
  83.6 4.1 %collective-permute-done.4 = bf16[4,4,4,16,256]{4,3,2,1,0:T(8,128)(2,1)} collective-permute-done((bf16[4,4,4,16,256]{4,3,2,1,0:T(8,128)(2,1)S(1)}, bf16[4,4,4,16,256]{4,3,2,1,0:T(8,128)(2,1)}, u32[]{:S(2)}, u32[]{:S(2)}) %collective-permute-start.4) | collective-permute-done | bytes 524320 | tf_op jit(solution)/shard_map/gather_yx/ppermute | solution.py:34
  90.0 3.4 %collective-permute-done.5 = bf16[4,4,4,16,256]{4,3,2,1,0:T(8,128)(2,1)} collective-permute-done((bf16[4,4,4,16,256]{4,3,2,1,0:T(8,128)(2,1)S(1)}, bf16[4,4,4,16,256]{4,3,2,1,0:T(8,128)(2,1)}, u32[]{:S(2)}, u32[]{:S(2)}) %collective-permute-start.5) | collective-permute-done | bytes 524320 | tf_op jit(solution)/shard_map/gather_yx/ppermute | solution.py:34
  93.4 8.2 %collective-permute-start.13 = (bf16[128,1024]{1,0:T(8,128)(2,1)}, bf16[128,1024]{1,0:T(8,128)(2,1)}, u32[]{:S(2)}, u32[]{:S(2)}) collective-permute-start(bf16[128,1024]{1,0:T(8,128)(2,1)} %param.10), channel_id=1, source_target_pairs={{0,1},{1,0},{2,3},{3,2},{4,5},{5,4},{6,7},{7,6},{8,9},{9,8},{10,11... | collective-permute-start | bytes 786440 | tf_op jit(solution)/shard_map/swap_tokens/ppermute | solution.py:52
  116.6 2.4 %reduce-precision_convert_fusion.1 = (bf16[128,256]{1,0:T(8,128)(2,1)S(1)}, bf16[128,256]{1,0:T(8,128)(2,1)S(1)}) fusion(bf16[128,8192]{1,0:T(8,128)(2,1)} %param.9, bf16[8192,256]{1,0:T(8,128)(2,1)S(1)} %bitcast.80), kind=kOutput, calls=%fused_computation.34 | convolution fusion | flops 537001984 | bytes 6422528 | tf_op jit(solution)/shard_map/project/dot_general | solution.py:75
  120.4 2.4 %reduce-precision_convert_fusion = (bf16[128,256]{1,0:T(8,128)(2,1)S(1)}, bf16[128,256]{1,0:T(8,128)(2,1)S(1)}) fusion(bf16[128,8192]{1,0:T(8,128)(2,1)} %collective-permute-done.12, bf16[8192,256]{1,0:T(8,128)(2,1)S(1)} %bitcast.81), kind=kOutput, calls=%fused_computation.32 | convolution fusion | flops 537001984 | bytes 6422528 | tf_op jit(solution)/shard_map/project/dot_general | solution.py:75
  124.1 22.9 %all_to_all.20 = f32[16,16,1024]{2,1,0:T(8,128)S(1)} all-to-all(f32[16,16,1024]{2,1,0:T(8,128)S(1)} %bitcast.84), channel_id=1, replica_groups=mesh['z_lo'=4,'x'=4,'y'=4,'z_hi'=4,'core'=2] {'x','y'}, dimensions={0} | all-to-all | bytes 2097152 | tf_op jit(solution)/shard_map/reduce_xy/all_to_all | solution.py:86
  147.1 18.8 %all_to_all.21 = f32[16,8,128]{2,1,0:T(8,128)S(1)} all-to-all(f32[16,8,128]{2,1,0:T(8,128)S(1)} %bitcast.88), channel_id=1, replica_groups=mesh['z_lo'=4,'x'=4,'y'=4,'z_hi'=4,'core'=2] {'z_hi','z_lo'}, dimensions={0} | all-to-all | bytes 131072 | tf_op jit(solution)/shard_map/reduce_z/all_to_all | solution.py:89
  166.6 20.7 %all_gather.4 = bf16[16,8,128]{2,1,0:T(8,128)(2,1)S(1)} all-gather(bf16[1,8,128]{2,1,0:T(8,128)(2,1)S(1)} %fusion.31), channel_id=1, replica_groups=mesh['z_lo'=4,'x'=4,'y'=4,'z_hi'=4,'core'=2] {'z_hi','z_lo'}, dimensions={0}, use_global_device_ids=true | all-gather | bytes 34816 | tf_op jit(solution)/shard_map/spread_z/all_gather | solution.py:101
  188.4 14.1 %all-to-all-start.3 = ((bf16[32,16,1024]{2,1,0:T(8,128)(2,1)}), bf16[32,16,1024]{2,1,0:T(8,128)(2,1)S(1)}, u32[]{:S(2)}, u32[]{:S(2)}) async-start(bf16[32,16,1024]{2,1,0:T(8,128)(2,1)} %broadcast_in_dim.35), calls=%async_computation.3 | async-start | bytes 2097152 | tf_op jit(solution)/shard_map/spread_xy/all_to_all | solution.py:103
  202.5 16.9 %all-to-all-done.3 = bf16[32,16,1024]{2,1,0:T(8,128)(2,1)S(1)} async-done(((bf16[32,16,1024]{2,1,0:T(8,128)(2,1)}), bf16[32,16,1024]{2,1,0:T(8,128)(2,1)S(1)}, u32[]{:S(2)}, u32[]{:S(2)}) %all-to-all-start.3) | async-done | bytes 1048608 | tf_op jit(solution)/shard_map/spread_xy/all_to_all | solution.py:103
  (64 shorter events, 28.3 us)
Async XLA Ops:
  0.6 1.0 copy-start
  2.7 38.8 %all-to-all-start = ((bf16[32,16,256]{2,1,0:T(8,128)(2,1)}), bf16[32,16,256]{2,1,0:T(8,128)(2,1)S(1)}, u32[]{:S(2)}, u32[]{:S(2)}) async-start(bf16[32,16,256]{2,1,0:T(8,128)(2,1)} %bitcast.3), calls=%async_computation | async-start | bytes 524288 | tf_op jit(solution)/shard_map/gather_z/all_to_all | solution.py:56
  41.5 18.3 %collective-permute-start = (bf16[4,4,16,256]{3,2,1,0:T(8,128)(2,1)S(1)}, bf16[4,4,16,256]{3,2,1,0:T(8,128)(2,1)S(1)}, u32[]{:S(2)}, u32[]{:S(2)}) collective-permute-start(bf16[4,4,16,256]{3,2,1,0:T(8,128)(2,1)S(1)} %get-tuple-element.6), channel_id=1, source_target_pairs={{0,32},{32,64},{64,96},{96,0},{1,33},{33,65},{65,97},{97,1},{2,34}... | collective-permute-start | bytes 393224 | tf_op jit(solution)/shard_map/gather_xy/ppermute | solution.py:34
  44.7 18.2 %collective-permute-start.1 = (bf16[4,4,16,256]{3,2,1,0:T(8,128)(2,1)S(1)}, bf16[4,4,16,256]{3,2,1,0:T(8,128)(2,1)S(1)}, u32[]{:S(2)}, u32[]{:S(2)}) collective-permute-start(bf16[4,4,16,256]{3,2,1,0:T(8,128)(2,1)S(1)} %get-tuple-element.6), channel_id=1, source_target_pairs={{0,64},{32,96},{64,0},{96,32},{1,65},{33,97},{65,1},{97,33},{2,66}... | collective-permute-start | bytes 393224 | tf_op jit(solution)/shard_map/gather_xy/ppermute | solution.py:34
  49.0 13.9 %collective-permute-start.2 = (bf16[4,4,16,256]{3,2,1,0:T(8,128)(2,1)S(1)}, bf16[4,4,16,256]{3,2,1,0:T(8,128)(2,1)S(1)}, u32[]{:S(2)}, u32[]{:S(2)}) collective-permute-start(bf16[4,4,16,256]{3,2,1,0:T(8,128)(2,1)S(1)} %get-tuple-element.6), channel_id=1, source_target_pairs={{0,96},{32,0},{64,32},{96,64},{1,97},{33,1},{65,33},{97,65},{2,98}... | collective-permute-start | bytes 393224 | tf_op jit(solution)/shard_map/gather_xy/ppermute | solution.py:34
  52.1 16.7 %collective-permute-start.6 = (bf16[4,4,16,256]{3,2,1,0:T(8,128)(2,1)S(1)}, bf16[4,4,16,256]{3,2,1,0:T(8,128)(2,1)S(1)}, u32[]{:S(2)}, u32[]{:S(2)}) collective-permute-start(bf16[4,4,16,256]{3,2,1,0:T(8,128)(2,1)S(1)} %get-tuple-element.7), channel_id=1, source_target_pairs={{0,8},{8,16},{16,24},{24,0},{1,9},{9,17},{17,25},{25,1},{2,10},{10... | collective-permute-start | bytes 393224 | tf_op jit(solution)/shard_map/gather_xy/ppermute | solution.py:34
  55.3 18.4 %collective-permute-start.7 = (bf16[4,4,16,256]{3,2,1,0:T(8,128)(2,1)S(1)}, bf16[4,4,16,256]{3,2,1,0:T(8,128)(2,1)S(1)}, u32[]{:S(2)}, u32[]{:S(2)}) collective-permute-start(bf16[4,4,16,256]{3,2,1,0:T(8,128)(2,1)S(1)} %get-tuple-element.7), channel_id=1, source_target_pairs={{0,16},{8,24},{16,0},{24,8},{1,17},{9,25},{17,1},{25,9},{2,18},{10... | collective-permute-start | bytes 393224 | tf_op jit(solution)/shard_map/gather_xy/ppermute | solution.py:34
  59.9 17.4 %collective-permute-start.8 = (bf16[4,4,16,256]{3,2,1,0:T(8,128)(2,1)S(1)}, bf16[4,4,16,256]{3,2,1,0:T(8,128)(2,1)S(1)}, u32[]{:S(2)}, u32[]{:S(2)}) collective-permute-start(bf16[4,4,16,256]{3,2,1,0:T(8,128)(2,1)S(1)} %get-tuple-element.7), channel_id=1, source_target_pairs={{0,24},{8,0},{16,8},{24,16},{1,25},{9,1},{17,9},{25,17},{2,26},{10... | collective-permute-start | bytes 393224 | tf_op jit(solution)/shard_map/gather_xy/ppermute | solution.py:34
  63.7 17.4 %collective-permute-start.3 = (bf16[4,4,4,16,256]{4,3,2,1,0:T(8,128)(2,1)S(1)}, bf16[4,4,4,16,256]{4,3,2,1,0:T(8,128)(2,1)}, u32[]{:S(2)}, u32[]{:S(2)}) collective-permute-start(bf16[4,4,4,16,256]{4,3,2,1,0:T(8,128)(2,1)S(1)} %broadcast_select_fusion.1), channel_id=1, source_target_pairs={{0,8},{8,16},{16,24},{24,0},{1,9},{9,17},{17,25},{25,1},{2,10},{10... | collective-permute-start | bytes 1572872 | tf_op jit(solution)/shard_map/gather_yx/ppermute | solution.py:34
  66.0 21.7 %collective-permute-start.4 = (bf16[4,4,4,16,256]{4,3,2,1,0:T(8,128)(2,1)S(1)}, bf16[4,4,4,16,256]{4,3,2,1,0:T(8,128)(2,1)}, u32[]{:S(2)}, u32[]{:S(2)}) collective-permute-start(bf16[4,4,4,16,256]{4,3,2,1,0:T(8,128)(2,1)S(1)} %broadcast_select_fusion.1), channel_id=1, source_target_pairs={{0,16},{8,24},{16,0},{24,8},{1,17},{9,25},{17,1},{25,9},{2,18},{10... | collective-permute-start | bytes 1572872 | tf_op jit(solution)/shard_map/gather_yx/ppermute | solution.py:34
  68.8 51.5 %collective-permute-start.12 = (bf16[128,8192]{1,0:T(8,128)(2,1)}, bf16[128,8192]{1,0:T(8,128)(2,1)}, u32[]{:S(2)}, u32[]{:S(2)}) collective-permute-start(bf16[128,8192]{1,0:T(8,128)(2,1)} %param.9), channel_id=1, source_target_pairs={{0,1},{1,0},{2,3},{3,2},{4,5},{5,4},{6,7},{7,6},{8,9},{9,8},{10,11... | collective-permute-start | bytes 6291464 | tf_op jit(solution)/shard_map/swap_tokens/ppermute | solution.py:51
  73.7 19.7 %collective-permute-start.5 = (bf16[4,4,4,16,256]{4,3,2,1,0:T(8,128)(2,1)S(1)}, bf16[4,4,4,16,256]{4,3,2,1,0:T(8,128)(2,1)}, u32[]{:S(2)}, u32[]{:S(2)}) collective-permute-start(bf16[4,4,4,16,256]{4,3,2,1,0:T(8,128)(2,1)S(1)} %broadcast_select_fusion.1), channel_id=1, source_target_pairs={{0,24},{8,0},{16,8},{24,16},{1,25},{9,1},{17,9},{25,17},{2,26},{10... | collective-permute-start | bytes 1572872 | tf_op jit(solution)/shard_map/gather_yx/ppermute | solution.py:34
  78.8 29.8 %collective-permute-start.9 = (bf16[4,4,4,16,256]{4,3,2,1,0:T(8,128)(2,1)}, bf16[4,4,4,16,256]{4,3,2,1,0:T(8,128)(2,1)}, u32[]{:S(2)}, u32[]{:S(2)}) collective-permute-start(bf16[4,4,4,16,256]{4,3,2,1,0:T(8,128)(2,1)} %broadcast_select_fusion), channel_id=1, source_target_pairs={{0,32},{32,64},{64,96},{96,0},{1,33},{33,65},{65,97},{97,1},{2,34}... | collective-permute-start | bytes 1572872 | tf_op jit(solution)/shard_map/gather_yx/ppermute | solution.py:34
  81.1 27.6 %collective-permute-start.10 = (bf16[4,4,4,16,256]{4,3,2,1,0:T(8,128)(2,1)}, bf16[4,4,4,16,256]{4,3,2,1,0:T(8,128)(2,1)}, u32[]{:S(2)}, u32[]{:S(2)}) collective-permute-start(bf16[4,4,4,16,256]{4,3,2,1,0:T(8,128)(2,1)} %broadcast_select_fusion), channel_id=1, source_target_pairs={{0,64},{32,96},{64,0},{96,32},{1,65},{33,97},{65,1},{97,33},{2,66}... | collective-permute-start | bytes 1572872 | tf_op jit(solution)/shard_map/gather_yx/ppermute | solution.py:34
  87.7 20.9 %collective-permute-start.11 = (bf16[4,4,4,16,256]{4,3,2,1,0:T(8,128)(2,1)}, bf16[4,4,4,16,256]{4,3,2,1,0:T(8,128)(2,1)}, u32[]{:S(2)}, u32[]{:S(2)}) collective-permute-start(bf16[4,4,4,16,256]{4,3,2,1,0:T(8,128)(2,1)} %broadcast_select_fusion), channel_id=1, source_target_pairs={{0,96},{32,0},{64,32},{96,64},{1,97},{33,1},{65,33},{97,65},{2,98}... | collective-permute-start | bytes 1572872 | tf_op jit(solution)/shard_map/gather_yx/ppermute | solution.py:34
  93.4 29.4 %collective-permute-start.13 = (bf16[128,1024]{1,0:T(8,128)(2,1)}, bf16[128,1024]{1,0:T(8,128)(2,1)}, u32[]{:S(2)}, u32[]{:S(2)}) collective-permute-start(bf16[128,1024]{1,0:T(8,128)(2,1)} %param.10), channel_id=1, source_target_pairs={{0,1},{1,0},{2,3},{3,2},{4,5},{5,4},{6,7},{7,6},{8,9},{9,8},{10,11... | collective-permute-start | bytes 786440 | tf_op jit(solution)/shard_map/swap_tokens/ppermute | solution.py:52
  114.1 1.6 copy-start.1
  124.1 41.8 %copy-start.2 = (f32[1,1024]{1,0:T(1,128)S(1)}, f32[1,1024]{1,0:T(1,128)}, u32[]{:S(2)}) copy-start(f32[1,1024]{1,0:T(1,128)} %param.13) | copy-start | bytes 12292
  124.1 41.8 %copy-start.3 = (f32[1,1024]{1,0:T(1,128)S(1)}, f32[1,1024]{1,0:T(1,128)}, u32[]{:S(2)}) copy-start(f32[1,1024]{1,0:T(1,128)} %param.12) | copy-start | bytes 12292
  188.4 31.0 %all-to-all-start.3 = ((bf16[32,16,1024]{2,1,0:T(8,128)(2,1)}), bf16[32,16,1024]{2,1,0:T(8,128)(2,1)S(1)}, u32[]{:S(2)}, u32[]{:S(2)}) async-start(bf16[32,16,1024]{2,1,0:T(8,128)(2,1)} %broadcast_in_dim.35), calls=%async_computation.3 | async-start | bytes 2097152 | tf_op jit(solution)/shard_map/spread_xy/all_to_all | solution.py:103

commit v2 on v1

v2 whole, which is shorter than its diff:
```python
import math

import jax
import jax.numpy as jnp
from jax import lax
from jax.sharding import Mesh
from jax.sharding import PartitionSpec as P

STEP = 1000

beta_first = 0.9
beta_second = 0.999
adam_epsilon = 1e-08

AXES = ("z_lo", "x", "y", "z_hi", "core")
Z = ("z_hi", "z_lo")
RANK = 512
TOKENS = 65536


def owner_row(core, xy, z):
    x, y = xy // 4, xy % 4
    z_hi, z_lo = z // 4, z % 4
    return (((z_lo * 4 + x) * 4 + y) * 4 + z_hi) * 2 + core


def reorder(basis, rows):
    pick = (lax.broadcasted_iota(jnp.int32, (RANK, RANK), 0) == rows[None, :]).astype(jnp.bfloat16)
    return jnp.dot(basis, pick, preferred_element_type=jnp.float32).astype(jnp.bfloat16)


def exchange(blocks, axes):
    return lax.all_to_all(blocks, axes, 0, 0, tiled=True)


def spread(block, axes, count):
    return exchange(jnp.broadcast_to(block[None], (count, *block.shape)), axes)


def quarter(tokens, at):
    return lax.dynamic_index_in_dim(
        tokens.reshape(128, 16, 4, 128), (at & 1) * 2 + (at >> 1), 2, keepdims=False
    ).reshape(128, 2048)


def local(normed_input, value_cotangent, basis, first_moment, second_moment):
    x_at, z_lo_at, core_at = (lax.axis_index(a) for a in ("x", "z_lo", "core"))
    swap = [(0, 1), (1, 0)]
    place = jnp.arange(RANK)
    with jax.named_scope("order"):
        ranked = reorder(basis, owner_row(place // 256, place // 16 % 16, place % 16))
        decoder = reorder(basis, owner_row(place // 16 % 2, place // 32, place % 16))
    with jax.named_scope("tokens_x"):
        pieces = [
            jnp.concatenate([quarter(normed_input, (x_at + k) & 3), value_cotangent], axis=1)
            for k in range(4)
        ]
        pieces = pieces[:1] + [
            lax.ppermute(pieces[k], "x", [(i, (i + k) % 4) for i in range(4)]) for k in (1, 3, 2)
        ]
    with jax.named_scope("tokens_core"):
        pieces += [lax.ppermute(piece, "core", swap) for piece in pieces]
    with jax.named_scope("gather_core"):
        rows = lax.dynamic_slice_in_dim(ranked, (x_at >> 1) * 128 + z_lo_at * 32, 32, 0)
        low, high = rows[:, :256], rows[:, 256:]
        theirs = lax.ppermute(jnp.where(core_at == 0, high, low), "core", swap)
        chunk = jnp.where(core_at == (x_at & 1), jnp.where(core_at == 0, low, high), theirs)
    with jax.named_scope("gather_z"):
        line = spread(chunk, Z, 16).reshape(512, 256)
    with jax.named_scope("gather_y"):
        whole = spread(line, "y", 4).reshape(2048, 256)
    with jax.named_scope("project"):
        reduced = jnp.concatenate(
            [
                jnp.dot(piece[:, :2048], whole, preferred_element_type=jnp.float32)
                for piece in pieces
            ]
        )
        cotangents = jnp.concatenate([piece[:, 2048:] for piece in pieces])
        high = lax.reduce_precision(reduced, 8, 7)
        low = (reduced - high).astype(jnp.bfloat16)
        partial = sum(
            lax.dot_general(
                part, cotangents, (((0,), (0,)), ((), ())), preferred_element_type=jnp.float32
            )
            for part in (high.astype(jnp.bfloat16), low)
        )
    with jax.named_scope("reduce_xy"):
        parts = exchange(partial.reshape(16, 16, 1024), ("x", "y"))
        summed = jnp.sum(parts, axis=0)
    with jax.named_scope("reduce_z"):
        parts = exchange(summed.reshape(16, 8, 128), Z)
        share = jnp.sum(parts, axis=0) * (1.0 / math.sqrt(TOKENS))
    with jax.named_scope("adam"):
        first, second = first_moment.reshape(8, 128), second_moment.reshape(8, 128)
        new_first = beta_first * first + (1.0 - beta_first) * share
        new_second = beta_second * second + (1.0 - beta_second) * share * share
        corr_first = 1.0 - beta_first**STEP
        corr_second = 1.0 - beta_second**STEP
        normalized = (
            new_first / corr_first / (jnp.sqrt(new_second / corr_second) + adam_epsilon)
        ).astype(jnp.bfloat16)
    with jax.named_scope("spread_z"):
        column = spread(normalized, Z, 16).reshape(16, 1024)
    with jax.named_scope("spread_xy"):
        step = spread(column, ("x", "y", "core"), 32).reshape(RANK, 1024)
    with jax.named_scope("decode"):
        update = jnp.dot(decoder, step, preferred_element_type=jnp.float32).astype(jnp.bfloat16)
    return new_first.reshape(1, 1024), new_second.reshape(1, 1024), update


def solution(mesh):
    fine = Mesh(mesh.devices.reshape(4, 4, 4, 4, 2), AXES)
    weights = P(("y", "z_hi", "core"), None)
    return jax.shard_map(
        local,
        mesh=fine,
        in_specs=(P(AXES, None), P(AXES, None), weights, P(AXES, None), P(AXES, None)),
        out_specs=(P(AXES, None), P(AXES, None), weights),
        check_vma=False,
    )
```

time: 222 us -> 193 us (0.87)
  blocking collectives: 62.4 us -> 35.2 us
  local copies, waits for them, and re-layouts: 11.6 us -> 27.1 us
  starting transfers between devices: 80.6 us -> 69.9 us
  other arithmetic: 9.54 us -> 3.26 us
  waiting for transfers between devices: 46.3 us -> 40.2 us
  matrix products: 9.71 us -> 14.5 us
    ppermute x14 -> x8, starting transfers between devices: 49.8 us -> 28.1 us  [the longest x3 10.8 us: local(): lax.ppermute(pieces[k], 'x', [(i, (i + k) % 4) for i in range(4)])]
    all_gather x1 -> x0, blocking collectives: 20.7 us -> none  [local(): lax.all_gather(normalized, Z, axis=0, tiled=False).reshape(16, 1024)]
    dynamic_slice x1 -> x2, local copies, waits for them, and re-layouts: 0.01 us -> 12.4 us  [the longest x1 12.4 us: quarter(): lax.dynamic_index_in_dim(tokens.reshape(128, 16, 4, 128), (at & 1) * 2 +...]
    all_to_all x2 -> x4, starting transfers between devices: 30.9 us -> 41.9 us  [exchange(): return lax.all_to_all(blocks, axes, 0, 0, tiled=True)]
    all_to_all x2, blocking collectives: 41.7 us -> 35.2 us  [exchange(): return lax.all_to_all(blocks, axes, 0, 0, tiled=True)]
    gather x4 -> x0, local copies, waits for them, and re-layouts: 5.17 us -> none  [ordered(): return jnp.take(stacked, (index - jnp.arange(4)) % 4, axis=0)]
    unnamed x10 -> x19, local copies, waits for them, and re-layouts: 2.39 us -> 7.15 us
    dot_general x4 -> x10, matrix products: 7.51 us -> 12.3 us  [the longest x8 10.8 us: local(): jnp.dot(piece[:, :2048], whole, preferred_element_type=jnp.float32)]
  transfers between devices with their start and end apart: 16 -> 12, of which waited for: 4 -> 5; matrix products, arithmetic and copies ran while one was open for 10% -> 5% of each run, Pallas kernels for 0% -> 0%
where the time goes in v2:
time: 193 us; the launch traced here: 191 us
  starting transfers between devices  69.9 us (36%)
  waiting for transfers between devices  40.2 us (21%)
  blocking collectives  35.2 us (18%)
  local copies, waits for them, and re-layouts  27.1 us (14%)
  matrix products  14.5 us (8%)
  other arithmetic  3.26 us (2%)
    all_to_all x4, starting transfers between devices, exchange(): return lax.all_to_all(blocks, axes, 0, 0, tiled=True)  41.9 us
    all_to_all x4, waiting for transfers between devices, exchange(): return lax.all_to_all(blocks, axes, 0, 0, tiled=True)  36.9 us
    all_to_all x2, blocking collectives, exchange(): return lax.all_to_all(blocks, axes, 0, 0, tiled=True)  35.2 us
    dynamic_slice x1, local copies, waits for them, and re-layouts, quarter(): lax.dynamic_index_in_dim(tokens.reshape(128, 16, 4, 128), (at & 1) * 2 +...  12.4 us
    dot_general x8, matrix products, local(): jnp.dot(piece[:, :2048], whole, preferred_element_type=jnp.float32)  10.8 us
    ppermute x3, starting transfers between devices, local(): lax.ppermute(pieces[k], 'x', [(i, (i + k) % 4) for i in range(4)])  10.8 us
    ppermute x4, starting transfers between devices, local(): pieces += [lax.ppermute(piece, 'core', swap) for piece in pieces]  10.3 us
    unnamed x19, local copies, waits for them, and re-layouts  7.15 us
  transfers between devices with their start and end apart: 12, of which 5 were waited for; matrix products, arithmetic and copies ran while one was open for 5% of the time, Pallas kernels for 0%

profile of v2, /device:TPU:1, one launch (start us, length us, event | category | flops | bytes accessed | tf_op | source)
XLA Modules:
  0.0 191.2 jit_solution(12961858487904242080)
XLA Ops:
  0.7 3.3 %reshape.269 = bf16[128,16,4,128]{3,2,1,0:T(4,128)(2,1)S(1)} reshape(bf16[128,8192]{1,0:T(8,128)(2,1)} %param.5) | data formatting | bytes 4194304 | tf_op jit(solution)/shard_map/tokens_x/reshape | solution.py:42
  3.9 12.4 %dynamic-slice_reduce_fusion.3 = (bf16[128,16,128]{2,1,0:T(8,128)(2,1)S(1)}, bf16[128,16,128]{2,1,0:T(8,128)(2,1)S(1)}, bf16[128,16,128]{2,1,0:T(8,128)(2,1)S(1)}, bf16[128,16,128]{2,1,0:T(8,128)(2,1)S(1)}) fusion(bf16[128,16,4,128]{3,2,1,0:T(4,128)(2,1)S(1)} %reshape.269, s32[]{:T(128)S(6)} %select_n.155, s32[]{:T(128)S(6)} %select_n.171, ...), kind=kLoop, calls=%fused_computation.23 | loop fusion | bytes 4194320 | tf_op jit(solution)/shard_map/tokens_x/jit(dynamic_index_in_dim)/dynamic_slice | solution.py:41
  17.5 1.9 pad_maximum_fusion
  19.4 3.9 %collective-permute-start.1 = (bf16[128,3072]{1,0:T(8,128)(2,1)}, bf16[128,3072]{1,0:T(8,128)(2,1)}, u32[]{:S(2)}, u32[]{:S(2)}) collective-permute-start(bf16[128,3072]{1,0:T(8,128)(2,1)} %get-tuple-element.10), channel_id=1, source_target_pairs={{0,32},{32,64},{64,96},{96,0},{1,33},{33,65},{65,97},{97,1},{2,34}... | collective-permute-start | bytes 2359304 | tf_op jit(solution)/shard_map/tokens_x/ppermute | solution.py:59
  23.3 3.2 %collective-permute-start.2 = (bf16[128,3072]{1,0:T(8,128)(2,1)}, bf16[128,3072]{1,0:T(8,128)(2,1)}, u32[]{:S(2)}, u32[]{:S(2)}) collective-permute-start(bf16[128,3072]{1,0:T(8,128)(2,1)} %get-tuple-element.8), channel_id=1, source_target_pairs={{0,96},{32,0},{64,32},{96,64},{1,97},{33,1},{65,33},{97,65},{2,98}... | collective-permute-start | bytes 2359304 | tf_op jit(solution)/shard_map/tokens_x/ppermute | solution.py:59
  26.5 3.6 %collective-permute-start.3 = (bf16[128,3072]{1,0:T(8,128)(2,1)}, bf16[128,3072]{1,0:T(8,128)(2,1)}, u32[]{:S(2)}, u32[]{:S(2)}) collective-permute-start(bf16[128,3072]{1,0:T(8,128)(2,1)} %get-tuple-element.9), channel_id=1, source_target_pairs={{0,64},{32,96},{64,0},{96,32},{1,65},{33,97},{65,1},{97,33},{2,66}... | collective-permute-start | bytes 2359304 | tf_op jit(solution)/shard_map/tokens_x/ppermute | solution.py:59
  30.6 7.0 %collective-permute-start = (bf16[32,256]{1,0:T(8,128)(2,1)S(1)}, bf16[32,256]{1,0:T(8,128)(2,1)S(1)}, u32[]{:S(2)}, u32[]{:S(2)}) collective-permute-start(bf16[32,256]{1,0:T(8,128)(2,1)S(1)} %broadcast_select_fusion), channel_id=1, source_target_pairs={{0,1},{1,0},{2,3},{3,2},{4,5},{5,4},{6,7},{7,6},{8,9},{9,8},{10,11... | collective-permute-start | bytes 49160 | tf_op jit(solution)/shard_map/gather_core/ppermute | solution.py:66
  39.2 11.3 %all-to-all-start = ((bf16[16,32,256]{2,1,0:T(8,128)(2,1)}), bf16[16,32,256]{2,1,0:T(8,128)(2,1)S(1)}, u32[]{:S(2)}, u32[]{:S(2)}) async-start(bf16[16,32,256]{2,1,0:T(8,128)(2,1)} %broadcast_in_dim.12), calls=%async_computation | async-start | bytes 524288 | tf_op jit(solution)/shard_map/gather_z/all_to_all | solution.py:33
  50.5 2.5 %collective-permute-start.4 = (bf16[128,3072]{1,0:T(8,128)(2,1)}, bf16[128,3072]{1,0:T(8,128)(2,1)}, u32[]{:S(2)}, u32[]{:S(2)}) collective-permute-start(bf16[128,3072]{1,0:T(8,128)(2,1)} %get-tuple-element.7), channel_id=1, source_target_pairs={{0,1},{1,0},{2,3},{3,2},{4,5},{5,4},{6,7},{7,6},{8,9},{9,8},{10,11... | collective-permute-start | bytes 2359304 | tf_op jit(solution)/shard_map/tokens_core/ppermute | solution.py:62
  53.1 1.9 %collective-permute-start.5 = (bf16[128,3072]{1,0:T(8,128)(2,1)}, bf16[128,3072]{1,0:T(8,128)(2,1)}, u32[]{:S(2)}, u32[]{:S(2)}) collective-permute-start(bf16[128,3072]{1,0:T(8,128)(2,1)} %collective-permute-done.1), channel_id=1, source_target_pairs={{0,1},{1,0},{2,3},{3,2},{4,5},{5,4},{6,7},{7,6},{8,9},{9,8},{10,11... | collective-permute-start | bytes 2359304 | tf_op jit(solution)/shard_map/tokens_core/ppermute | solution.py:62
  55.0 2.4 %collective-permute-start.6 = (bf16[128,3072]{1,0:T(8,128)(2,1)}, bf16[128,3072]{1,0:T(8,128)(2,1)}, u32[]{:S(2)}, u32[]{:S(2)}) collective-permute-start(bf16[128,3072]{1,0:T(8,128)(2,1)} %collective-permute-done.2), channel_id=1, source_target_pairs={{0,1},{1,0},{2,3},{3,2},{4,5},{5,4},{6,7},{7,6},{8,9},{9,8},{10,11... | collective-permute-start | bytes 2359304 | tf_op jit(solution)/shard_map/tokens_core/ppermute | solution.py:62
  57.5 2.4 %collective-permute-done.3 = bf16[128,3072]{1,0:T(8,128)(2,1)} collective-permute-done((bf16[128,3072]{1,0:T(8,128)(2,1)}, bf16[128,3072]{1,0:T(8,128)(2,1)}, u32[]{:S(2)}, u32[]{:S(2)}) %collective-permute-start.3) | collective-permute-done | bytes 786464 | tf_op jit(solution)/shard_map/tokens_x/ppermute | solution.py:59
  59.9 3.4 %collective-permute-start.7 = (bf16[128,3072]{1,0:T(8,128)(2,1)}, bf16[128,3072]{1,0:T(8,128)(2,1)}, u32[]{:S(2)}, u32[]{:S(2)}) collective-permute-start(bf16[128,3072]{1,0:T(8,128)(2,1)} %collective-permute-done.3), channel_id=1, source_target_pairs={{0,1},{1,0},{2,3},{3,2},{4,5},{5,4},{6,7},{7,6},{8,9},{9,8},{10,11... | collective-permute-start | bytes 2359304 | tf_op jit(solution)/shard_map/tokens_core/ppermute | solution.py:62
  67.3 6.3 %all-to-all-start.1 = ((bf16[4,512,256]{2,1,0:T(8,128)(2,1)}), bf16[4,512,256]{2,1,0:T(8,128)(2,1)S(1)}, u32[]{:S(2)}, u32[]{:S(2)}) async-start(bf16[4,512,256]{2,1,0:T(8,128)(2,1)} %broadcast_in_dim.14), calls=%async_computation.1 | async-start | bytes 2097152 | tf_op jit(solution)/shard_map/gather_y/all_to_all | solution.py:33
  77.6 9.6 %all-to-all-done.1 = bf16[4,512,256]{2,1,0:T(8,128)(2,1)S(1)} async-done(((bf16[4,512,256]{2,1,0:T(8,128)(2,1)}), bf16[4,512,256]{2,1,0:T(8,128)(2,1)S(1)}, u32[]{:S(2)}, u32[]{:S(2)}) %all-to-all-start.1) | async-done | bytes 1048608 | tf_op jit(solution)/shard_map/gather_y/all_to_all | solution.py:33
  87.2 1.3 convolution_dynamic-update-slice_fusion.7
  88.6 1.3 convolution_dynamic-update-slice_fusion.6
  99.6 20.9 %all_to_all.30 = f32[16,16,1024]{2,1,0:T(8,128)S(1)} all-to-all(f32[16,16,1024]{2,1,0:T(8,128)S(1)} %bitcast.52), channel_id=1, replica_groups=mesh['z_lo'=4,'x'=4,'y'=4,'z_hi'=4,'core'=2] {'x','y'}, dimensions={0} | all-to-all | bytes 2097152 | tf_op jit(solution)/shard_map/reduce_xy/all_to_all | solution.py:33
  121.2 14.9 %all-to-all-start.3 = ((f32[16,8,128]{2,1,0:T(8,128)}), f32[16,8,128]{2,1,0:T(8,128)S(1)}, u32[]{:S(2)}, u32[]{:S(2)}) async-start(f32[16,8,128]{2,1,0:T(8,128)} %bitcast.18), calls=%async_computation.3 | async-start | bytes 131072 | tf_op jit(solution)/shard_map/reduce_z/all_to_all | solution.py:33
  136.2 11.5 %all-to-all-done.3 = f32[16,8,128]{2,1,0:T(8,128)S(1)} async-done(((f32[16,8,128]{2,1,0:T(8,128)}), f32[16,8,128]{2,1,0:T(8,128)S(1)}, u32[]{:S(2)}, u32[]{:S(2)}) %all-to-all-start.3) | async-done | bytes 65568 | tf_op jit(solution)/shard_map/reduce_z/all_to_all | solution.py:33
  147.7 14.3 %all_to_all.31 = bf16[16,8,128]{2,1,0:T(8,128)(2,1)S(1)} all-to-all(bf16[16,8,128]{2,1,0:T(8,128)(2,1)S(1)} %broadcast_in_dim.15), channel_id=1, replica_groups=mesh['z_lo'=4,'x'=4,'y'=4,'z_hi'=4,'core'=2] {'z_hi','z_lo'}, dimensions={0} | all-to-all | bytes 65536 | tf_op jit(solution)/shard_map/spread_z/all_to_all | solution.py:33
  163.1 9.3 %all-to-all-start.5 = ((bf16[32,16,1024]{2,1,0:T(8,128)(2,1)}), bf16[32,16,1024]{2,1,0:T(8,128)(2,1)S(1)}, u32[]{:S(2)}, u32[]{:S(2)}) async-start(bf16[32,16,1024]{2,1,0:T(8,128)(2,1)} %broadcast_in_dim.33), calls=%async_computation.5 | async-start | bytes 2097152 | tf_op jit(solution)/shard_map/spread_xy/all_to_all | solution.py:33
  173.6 15.8 %all-to-all-done.5 = bf16[32,16,1024]{2,1,0:T(8,128)(2,1)S(1)} async-done(((bf16[32,16,1024]{2,1,0:T(8,128)(2,1)}), bf16[32,16,1024]{2,1,0:T(8,128)(2,1)S(1)}, u32[]{:S(2)}, u32[]{:S(2)}) %all-to-all-start.5) | async-done | bytes 1048608 | tf_op jit(solution)/shard_map/spread_xy/all_to_all | solution.py:33
  189.4 1.8 convolution_convert_fusion
  (55 shorter events, 23.6 us)
Async XLA Ops:
  0.6 29.6 %copy-start = (bf16[256,512]{1,0:T(8,128)(2,1)S(1)}, bf16[256,512]{1,0:T(8,128)(2,1)}, u32[]{:S(2)}) copy-start(bf16[256,512]{1,0:T(8,128)(2,1)} %param.7) | copy-start | bytes 786436
  16.3 0.8 copy-start.1
  16.3 1.1 copy-start.2
  19.4 33.7 %collective-permute-start.1 = (bf16[128,3072]{1,0:T(8,128)(2,1)}, bf16[128,3072]{1,0:T(8,128)(2,1)}, u32[]{:S(2)}, u32[]{:S(2)}) collective-permute-start(bf16[128,3072]{1,0:T(8,128)(2,1)} %get-tuple-element.10), channel_id=1, source_target_pairs={{0,32},{32,64},{64,96},{96,0},{1,33},{33,65},{65,97},{97,1},{2,34}... | collective-permute-start | bytes 2359304 | tf_op jit(solution)/shard_map/tokens_x/ppermute | solution.py:59
  23.3 31.7 %collective-permute-start.2 = (bf16[128,3072]{1,0:T(8,128)(2,1)}, bf16[128,3072]{1,0:T(8,128)(2,1)}, u32[]{:S(2)}, u32[]{:S(2)}) collective-permute-start(bf16[128,3072]{1,0:T(8,128)(2,1)} %get-tuple-element.8), channel_id=1, source_target_pairs={{0,96},{32,0},{64,32},{96,64},{1,97},{33,1},{65,33},{97,65},{2,98}... | collective-permute-start | bytes 2359304 | tf_op jit(solution)/shard_map/tokens_x/ppermute | solution.py:59
  26.5 33.3 %collective-permute-start.3 = (bf16[128,3072]{1,0:T(8,128)(2,1)}, bf16[128,3072]{1,0:T(8,128)(2,1)}, u32[]{:S(2)}, u32[]{:S(2)}) collective-permute-start(bf16[128,3072]{1,0:T(8,128)(2,1)} %get-tuple-element.9), channel_id=1, source_target_pairs={{0,64},{32,96},{64,0},{96,32},{1,65},{33,97},{65,1},{97,33},{2,66}... | collective-permute-start | bytes 2359304 | tf_op jit(solution)/shard_map/tokens_x/ppermute | solution.py:59
  30.6 7.8 %collective-permute-start = (bf16[32,256]{1,0:T(8,128)(2,1)S(1)}, bf16[32,256]{1,0:T(8,128)(2,1)S(1)}, u32[]{:S(2)}, u32[]{:S(2)}) collective-permute-start(bf16[32,256]{1,0:T(8,128)(2,1)S(1)} %broadcast_select_fusion), channel_id=1, source_target_pairs={{0,1},{1,0},{2,3},{3,2},{4,5},{5,4},{6,7},{7,6},{8,9},{9,8},{10,11... | collective-permute-start | bytes 49160 | tf_op jit(solution)/shard_map/gather_core/ppermute | solution.py:66
  39.2 27.1 %all-to-all-start = ((bf16[16,32,256]{2,1,0:T(8,128)(2,1)}), bf16[16,32,256]{2,1,0:T(8,128)(2,1)S(1)}, u32[]{:S(2)}, u32[]{:S(2)}) async-start(bf16[16,32,256]{2,1,0:T(8,128)(2,1)} %broadcast_in_dim.12), calls=%async_computation | async-start | bytes 524288 | tf_op jit(solution)/shard_map/gather_z/all_to_all | solution.py:33
  50.5 23.1 %collective-permute-start.4 = (bf16[128,3072]{1,0:T(8,128)(2,1)}, bf16[128,3072]{1,0:T(8,128)(2,1)}, u32[]{:S(2)}, u32[]{:S(2)}) collective-permute-start(bf16[128,3072]{1,0:T(8,128)(2,1)} %get-tuple-element.7), channel_id=1, source_target_pairs={{0,1},{1,0},{2,3},{3,2},{4,5},{5,4},{6,7},{7,6},{8,9},{9,8},{10,11... | collective-permute-start | bytes 2359304 | tf_op jit(solution)/shard_map/tokens_core/ppermute | solution.py:62
  53.1 21.5 %collective-permute-start.5 = (bf16[128,3072]{1,0:T(8,128)(2,1)}, bf16[128,3072]{1,0:T(8,128)(2,1)}, u32[]{:S(2)}, u32[]{:S(2)}) collective-permute-start(bf16[128,3072]{1,0:T(8,128)(2,1)} %collective-permute-done.1), channel_id=1, source_target_pairs={{0,1},{1,0},{2,3},{3,2},{4,5},{5,4},{6,7},{7,6},{8,9},{9,8},{10,11... | collective-permute-start | bytes 2359304 | tf_op jit(solution)/shard_map/tokens_core/ppermute | solution.py:62
  55.0 20.5 %collective-permute-start.6 = (bf16[128,3072]{1,0:T(8,128)(2,1)}, bf16[128,3072]{1,0:T(8,128)(2,1)}, u32[]{:S(2)}, u32[]{:S(2)}) collective-permute-start(bf16[128,3072]{1,0:T(8,128)(2,1)} %collective-permute-done.2), channel_id=1, source_target_pairs={{0,1},{1,0},{2,3},{3,2},{4,5},{5,4},{6,7},{7,6},{8,9},{9,8},{10,11... | collective-permute-start | bytes 2359304 | tf_op jit(solution)/shard_map/tokens_core/ppermute | solution.py:62
  59.9 16.7 %collective-permute-start.7 = (bf16[128,3072]{1,0:T(8,128)(2,1)}, bf16[128,3072]{1,0:T(8,128)(2,1)}, u32[]{:S(2)}, u32[]{:S(2)}) collective-permute-start(bf16[128,3072]{1,0:T(8,128)(2,1)} %collective-permute-done.3), channel_id=1, source_target_pairs={{0,1},{1,0},{2,3},{3,2},{4,5},{5,4},{6,7},{7,6},{8,9},{9,8},{10,11... | collective-permute-start | bytes 2359304 | tf_op jit(solution)/shard_map/tokens_core/ppermute | solution.py:62
  67.3 19.9 %all-to-all-start.1 = ((bf16[4,512,256]{2,1,0:T(8,128)(2,1)}), bf16[4,512,256]{2,1,0:T(8,128)(2,1)S(1)}, u32[]{:S(2)}, u32[]{:S(2)}) async-start(bf16[4,512,256]{2,1,0:T(8,128)(2,1)} %broadcast_in_dim.14), calls=%async_computation.1 | async-start | bytes 2097152 | tf_op jit(solution)/shard_map/gather_y/all_to_all | solution.py:33
  99.5 36.6 %copy-start.3 = (f32[1,1024]{1,0:T(1,128)S(1)}, f32[1,1024]{1,0:T(1,128)}, u32[]{:S(2)}) copy-start(f32[1,1024]{1,0:T(1,128)} %param.8) | copy-start | bytes 12292
  99.6 36.6 %copy-start.4 = (f32[1,1024]{1,0:T(1,128)S(1)}, f32[1,1024]{1,0:T(1,128)}, u32[]{:S(2)}) copy-start(f32[1,1024]{1,0:T(1,128)} %param.9) | copy-start | bytes 12292
  121.2 26.5 %all-to-all-start.3 = ((f32[16,8,128]{2,1,0:T(8,128)}), f32[16,8,128]{2,1,0:T(8,128)S(1)}, u32[]{:S(2)}, u32[]{:S(2)}) async-start(f32[16,8,128]{2,1,0:T(8,128)} %bitcast.18), calls=%async_computation.3 | async-start | bytes 131072 | tf_op jit(solution)/shard_map/reduce_z/all_to_all | solution.py:33
  163.1 26.3 %all-to-all-start.5 = ((bf16[32,16,1024]{2,1,0:T(8,128)(2,1)}), bf16[32,16,1024]{2,1,0:T(8,128)(2,1)S(1)}, u32[]{:S(2)}, u32[]{:S(2)}) async-start(bf16[32,16,1024]{2,1,0:T(8,128)(2,1)} %broadcast_in_dim.33), calls=%async_computation.5 | async-start | bytes 2097152 | tf_op jit(solution)/shard_map/spread_xy/all_to_all | solution.py:33

commit v3 on v2

v3 whole, which is shorter than its diff:
```python
import math

import jax
import jax.numpy as jnp
from jax import lax
from jax.experimental import pallas as pl
from jax.experimental.pallas import tpu as pltpu
from jax.sharding import Mesh
from jax.sharding import PartitionSpec as P

STEP = 1000

beta_first = 0.9
beta_second = 0.999
adam_epsilon = 1e-08

AXES = ("z_lo", "x", "y", "z_hi", "core")
RANK = 512
TOKENS = 65536
KVW = 1024
QUARTER = 2048


def reorder(basis, rows):
    pick = (lax.broadcasted_iota(jnp.int32, (RANK, RANK), 0) == rows[None, :]).astype(jnp.bfloat16)
    return jnp.dot(basis, pick, preferred_element_type=jnp.float32).astype(jnp.bfloat16)


def exchange(blocks, axes):
    return lax.all_to_all(blocks, axes, 0, 0, tiled=True)


def spread(block, axes, count):
    return exchange(jnp.broadcast_to(block[None], (count, *block.shape)), axes)


def pack_kernel(x_ref, tokens_ref, cotangent_ref, *out_refs):
    for k, out_ref in enumerate(out_refs):
        at = (x_ref[0] + k) & 3
        offset = pl.multiple_of((at & 1) * 256 + (at >> 1) * 128, 128)
        for block in range(16):
            out_ref[:, block * 128 : block * 128 + 128] = tokens_ref[
                :, pl.ds(pl.multiple_of(block * 512 + offset, 128), 128)
            ]
        out_ref[:, QUARTER:] = cotangent_ref[...]


def pack(x_at, tokens, cotangent):
    rows = 32
    return pl.pallas_call(
        pack_kernel,
        grid=(128 // rows,),
        in_specs=[
            pl.BlockSpec(memory_space=pltpu.SMEM),
            pl.BlockSpec((rows, 8192), lambda i: (i, 0)),
            pl.BlockSpec((rows, KVW), lambda i: (i, 0)),
        ],
        out_specs=[pl.BlockSpec((rows, QUARTER + KVW), lambda i: (i, 0))] * 4,
        out_shape=[jax.ShapeDtypeStruct((128, QUARTER + KVW), jnp.bfloat16)] * 4,
        compiler_params=pltpu.CompilerParams(vmem_limit_bytes=32 * 2**20),
        cost_estimate=pl.CostEstimate(flops=0, bytes_accessed=6 * 2**20, transcendentals=0),
        name="pack",
    )(x_at[None], tokens, cotangent)


def project_kernel(*refs):
    *pieces, whole_ref, out_ref, split_ref = refs
    whole = whole_ref[...]
    count = len(pieces)
    for k, piece in enumerate(pieces):
        reduced = jnp.dot(piece[:, :QUARTER], whole, preferred_element_type=jnp.float32)
        high = reduced.astype(jnp.bfloat16)
        low = (reduced - high.astype(jnp.float32)).astype(jnp.bfloat16)
        split_ref[k * 128 : k * 128 + 128] = high
        split_ref[(count + k) * 128 : (count + k) * 128 + 128] = low
    for n in range(0, KVW, 256):
        columns = [piece[:, QUARTER + n : QUARTER + n + 256] for piece in pieces]
        out_ref[:, n : n + 256] = lax.dot_general(
            split_ref[...],
            jnp.concatenate(columns + columns, axis=0),
            (((0,), (0,)), ((), ())),
            preferred_element_type=jnp.float32,
        ).astype(jnp.bfloat16)


def project(pieces, whole):
    vmem = pl.BlockSpec(memory_space=pltpu.VMEM)
    return pl.pallas_call(
        project_kernel,
        in_specs=[vmem] * (len(pieces) + 1),
        out_specs=vmem,
        out_shape=jax.ShapeDtypeStruct((256, KVW), jnp.bfloat16),
        scratch_shapes=[pltpu.VMEM((2 * 128 * len(pieces), 256), jnp.bfloat16)],
        compiler_params=pltpu.CompilerParams(vmem_limit_bytes=40 * 2**20),
        cost_estimate=pl.CostEstimate(
            flops=2 * 2**30, bytes_accessed=8 * 2**20, transcendentals=0
        ),
        name="project",
    )(*pieces, whole)


def local(normed_input, value_cotangent, basis, first_moment, second_moment):
    x_at, z_hi_at, z_lo_at, core_at = (lax.axis_index(a) for a in ("x", "z_hi", "z_lo", "core"))
    swap = [(0, 1), (1, 0)]
    place = jnp.arange(RANK)
    with jax.named_scope("order"):
        ranked = reorder(basis, (place & 255) * 2 + (place >> 8))
        decoder = reorder(basis, (place & ~7) + (place & 3) * 2 + (place >> 2 & 1))
    with jax.named_scope("gather_core"):
        rows = lax.dynamic_slice_in_dim(ranked, (x_at >> 1) * 128 + z_lo_at * 32, 32, 0)
        low, high = rows[:, :256], rows[:, 256:]
        theirs = lax.ppermute(jnp.where(core_at == 0, high, low), "core", swap)
        chunk = jnp.where(core_at == (x_at & 1), jnp.where(core_at == 0, low, high), theirs)
    with jax.named_scope("tokens_x"):
        packed = pack(x_at, normed_input, value_cotangent)
        pieces = [packed[0]] + [
            lax.ppermute(packed[k], "x", [(i, (i + k) % 4) for i in range(4)]) for k in (1, 3, 2)
        ]
    with jax.named_scope("tokens_core"):
        pieces += [lax.ppermute(piece, "core", swap) for piece in pieces]
    with jax.named_scope("gather_z"):
        line = spread(chunk, ("z_hi", "z_lo"), 16).reshape(512, 256)
    with jax.named_scope("gather_y"):
        whole = spread(line, "y", 4).reshape(QUARTER, 256)
    with jax.named_scope("moments_z"):
        own = jnp.concatenate([first_moment, second_moment])
        row = lax.broadcasted_iota(jnp.int32, (4, KVW), 0)
        first = second = jnp.zeros((4, KVW), jnp.float32)
        for k in range(4):
            theirs = lax.ppermute(own, "z_hi", [(i, (i + k) % 4) for i in range(4)]) if k else own
            place_of = row == ((z_hi_at - k) & 3)
            first = jnp.where(place_of, theirs[:1], first)
            second = jnp.where(place_of, theirs[1:], second)
    with jax.named_scope("project"):
        partial = project(pieces, whole)
    with jax.named_scope("reduce_plane"):
        parts = exchange(partial.reshape(64, 4, KVW), ("z_lo", "x", "y"))
        summed = jnp.sum(parts.astype(jnp.float32), axis=0)
    with jax.named_scope("reduce_z"):
        share = jnp.sum(spread(summed, "z_hi", 4), axis=0) * (1.0 / math.sqrt(TOKENS))
    with jax.named_scope("adam"):
        new_first = beta_first * first + (1.0 - beta_first) * share
        new_second = beta_second * second + (1.0 - beta_second) * share * share
        corr_first = 1.0 - beta_first**STEP
        corr_second = 1.0 - beta_second**STEP
        normalized = (
            new_first / corr_first / (jnp.sqrt(new_second / corr_second) + adam_epsilon)
        ).astype(jnp.bfloat16)
    with jax.named_scope("spread_plane"):
        step = spread(normalized, ("z_lo", "x", "y", "core"), 128).reshape(RANK, KVW)
    with jax.named_scope("decode"):
        update = jnp.dot(decoder, step, preferred_element_type=jnp.float32).astype(jnp.bfloat16)
    with jax.named_scope("own"):
        own_first = lax.dynamic_slice_in_dim(new_first, z_hi_at, 1, 0)
        own_second = lax.dynamic_slice_in_dim(new_second, z_hi_at, 1, 0)
    return own_first, own_second, update


def solution(mesh):
    fine = Mesh(mesh.devices.reshape(4, 4, 4, 4, 2), AXES)
    weights = P(("y", "z_hi", "core"), None)
    return jax.shard_map(
        local,
        mesh=fine,
        in_specs=(P(AXES, None), P(AXES, None), weights, P(AXES, None), P(AXES, None)),
        out_specs=(P(AXES, None), P(AXES, None), weights),
        check_vma=False,
    )
```

time: 193 us -> 194 us (level)
  starting transfers between devices: 69.9 us -> 110 us
  blocking collectives: 35.2 us -> 0 us
  waiting for transfers between devices: 40.2 us -> 64.5 us
  local copies, waits for them, and re-layouts: 27.1 us -> 9.11 us
  matrix products: 14.5 us -> 2.19 us
  Pallas kernels: 0 us -> 5.29 us
  other arithmetic: 3.26 us -> 0.44 us
    all_to_all x2 -> x0, blocking collectives: 35.2 us -> none  [exchange(): return lax.all_to_all(blocks, axes, 0, 0, tiled=True)]
    all_to_all x4 -> x5, waiting for transfers between devices: 36.9 us -> 55.5 us  [exchange(): return lax.all_to_all(blocks, axes, 0, 0, tiled=True)]
    ppermute x3 -> x6, starting transfers between devices: 10.8 us -> 28.2 us  [the longest x3 18.3 us: local(): lax.ppermute(own, 'z_hi', [(i, (i + k) % 4) for i in range(4)])]
    ppermute x4, starting transfers between devices: 10.3 us -> 26.7 us  [local(): pieces += [lax.ppermute(piece, 'core', swap) for piece in pieces]]
    dot_general x10 -> x0, matrix products: 12.3 us -> none  [the longest x8 10.8 us: local(): jnp.dot(piece[:, :2048], whole, preferred_element_type=jnp.float32)]
    dynamic_slice x1, local copies, waits for them, and re-layouts: 12.4 us -> 0.61 us  [local(): own_second = lax.dynamic_slice_in_dim(new_second, z_hi_at, 1, 0)]
    ppermute x3 -> x6, waiting for transfers between devices: 2.41 us -> 8.24 us  [the longest x3 8.23 us: local(): lax.ppermute(packed[k], 'x', [(i, (i + k) % 4) for i in range(4)])]
    pallas_call x0 -> x2, Pallas kernels: none -> 5.29 us  [the longest x1 4.67 us: project(): pl.pallas_call(project_kernel, in_specs=[vmem] * (len(pieces) + 1), out_s...]
  transfers between devices with their start and end apart: 12 -> 16, of which waited for: 5 -> 5; matrix products, arithmetic and copies ran while one was open for 5% -> 1% of each run, Pallas kernels for 0% -> 0%
where the time goes in v3:
time: 194 us; the launch traced here: 193 us
  starting transfers between devices  110 us (57%)
  waiting for transfers between devices  64.5 us (33%)
  local copies, waits for them, and re-layouts  9.11 us (5%)
  Pallas kernels  5.29 us (3%)
  matrix products  2.19 us (1%)
    all_to_all x5, waiting for transfers between devices, exchange(): return lax.all_to_all(blocks, axes, 0, 0, tiled=True)  55.5 us
    all_to_all x5, starting transfers between devices, exchange(): return lax.all_to_all(blocks, axes, 0, 0, tiled=True)  46.6 us
    ppermute x4, starting transfers between devices, local(): pieces += [lax.ppermute(piece, 'core', swap) for piece in pieces]  26.7 us
    ppermute x3, starting transfers between devices, local(): lax.ppermute(own, 'z_hi', [(i, (i + k) % 4) for i in range(4)])  18.3 us
    ppermute x3, starting transfers between devices, local(): lax.ppermute(packed[k], 'x', [(i, (i + k) % 4) for i in range(4)])  9.94 us
    ppermute x1, starting transfers between devices, local(): theirs = lax.ppermute(jnp.where(core_at == 0, high, low), 'core', swap)  8.78 us
    ppermute x3, waiting for transfers between devices, local(): lax.ppermute(packed[k], 'x', [(i, (i + k) % 4) for i in range(4)])  8.23 us
    pallas_call x1, Pallas kernels, project(): pl.pallas_call(project_kernel, in_specs=[vmem] * (len(pieces) + 1), out_s...  4.67 us
  transfers between devices with their start and end apart: 16, of which 5 were waited for; matrix products, arithmetic and copies ran while one was open for 1% of the time, Pallas kernels for 0%

profile of v3, /device:TPU:1, one launch (start us, length us, event | category | flops | bytes accessed | tf_op | source)
XLA Modules:
  0.0 192.9 jit_solution(13749251013570635573)
XLA Ops:
  2.0 8.8 %collective-permute-start.10 = (bf16[32,256]{1,0:T(8,128)(2,1)S(1)}, bf16[32,256]{1,0:T(8,128)(2,1)S(1)}, u32[]{:S(2)}, u32[]{:S(2)}) collective-permute-start(bf16[32,256]{1,0:T(8,128)(2,1)S(1)} %broadcast_select_fusion), channel_id=1, source_target_pairs={{0,1},{1,0},{2,3},{3,2},{4,5},{5,4},{6,7},{7,6},{8,9},{9,8},{10,11... | collective-permute-start | bytes 49160 | tf_op jit(solution)/shard_map/gather_core/ppermute | solution.py:112
  12.3 9.5 %all-to-all-start = ((bf16[16,32,256]{2,1,0:T(8,128)(2,1)}), bf16[16,32,256]{2,1,0:T(8,128)(2,1)S(1)}, u32[]{:S(2)}, u32[]{:S(2)}) async-start(bf16[16,32,256]{2,1,0:T(8,128)(2,1)} %broadcast_in_dim.102), calls=%async_computation | async-start | bytes 524288 | tf_op jit(solution)/shard_map/gather_z/all_to_all | solution.py:30
  21.9 1.6 copy-done.1
  25.1 3.1 %collective-permute-start.3 = (bf16[128,3072]{1,0:T(8,128)(2,1)S(1)}, bf16[128,3072]{1,0:T(8,128)(2,1)S(1)}, u32[]{:S(2)}, u32[]{:S(2)}) collective-permute-start(bf16[128,3072]{1,0:T(8,128)(2,1)S(1)} %get-tuple-element.8), channel_id=1, source_target_pairs={{0,32},{32,64},{64,96},{96,0},{1,33},{33,65},{65,97},{97,1},{2,34}... | collective-permute-start | bytes 2359304 | tf_op jit(solution)/shard_map/tokens_x/ppermute | solution.py:117
  28.2 3.4 %collective-permute-start.4 = (bf16[128,3072]{1,0:T(8,128)(2,1)S(1)}, bf16[128,3072]{1,0:T(8,128)(2,1)}, u32[]{:S(2)}, u32[]{:S(2)}) collective-permute-start(bf16[128,3072]{1,0:T(8,128)(2,1)S(1)} %get-tuple-element.9), channel_id=1, source_target_pairs={{0,96},{32,0},{64,32},{96,64},{1,97},{33,1},{65,33},{97,65},{2,98}... | collective-permute-start | bytes 2359304 | tf_op jit(solution)/shard_map/tokens_x/ppermute | solution.py:117
  31.6 3.4 %collective-permute-start.5 = (bf16[128,3072]{1,0:T(8,128)(2,1)S(1)}, bf16[128,3072]{1,0:T(8,128)(2,1)}, u32[]{:S(2)}, u32[]{:S(2)}) collective-permute-start(bf16[128,3072]{1,0:T(8,128)(2,1)S(1)} %get-tuple-element.10), channel_id=1, source_target_pairs={{0,64},{32,96},{64,0},{96,32},{1,65},{33,97},{65,1},{97,33},{2,66}... | collective-permute-start | bytes 2359304 | tf_op jit(solution)/shard_map/tokens_x/ppermute | solution.py:117
  35.0 3.4 %collective-permute-start.6 = (bf16[128,3072]{1,0:T(8,128)(2,1)S(1)}, bf16[128,3072]{1,0:T(8,128)(2,1)}, u32[]{:S(2)}, u32[]{:S(2)}) collective-permute-start(bf16[128,3072]{1,0:T(8,128)(2,1)S(1)} %get-tuple-element.7.refs_0_), channel_id=1, source_target_pairs={{0,1},{1,0},{2,3},{3,2},{4,5},{5,4},{6,7},{7,6},{8,9},{9,8},{10,11... | collective-permute-start | bytes 2359304 | tf_op jit(solution)/shard_map/tokens_core/ppermute | solution.py:120
  38.4 8.2 %collective-permute-done.3.refs_1_ = bf16[128,3072]{1,0:T(8,128)(2,1)S(1)} collective-permute-done((bf16[128,3072]{1,0:T(8,128)(2,1)S(1)}, bf16[128,3072]{1,0:T(8,128)(2,1)S(1)}, u32[]{:S(2)}, u32[]{:S(2)}) %collective-permute-start.3) | collective-permute-done | bytes 786464 | tf_op jit(solution)/shard_map/tokens_x/ppermute | solution.py:117
  46.6 3.5 %collective-permute-start.7 = (bf16[128,3072]{1,0:T(8,128)(2,1)S(1)}, bf16[128,3072]{1,0:T(8,128)(2,1)}, u32[]{:S(2)}, u32[]{:S(2)}) collective-permute-start(bf16[128,3072]{1,0:T(8,128)(2,1)S(1)} %collective-permute-done.3.refs_1_), channel_id=1, source_target_pairs={{0,1},{1,0},{2,3},{3,2},{4,5},{5,4},{6,7},{7,6},{8,9},{9,8},{10,11... | collective-permute-start | bytes 2359304 | tf_op jit(solution)/shard_map/tokens_core/ppermute | solution.py:120
  50.1 17.9 %collective-permute-start.8 = (bf16[128,3072]{1,0:T(8,128)(2,1)}, bf16[128,3072]{1,0:T(8,128)(2,1)}, u32[]{:S(2)}, u32[]{:S(2)}) collective-permute-start(bf16[128,3072]{1,0:T(8,128)(2,1)} %collective-permute-done.4.refs_2_), channel_id=1, source_target_pairs={{0,1},{1,0},{2,3},{3,2},{4,5},{5,4},{6,7},{7,6},{8,9},{9,8},{10,11... | collective-permute-start | bytes 2359304 | tf_op jit(solution)/shard_map/tokens_core/ppermute | solution.py:120
  68.1 1.9 collective-permute-start.9
  71.1 4.2 %all-to-all-start.1 = ((bf16[4,512,256]{2,1,0:T(8,128)(2,1)}), bf16[4,512,256]{2,1,0:T(8,128)(2,1)S(1)}, u32[]{:S(2)}, u32[]{:S(2)}) async-start(bf16[4,512,256]{2,1,0:T(8,128)(2,1)} %broadcast_in_dim.104), calls=%async_computation.1 | async-start | bytes 2097152 | tf_op jit(solution)/shard_map/gather_y/all_to_all | solution.py:30
  75.3 14.4 %all-to-all-done.1 = bf16[4,512,256]{2,1,0:T(8,128)(2,1)S(1)} async-done(((bf16[4,512,256]{2,1,0:T(8,128)(2,1)}), bf16[4,512,256]{2,1,0:T(8,128)(2,1)S(1)}, u32[]{:S(2)}, u32[]{:S(2)}) %all-to-all-start.1) | async-done | bytes 1048608 | tf_op jit(solution)/shard_map/gather_y/all_to_all | solution.py:30
  89.7 4.7 %project.1 = bf16[256,1024]{1,0:T(8,128)(2,1)S(1)} custom-call(bf16[128,3072]{1,0:T(8,128)(2,1)S(1)} %get-tuple-element.7.refs_0_, bf16[128,3072]{1,0:T(8,128)(2,1)S(1)} %collective-permute-done.3.refs_1_, bf16[128,3072]{1,0:T(8,128)(2,1)} %collective-permute-done.4.refs_2_, bf16[128,3072]{1,0:T(8,128)(2,1)} %collective-permute-done.5.refs_3_, ...), custom_call_target="tpu_custom_call" | custom-call | flops 2147483648 | bytes 8388608 | tf_op jit(solution)/shard_map/project/project/pallas_call | solution.py:88
  95.4 9.3 %all-to-all-start.2 = ((bf16[64,4,1024]{2,1,0:T(4,128)(2,1)}), bf16[64,4,1024]{2,1,0:T(4,128)(2,1)S(1)}, u32[]{:S(2)}, u32[]{:S(2)}) async-start(bf16[64,4,1024]{2,1,0:T(4,128)(2,1)} %reshape.263), calls=%async_computation.2 | async-start | bytes 1048576 | tf_op jit(solution)/shard_map/reduce_plane/all_to_all | solution.py:30
  104.7 4.3 %collective-permute-start = (f32[2,1024]{1,0:T(2,128)S(1)}, f32[2,1024]{1,0:T(2,128)S(1)}, u32[]{:S(2)}, u32[]{:S(2)}) collective-permute-start(f32[2,1024]{1,0:T(2,128)S(1)} %pad_maximum_fusion), channel_id=1, source_target_pairs={{0,6},{2,0},{4,2},{6,4},{1,7},{3,1},{5,3},{7,5},{8,14},{10,8},{12,... | collective-permute-start | bytes 24584 | tf_op jit(solution)/shard_map/moments_z/ppermute | solution.py:130
  109.0 9.7 %collective-permute-start.1 = (f32[2,1024]{1,0:T(2,128)S(1)}, f32[2,1024]{1,0:T(2,128)S(1)}, u32[]{:S(2)}, u32[]{:S(2)}) collective-permute-start(f32[2,1024]{1,0:T(2,128)S(1)} %pad_maximum_fusion), channel_id=1, source_target_pairs={{0,4},{2,6},{4,0},{6,2},{1,5},{3,7},{5,1},{7,3},{8,12},{10,14},{12... | collective-permute-start | bytes 24584 | tf_op jit(solution)/shard_map/moments_z/ppermute | solution.py:130
  118.7 4.3 %collective-permute-start.2 = (f32[2,1024]{1,0:T(2,128)S(1)}, f32[2,1024]{1,0:T(2,128)S(1)}, u32[]{:S(2)}, u32[]{:S(2)}) collective-permute-start(f32[2,1024]{1,0:T(2,128)S(1)} %pad_maximum_fusion), channel_id=1, source_target_pairs={{0,2},{2,4},{4,6},{6,0},{1,3},{3,5},{5,7},{7,1},{8,10},{10,12},{12... | collective-permute-start | bytes 24584 | tf_op jit(solution)/shard_map/moments_z/ppermute | solution.py:130
  124.0 8.2 %all-to-all-start.3 = ((f32[4,4,1024]{2,1,0:T(4,128)}), f32[4,4,1024]{2,1,0:T(4,128)S(1)}, u32[]{:S(2)}, u32[]{:S(2)}) async-start(f32[4,4,1024]{2,1,0:T(4,128)} %broadcast_in_dim.105), calls=%async_computation.3 | async-start | bytes 131072 | tf_op jit(solution)/shard_map/reduce_z/all_to_all | solution.py:30
  132.2 12.2 %all-to-all-done.3 = f32[4,4,1024]{2,1,0:T(4,128)S(1)} async-done(((f32[4,4,1024]{2,1,0:T(4,128)}), f32[4,4,1024]{2,1,0:T(4,128)S(1)}, u32[]{:S(2)}, u32[]{:S(2)}) %all-to-all-start.3) | async-done | bytes 65568 | tf_op jit(solution)/shard_map/reduce_z/all_to_all | solution.py:30
  144.5 1.3 broadcast_in_dim.114
  145.8 15.4 %all-to-all-start.4 = ((bf16[128,4,1024]{2,1,0:T(4,128)(2,1)}), bf16[128,4,1024]{2,1,0:T(4,128)(2,1)S(1)}, u32[]{:S(2)}, u32[]{:S(2)}) async-start(bf16[128,4,1024]{2,1,0:T(4,128)(2,1)} %broadcast_in_dim.114), calls=%async_computation.4 | async-start | bytes 2097152 | tf_op jit(solution)/shard_map/spread_plane/all_to_all | solution.py:30
  161.9 28.9 %all-to-all-done.4 = bf16[128,4,1024]{2,1,0:T(4,128)(2,1)S(1)} async-done(((bf16[128,4,1024]{2,1,0:T(4,128)(2,1)}), bf16[128,4,1024]{2,1,0:T(4,128)(2,1)S(1)}, u32[]{:S(2)}, u32[]{:S(2)}) %all-to-all-start.4) | async-done | bytes 1048608 | tf_op jit(solution)/shard_map/spread_plane/all_to_all | solution.py:30
  191.1 1.8 convolution_convert_fusion
  (45 shorter events, 8.5 us)
Async XLA Ops:
  0.6 1.0 copy-start
  2.0 9.6 %collective-permute-start.10 = (bf16[32,256]{1,0:T(8,128)(2,1)S(1)}, bf16[32,256]{1,0:T(8,128)(2,1)S(1)}, u32[]{:S(2)}, u32[]{:S(2)}) collective-permute-start(bf16[32,256]{1,0:T(8,128)(2,1)S(1)} %broadcast_select_fusion), channel_id=1, source_target_pairs={{0,1},{1,0},{2,3},{3,2},{4,5},{5,4},{6,7},{7,6},{8,9},{9,8},{10,11... | collective-permute-start | bytes 49160 | tf_op jit(solution)/shard_map/gather_core/ppermute | solution.py:112
  12.3 57.7 %all-to-all-start = ((bf16[16,32,256]{2,1,0:T(8,128)(2,1)}), bf16[16,32,256]{2,1,0:T(8,128)(2,1)S(1)}, u32[]{:S(2)}, u32[]{:S(2)}) async-start(bf16[16,32,256]{2,1,0:T(8,128)(2,1)} %broadcast_in_dim.102), calls=%async_computation | async-start | bytes 524288 | tf_op jit(solution)/shard_map/gather_z/all_to_all | solution.py:30
  21.9 1.6 copy-start.1
  23.5 0.9 copy-start.2
  25.1 21.6 %collective-permute-start.3 = (bf16[128,3072]{1,0:T(8,128)(2,1)S(1)}, bf16[128,3072]{1,0:T(8,128)(2,1)S(1)}, u32[]{:S(2)}, u32[]{:S(2)}) collective-permute-start(bf16[128,3072]{1,0:T(8,128)(2,1)S(1)} %get-tuple-element.8), channel_id=1, source_target_pairs={{0,32},{32,64},{64,96},{96,0},{1,33},{33,65},{65,97},{97,1},{2,34}... | collective-permute-start | bytes 2359304 | tf_op jit(solution)/shard_map/tokens_x/ppermute | solution.py:117
  28.2 21.9 %collective-permute-start.4 = (bf16[128,3072]{1,0:T(8,128)(2,1)S(1)}, bf16[128,3072]{1,0:T(8,128)(2,1)}, u32[]{:S(2)}, u32[]{:S(2)}) collective-permute-start(bf16[128,3072]{1,0:T(8,128)(2,1)S(1)} %get-tuple-element.9), channel_id=1, source_target_pairs={{0,96},{32,0},{64,32},{96,64},{1,97},{33,1},{65,33},{97,65},{2,98}... | collective-permute-start | bytes 2359304 | tf_op jit(solution)/shard_map/tokens_x/ppermute | solution.py:117
  31.6 36.5 %collective-permute-start.5 = (bf16[128,3072]{1,0:T(8,128)(2,1)S(1)}, bf16[128,3072]{1,0:T(8,128)(2,1)}, u32[]{:S(2)}, u32[]{:S(2)}) collective-permute-start(bf16[128,3072]{1,0:T(8,128)(2,1)S(1)} %get-tuple-element.10), channel_id=1, source_target_pairs={{0,64},{32,96},{64,0},{96,32},{1,65},{33,97},{65,1},{97,33},{2,66}... | collective-permute-start | bytes 2359304 | tf_op jit(solution)/shard_map/tokens_x/ppermute | solution.py:117
  35.0 40.3 %collective-permute-start.6 = (bf16[128,3072]{1,0:T(8,128)(2,1)S(1)}, bf16[128,3072]{1,0:T(8,128)(2,1)}, u32[]{:S(2)}, u32[]{:S(2)}) collective-permute-start(bf16[128,3072]{1,0:T(8,128)(2,1)S(1)} %get-tuple-element.7.refs_0_), channel_id=1, source_target_pairs={{0,1},{1,0},{2,3},{3,2},{4,5},{5,4},{6,7},{7,6},{8,9},{9,8},{10,11... | collective-permute-start | bytes 2359304 | tf_op jit(solution)/shard_map/tokens_core/ppermute | solution.py:120
  46.6 28.7 %collective-permute-start.7 = (bf16[128,3072]{1,0:T(8,128)(2,1)S(1)}, bf16[128,3072]{1,0:T(8,128)(2,1)}, u32[]{:S(2)}, u32[]{:S(2)}) collective-permute-start(bf16[128,3072]{1,0:T(8,128)(2,1)S(1)} %collective-permute-done.3.refs_1_), channel_id=1, source_target_pairs={{0,1},{1,0},{2,3},{3,2},{4,5},{5,4},{6,7},{7,6},{8,9},{9,8},{10,11... | collective-permute-start | bytes 2359304 | tf_op jit(solution)/shard_map/tokens_core/ppermute | solution.py:120
  50.1 25.2 %collective-permute-start.8 = (bf16[128,3072]{1,0:T(8,128)(2,1)}, bf16[128,3072]{1,0:T(8,128)(2,1)}, u32[]{:S(2)}, u32[]{:S(2)}) collective-permute-start(bf16[128,3072]{1,0:T(8,128)(2,1)} %collective-permute-done.4.refs_2_), channel_id=1, source_target_pairs={{0,1},{1,0},{2,3},{3,2},{4,5},{5,4},{6,7},{7,6},{8,9},{9,8},{10,11... | collective-permute-start | bytes 2359304 | tf_op jit(solution)/shard_map/tokens_core/ppermute | solution.py:120
  68.1 7.2 %collective-permute-start.9 = (bf16[128,3072]{1,0:T(8,128)(2,1)}, bf16[128,3072]{1,0:T(8,128)(2,1)}, u32[]{:S(2)}, u32[]{:S(2)}) collective-permute-start(bf16[128,3072]{1,0:T(8,128)(2,1)} %collective-permute-done.5.refs_3_), channel_id=1, source_target_pairs={{0,1},{1,0},{2,3},{3,2},{4,5},{5,4},{6,7},{7,6},{8,9},{9,8},{10,11... | collective-permute-start | bytes 2359304 | tf_op jit(solution)/shard_map/tokens_core/ppermute | solution.py:120
  71.1 18.6 %all-to-all-start.1 = ((bf16[4,512,256]{2,1,0:T(8,128)(2,1)}), bf16[4,512,256]{2,1,0:T(8,128)(2,1)S(1)}, u32[]{:S(2)}, u32[]{:S(2)}) async-start(bf16[4,512,256]{2,1,0:T(8,128)(2,1)} %broadcast_in_dim.104), calls=%async_computation.1 | async-start | bytes 2097152 | tf_op jit(solution)/shard_map/gather_y/all_to_all | solution.py:30
  94.4 10.3 %copy-start.3 = (f32[1,1024]{1,0:T(1,128)S(1)}, f32[1,1024]{1,0:T(1,128)}, u32[]{:S(2)}) copy-start(f32[1,1024]{1,0:T(1,128)} %param.9) | copy-start | bytes 12292
  94.4 10.3 %copy-start.4 = (f32[1,1024]{1,0:T(1,128)S(1)}, f32[1,1024]{1,0:T(1,128)}, u32[]{:S(2)}) copy-start(f32[1,1024]{1,0:T(1,128)} %param.8) | copy-start | bytes 12292
  95.4 27.8 %all-to-all-start.2 = ((bf16[64,4,1024]{2,1,0:T(4,128)(2,1)}), bf16[64,4,1024]{2,1,0:T(4,128)(2,1)S(1)}, u32[]{:S(2)}, u32[]{:S(2)}) async-start(bf16[64,4,1024]{2,1,0:T(4,128)(2,1)} %reshape.263), calls=%async_computation.2 | async-start | bytes 1048576 | tf_op jit(solution)/shard_map/reduce_plane/all_to_all | solution.py:30
  104.7 18.4 %collective-permute-start = (f32[2,1024]{1,0:T(2,128)S(1)}, f32[2,1024]{1,0:T(2,128)S(1)}, u32[]{:S(2)}, u32[]{:S(2)}) collective-permute-start(f32[2,1024]{1,0:T(2,128)S(1)} %pad_maximum_fusion), channel_id=1, source_target_pairs={{0,6},{2,0},{4,2},{6,4},{1,7},{3,1},{5,3},{7,5},{8,14},{10,8},{12,... | collective-permute-start | bytes 24584 | tf_op jit(solution)/shard_map/moments_z/ppermute | solution.py:130
  109.0 14.1 %collective-permute-start.1 = (f32[2,1024]{1,0:T(2,128)S(1)}, f32[2,1024]{1,0:T(2,128)S(1)}, u32[]{:S(2)}, u32[]{:S(2)}) collective-permute-start(f32[2,1024]{1,0:T(2,128)S(1)} %pad_maximum_fusion), channel_id=1, source_target_pairs={{0,4},{2,6},{4,0},{6,2},{1,5},{3,7},{5,1},{7,3},{8,12},{10,14},{12... | collective-permute-start | bytes 24584 | tf_op jit(solution)/shard_map/moments_z/ppermute | solution.py:130
  118.7 13.5 %collective-permute-start.2 = (f32[2,1024]{1,0:T(2,128)S(1)}, f32[2,1024]{1,0:T(2,128)S(1)}, u32[]{:S(2)}, u32[]{:S(2)}) collective-permute-start(f32[2,1024]{1,0:T(2,128)S(1)} %pad_maximum_fusion), channel_id=1, source_target_pairs={{0,2},{2,4},{4,6},{6,0},{1,3},{3,5},{5,7},{7,1},{8,10},{10,12},{12... | collective-permute-start | bytes 24584 | tf_op jit(solution)/shard_map/moments_z/ppermute | solution.py:130
  124.0 20.4 %all-to-all-start.3 = ((f32[4,4,1024]{2,1,0:T(4,128)}), f32[4,4,1024]{2,1,0:T(4,128)S(1)}, u32[]{:S(2)}, u32[]{:S(2)}) async-start(f32[4,4,1024]{2,1,0:T(4,128)} %broadcast_in_dim.105), calls=%async_computation.3 | async-start | bytes 131072 | tf_op jit(solution)/shard_map/reduce_z/all_to_all | solution.py:30
  145.8 45.0 %all-to-all-start.4 = ((bf16[128,4,1024]{2,1,0:T(4,128)(2,1)}), bf16[128,4,1024]{2,1,0:T(4,128)(2,1)S(1)}, u32[]{:S(2)}, u32[]{:S(2)}) async-start(bf16[128,4,1024]{2,1,0:T(4,128)(2,1)} %broadcast_in_dim.114), calls=%async_computation.4 | async-start | bytes 2097152 | tf_op jit(solution)/shard_map/spread_plane/all_to_all | solution.py:30

commit v4 on v3

--- a/solution.py
+++ b/solution.py
@@ -15,10 +15,17 @@
 adam_epsilon = 1e-08
 
 AXES = ("z_lo", "x", "y", "z_hi", "core")
+Z = ("z_hi", "z_lo")
 RANK = 512
 TOKENS = 65536
 KVW = 1024
 QUARTER = 2048
+
+
+def owner_row(core, xy, z):
+    x, y = xy >> 2, xy & 3
+    z_hi, z_lo = z >> 2, z & 3
+    return (((z_lo * 4 + x) * 4 + y) * 4 + z_hi) * 2 + core
 
 
 def reorder(basis, rows):
@@ -63,16 +70,39 @@
     )(x_at[None], tokens, cotangent)
 
 
+def join_kernel(*refs):
+    *pieces, _, out_ref = refs
+    for k, piece in enumerate(pieces):
+        rows = piece.shape[0]
+        out_ref[k * rows : k * rows + rows] = piece[...]
+
+
+def join(pieces, other):
+    rows, columns = pieces[0].shape
+    vmem = pl.BlockSpec(memory_space=pltpu.VMEM)
+    return pl.pallas_call(
+        join_kernel,
+        in_specs=[vmem] * len(pieces) + [pl.BlockSpec(memory_space=pl.ANY)],
+        out_specs=vmem,
+        out_shape=jax.ShapeDtypeStruct((rows * len(pieces), columns), jnp.bfloat16),
+        compiler_params=pltpu.CompilerParams(vmem_limit_bytes=16 * 2**20),
+        cost_estimate=pl.CostEstimate(flops=0, bytes_accessed=2**20, transcendentals=0),
+        name="join",
+    )(*pieces, other)
+
+
 def project_kernel(*refs):
     *pieces, whole_ref, out_ref, split_ref = refs
     whole = whole_ref[...]
-    count = len(pieces)
-    for k, piece in enumerate(pieces):
+    at, tokens = 0, split_ref.shape[0] // 2
+    for piece in pieces:
+        rows = piece.shape[0]
         reduced = jnp.dot(piece[:, :QUARTER], whole, preferred_element_type=jnp.float32)
         high = reduced.astype(jnp.bfloat16)
         low = (reduced - high.astype(jnp.float32)).astype(jnp.bfloat16)
-        split_ref[k * 128 : k * 128 + 128] = high
-        split_ref[(count + k) * 128 : (count + k) * 128 + 128] = low
+        split_ref[at : at + rows] = high
+        split_ref[tokens + at : tokens + at + rows] = low
+        at += rows
     for n in range(0, KVW, 256):
         columns = [piece[:, QUARTER + n : QUARTER + n + 256] for piece in pieces]
         out_ref[:, n : n + 256] = lax.dot_general(
@@ -80,7 +110,7 @@
             jnp.concatenate(columns + columns, axis=0),
             (((0,), (0,)), ((), ())),
             preferred_element_type=jnp.float32,
-        ).astype(jnp.bfloat16)
+        )
 
 
 def project(pieces, whole):
@@ -89,8 +119,8 @@
         project_kernel,
         in_specs=[vmem] * (len(pieces) + 1),
         out_specs=vmem,
-        out_shape=jax.ShapeDtypeStruct((256, KVW), jnp.bfloat16),
-        scratch_shapes=[pltpu.VMEM((2 * 128 * len(pieces), 256), jnp.bfloat16)],
+        out_shape=jax.ShapeDtypeStruct((256, KVW), jnp.float32),
+        scratch_shapes=[pltpu.VMEM((2048, 256), jnp.bfloat16)],
         compiler_params=pltpu.CompilerParams(vmem_limit_bytes=40 * 2**20),
         cost_estimate=pl.CostEstimate(
             flops=2 * 2**30, bytes_accessed=8 * 2**20, transcendentals=0
@@ -100,12 +130,12 @@
 
 
 def local(normed_input, value_cotangent, basis, first_moment, second_moment):
-    x_at, z_hi_at, z_lo_at, core_at = (lax.axis_index(a) for a in ("x", "z_hi", "z_lo", "core"))
+    x_at, z_lo_at, core_at = (lax.axis_index(a) for a in ("x", "z_lo", "core"))
     swap = [(0, 1), (1, 0)]
     place = jnp.arange(RANK)
     with jax.named_scope("order"):
-        ranked = reorder(basis, (place & 255) * 2 + (place >> 8))
-        decoder = reorder(basis, (place & ~7) + (place & 3) * 2 + (place >> 2 & 1))
+        ranked = reorder(basis, owner_row(place >> 8, place >> 4 & 15, place & 15))
+        decoder = reorder(basis, owner_row(place >> 4 & 1, place >> 5, place & 15))
     with jax.named_scope("gather_core"):
         rows = lax.dynamic_slice_in_dim(ranked, (x_at >> 1) * 128 + z_lo_at * 32, 32, 0)
         low, high = rows[:, :256], rows[:, 256:]
@@ -116,29 +146,22 @@
         pieces = [packed[0]] + [
             lax.ppermute(packed[k], "x", [(i, (i + k) % 4) for i in range(4)]) for k in (1, 3, 2)
         ]
-    with jax.named_scope("tokens_core"):
-        pieces += [lax.ppermute(piece, "core", swap) for piece in pieces]
     with jax.named_scope("gather_z"):
-        line = spread(chunk, ("z_hi", "z_lo"), 16).reshape(512, 256)
+        line = spread(join([chunk], packed[1]), Z, 16).reshape(512, 256)
     with jax.named_scope("gather_y"):
         whole = spread(line, "y", 4).reshape(QUARTER, 256)
-    with jax.named_scope("moments_z"):
-        own = jnp.concatenate([first_moment, second_moment])
-        row = lax.broadcasted_iota(jnp.int32, (4, KVW), 0)
-        first = second = jnp.zeros((4, KVW), jnp.float32)
-        for k in range(4):
-            theirs = lax.ppermute(own, "z_hi", [(i, (i + k) % 4) for i in range(4)]) if k else own
-            place_of = row == ((z_hi_at - k) & 3)
-            first = jnp.where(place_of, theirs[:1], first)
-            second = jnp.where(place_of, theirs[1:], second)
+    with jax.named_scope("tokens_core"):
+        held = join(pieces, whole)
+        held = [held, lax.ppermute(held, "core", swap)]
     with jax.named_scope("project"):
-        partial = project(pieces, whole)
-    with jax.named_scope("reduce_plane"):
-        parts = exchange(partial.reshape(64, 4, KVW), ("z_lo", "x", "y"))
-        summed = jnp.sum(parts.astype(jnp.float32), axis=0)
+        partial = project(held, whole)
+    with jax.named_scope("reduce_xy"):
+        summed = jnp.sum(exchange(partial.reshape(16, 16, KVW), ("x", "y")), axis=0)
     with jax.named_scope("reduce_z"):
-        share = jnp.sum(spread(summed, "z_hi", 4), axis=0) * (1.0 / math.sqrt(TOKENS))
+        share = jnp.sum(exchange(summed.reshape(16, 8, 128), Z), axis=0)
+        share = share * (1.0 / math.sqrt(TOKENS))
     with jax.named_scope("adam"):
+        first, second = first_moment.reshape(8, 128), second_moment.reshape(8, 128)
         new_first = beta_first * first + (1.0 - beta_first) * share
         new_second = beta_second * second + (1.0 - beta_second) * share * share
         corr_first = 1.0 - beta_first**STEP
@@ -146,14 +169,13 @@
         normalized = (
             new_first / corr_first / (jnp.sqrt(new_second / corr_second) + adam_epsilon)
         ).astype(jnp.bfloat16)
-    with jax.named_scope("spread_plane"):
-        step = spread(normalized, ("z_lo", "x", "y", "core"), 128).reshape(RANK, KVW)
+    with jax.named_scope("spread_z"):
+        column = spread(normalized, Z, 16).reshape(16, KVW)
+    with jax.named_scope("spread_xy"):
+        step = spread(column, ("x", "y", "core"), 32).reshape(RANK, KVW)
     with jax.named_scope("decode"):
         update = jnp.dot(decoder, step, preferred_element_type=jnp.float32).astype(jnp.bfloat16)
-    with jax.named_scope("own"):
-        own_first = lax.dynamic_slice_in_dim(new_first, z_hi_at, 1, 0)
-        own_second = lax.dynamic_slice_in_dim(new_second, z_hi_at, 1, 0)
-    return own_first, own_second, update
+    return new_first.reshape(1, KVW), new_second.reshape(1, KVW), update
 
 
 def solution(mesh):

time: 194 us -> 169 us (0.87)
  starting transfers between devices: 110 us -> 55.4 us
  blocking collectives: 0 us -> 37.4 us
  waiting for transfers between devices: 64.5 us -> 58.2 us
  local copies, waits for them, and re-layouts: 9.11 us -> 7.02 us
    ppermute x7 -> x1, starting transfers between devices: 45 us -> 3.25 us  [local(): held = [held, lax.ppermute(held, 'core', swap)]]
    all_to_all x0 -> x2, blocking collectives: none -> 37.4 us  [exchange(): return lax.all_to_all(blocks, axes, 0, 0, tiled=True)]
    all_to_all x5 -> x4, waiting for transfers between devices: 55.5 us -> 32.5 us  [exchange(): return lax.all_to_all(blocks, axes, 0, 0, tiled=True)]
    all_to_all x5 -> x4, starting transfers between devices: 46.6 us -> 33.4 us  [exchange(): return lax.all_to_all(blocks, axes, 0, 0, tiled=True)]
    ppermute x3, waiting for transfers between devices: 8.23 us -> 20.4 us  [local(): lax.ppermute(packed[k], 'x', [(i, (i + k) % 4) for i in range(4)])]
    ppermute x7 -> x1, waiting for transfers between devices: 0.02 us -> 5.26 us  [local(): held = [held, lax.ppermute(held, 'core', swap)]]
    pallas_call x1, Pallas kernels: 4.67 us -> 2.45 us  [project(): pl.pallas_call(project_kernel, in_specs=[vmem] * (len(pieces) + 1), out_s...]
    unnamed x10 -> x12, local copies, waits for them, and re-layouts: 3.47 us -> 4.12 us
  transfers between devices with their start and end apart: 16 -> 9, of which waited for: 5 -> 7; matrix products, arithmetic and copies ran while one was open for 1% -> 1% of each run, Pallas kernels for 0% -> 1%
where the time goes in v4:
time: 169 us; the launch traced here: 168 us
  waiting for transfers between devices  58.2 us (34%)
  starting transfers between devices  55.4 us (33%)
  blocking collectives  37.4 us (22%)
  local copies, waits for them, and re-layouts  7.02 us (4%)
  Pallas kernels  6.15 us (4%)
  matrix products  2.19 us (1%)
    all_to_all x2, blocking collectives, exchange(): return lax.all_to_all(blocks, axes, 0, 0, tiled=True)  37.4 us
    all_to_all x4, starting transfers between devices, exchange(): return lax.all_to_all(blocks, axes, 0, 0, tiled=True)  33.4 us
    all_to_all x4, waiting for transfers between devices, exchange(): return lax.all_to_all(blocks, axes, 0, 0, tiled=True)  32.5 us
    ppermute x3, waiting for transfers between devices, local(): lax.ppermute(packed[k], 'x', [(i, (i + k) % 4) for i in range(4)])  20.4 us
    ppermute x3, starting transfers between devices, local(): lax.ppermute(packed[k], 'x', [(i, (i + k) % 4) for i in range(4)])  9.94 us
    ppermute x1, starting transfers between devices, local(): theirs = lax.ppermute(jnp.where(core_at == 0, high, low), 'core', swap)  8.78 us
    ppermute x1, waiting for transfers between devices, local(): held = [held, lax.ppermute(held, 'core', swap)]  5.26 us
    unnamed x12, local copies, waits for them, and re-layouts  4.12 us
  transfers between devices with their start and end apart: 9, of which 7 were waited for; matrix products, arithmetic and copies ran while one was open for 1% of the time, Pallas kernels for 1%

profile of v4, /device:TPU:1, one launch (start us, length us, event | category | flops | bytes accessed | tf_op | source)
XLA Modules:
  0.0 167.9 jit_solution(2767882466626177463)
XLA Ops:
  2.0 8.8 %collective-permute-start.3 = (bf16[32,256]{1,0:T(8,128)(2,1)S(1)}, bf16[32,256]{1,0:T(8,128)(2,1)S(1)}, u32[]{:S(2)}, u32[]{:S(2)}) collective-permute-start(bf16[32,256]{1,0:T(8,128)(2,1)S(1)} %broadcast_select_fusion), channel_id=1, source_target_pairs={{0,1},{1,0},{2,3},{3,2},{4,5},{5,4},{6,7},{7,6},{8,9},{9,8},{10,11... | collective-permute-start | bytes 49160 | tf_op jit(solution)/shard_map/gather_core/ppermute | solution.py:142
  10.8 1.6 copy-done.1
  13.3 2.1 %pack.1 = (bf16[128,3072]{1,0:T(8,128)(2,1)S(1)}, bf16[128,3072]{1,0:T(8,128)(2,1)}, bf16[128,3072]{1,0:T(8,128)(2,1)}, bf16[128,3072]{1,0:T(8,128)(2,1)}) custom-call(s32[1]{0:T(128)} %bitcast.x_ref, bf16[128,8192]{1,0:T(8,128)(2,1)S(1)} %copy-done.1, bf16[128,1024]{1,0:T(8,128)(2,1)S(1)} %copy-done.2), custom_call_target="tpu_custom_call" | custom-call | bytes 6291456 | tf_op jit(solution)/shard_map/tokens_x/pack/pallas_call | solution.py:57
  16.2 9.5 %all-to-all-start = ((bf16[16,32,256]{2,1,0:T(8,128)(2,1)}), bf16[16,32,256]{2,1,0:T(8,128)(2,1)S(1)}, u32[]{:S(2)}, u32[]{:S(2)}) async-start(bf16[16,32,256]{2,1,0:T(8,128)(2,1)} %broadcast_in_dim.15), calls=%async_computation | async-start | bytes 524288 | tf_op jit(solution)/shard_map/gather_z/all_to_all | solution.py:37
  25.8 3.1 %collective-permute-start = (bf16[128,3072]{1,0:T(8,128)(2,1)}, bf16[128,3072]{1,0:T(8,128)(2,1)S(1)}, u32[]{:S(2)}, u32[]{:S(2)}) collective-permute-start(bf16[128,3072]{1,0:T(8,128)(2,1)} %get-tuple-element.8.refs_1_), channel_id=1, source_target_pairs={{0,32},{32,64},{64,96},{96,0},{1,33},{33,65},{65,97},{97,1},{2,34}... | collective-permute-start | bytes 2359304 | tf_op jit(solution)/shard_map/tokens_x/ppermute | solution.py:147
  28.9 3.4 %collective-permute-start.1 = (bf16[128,3072]{1,0:T(8,128)(2,1)}, bf16[128,3072]{1,0:T(8,128)(2,1)}, u32[]{:S(2)}, u32[]{:S(2)}) collective-permute-start(bf16[128,3072]{1,0:T(8,128)(2,1)} %get-tuple-element.9), channel_id=1, source_target_pairs={{0,96},{32,0},{64,32},{96,64},{1,97},{33,1},{65,33},{97,65},{2,98}... | collective-permute-start | bytes 2359304 | tf_op jit(solution)/shard_map/tokens_x/ppermute | solution.py:147
  32.3 3.4 %collective-permute-start.2 = (bf16[128,3072]{1,0:T(8,128)(2,1)}, bf16[128,3072]{1,0:T(8,128)(2,1)}, u32[]{:S(2)}, u32[]{:S(2)}) collective-permute-start(bf16[128,3072]{1,0:T(8,128)(2,1)} %get-tuple-element.10), channel_id=1, source_target_pairs={{0,64},{32,96},{64,0},{96,32},{1,65},{33,97},{65,1},{97,33},{2,66}... | collective-permute-start | bytes 2359304 | tf_op jit(solution)/shard_map/tokens_x/ppermute | solution.py:147
  35.7 4.5 %all-to-all-done = bf16[16,32,256]{2,1,0:T(8,128)(2,1)S(1)} async-done(((bf16[16,32,256]{2,1,0:T(8,128)(2,1)}), bf16[16,32,256]{2,1,0:T(8,128)(2,1)S(1)}, u32[]{:S(2)}, u32[]{:S(2)}) %all-to-all-start) | async-done | bytes 262176 | tf_op jit(solution)/shard_map/gather_z/all_to_all | solution.py:37
  41.3 4.2 %all-to-all-start.1 = ((bf16[4,512,256]{2,1,0:T(8,128)(2,1)}), bf16[4,512,256]{2,1,0:T(8,128)(2,1)S(1)}, u32[]{:S(2)}, u32[]{:S(2)}) async-start(bf16[4,512,256]{2,1,0:T(8,128)(2,1)} %broadcast_in_dim.34), calls=%async_computation.1 | async-start | bytes 2097152 | tf_op jit(solution)/shard_map/gather_y/all_to_all | solution.py:37
  45.4 2.5 %collective-permute-done.refs_1_ = bf16[128,3072]{1,0:T(8,128)(2,1)S(1)} collective-permute-done((bf16[128,3072]{1,0:T(8,128)(2,1)}, bf16[128,3072]{1,0:T(8,128)(2,1)S(1)}, u32[]{:S(2)}, u32[]{:S(2)}) %collective-permute-start) | collective-permute-done | bytes 786464 | tf_op jit(solution)/shard_map/tokens_x/ppermute | solution.py:147
  47.9 1.7 %collective-permute-done.1.refs_2_ = bf16[128,3072]{1,0:T(8,128)(2,1)} collective-permute-done((bf16[128,3072]{1,0:T(8,128)(2,1)}, bf16[128,3072]{1,0:T(8,128)(2,1)}, u32[]{:S(2)}, u32[]{:S(2)}) %collective-permute-start.1) | collective-permute-done | bytes 786464 | tf_op jit(solution)/shard_map/tokens_x/ppermute | solution.py:147
  49.6 16.2 %collective-permute-done.2.refs_3_ = bf16[128,3072]{1,0:T(8,128)(2,1)} collective-permute-done((bf16[128,3072]{1,0:T(8,128)(2,1)}, bf16[128,3072]{1,0:T(8,128)(2,1)}, u32[]{:S(2)}, u32[]{:S(2)}) %collective-permute-start.2) | collective-permute-done | bytes 786464 | tf_op jit(solution)/shard_map/tokens_x/ppermute | solution.py:147
  65.9 1.6 join.3.refs_0_
  67.5 3.2 %collective-permute-start.4 = (bf16[512,3072]{1,0:T(8,128)(2,1)S(1)}, bf16[512,3072]{1,0:T(8,128)(2,1)S(1)}, u32[]{:S(2)}, u32[]{:S(2)}) collective-permute-start(bf16[512,3072]{1,0:T(8,128)(2,1)S(1)} %join.3.refs_0_), channel_id=1, source_target_pairs={{0,1},{1,0},{2,3},{3,2},{4,5},{5,4},{6,7},{7,6},{8,9},{9,8},{10,11... | collective-permute-start | bytes 9437192 | tf_op jit(solution)/shard_map/tokens_core/ppermute | solution.py:155
  70.7 5.3 %collective-permute-done.4.refs_1_ = bf16[512,3072]{1,0:T(8,128)(2,1)S(1)} collective-permute-done((bf16[512,3072]{1,0:T(8,128)(2,1)S(1)}, bf16[512,3072]{1,0:T(8,128)(2,1)S(1)}, u32[]{:S(2)}, u32[]{:S(2)}) %collective-permute-start.4) | collective-permute-done | bytes 3145760 | tf_op jit(solution)/shard_map/tokens_core/ppermute | solution.py:155
  76.0 2.5 %project.1 = f32[256,1024]{1,0:T(8,128)S(1)} custom-call(bf16[512,3072]{1,0:T(8,128)(2,1)S(1)} %join.3.refs_0_, bf16[512,3072]{1,0:T(8,128)(2,1)S(1)} %collective-permute-done.4.refs_1_, bf16[2048,256]{1,0:T(8,128)(2,1)S(1)} %bitcast.21), custom_call_target="tpu_custom_call" | custom-call | flops 2147483648 | bytes 8388608 | tf_op jit(solution)/shard_map/project/project/pallas_call | solution.py:118
  78.5 23.2 %all_to_all.30 = f32[16,16,1024]{2,1,0:T(8,128)S(1)} all-to-all(f32[16,16,1024]{2,1,0:T(8,128)S(1)} %bitcast.22), channel_id=1, replica_groups=mesh['z_lo'=4,'x'=4,'y'=4,'z_hi'=4,'core'=2] {'x','y'}, dimensions={0} | all-to-all | bytes 2097152 | tf_op jit(solution)/shard_map/reduce_xy/all_to_all | solution.py:37
  102.3 11.4 %all-to-all-start.3 = ((f32[16,8,128]{2,1,0:T(8,128)}), f32[16,8,128]{2,1,0:T(8,128)S(1)}, u32[]{:S(2)}, u32[]{:S(2)}) async-start(f32[16,8,128]{2,1,0:T(8,128)} %bitcast.11), calls=%async_computation.3 | async-start | bytes 131072 | tf_op jit(solution)/shard_map/reduce_z/all_to_all | solution.py:37
  113.8 11.6 %all-to-all-done.3 = f32[16,8,128]{2,1,0:T(8,128)S(1)} async-done(((f32[16,8,128]{2,1,0:T(8,128)}), f32[16,8,128]{2,1,0:T(8,128)S(1)}, u32[]{:S(2)}, u32[]{:S(2)}) %all-to-all-start.3) | async-done | bytes 65568 | tf_op jit(solution)/shard_map/reduce_z/all_to_all | solution.py:37
  125.5 14.2 %all_to_all.31 = bf16[16,8,128]{2,1,0:T(8,128)(2,1)S(1)} all-to-all(bf16[16,8,128]{2,1,0:T(8,128)(2,1)S(1)} %broadcast_in_dim.35), channel_id=1, replica_groups=mesh['z_lo'=4,'x'=4,'y'=4,'z_hi'=4,'core'=2] {'z_hi','z_lo'}, dimensions={0} | all-to-all | bytes 65536 | tf_op jit(solution)/shard_map/spread_z/all_to_all | solution.py:37
  139.7 1.1 broadcast_in_dim.37
  140.8 8.2 %all-to-all-start.5 = ((bf16[32,16,1024]{2,1,0:T(8,128)(2,1)}), bf16[32,16,1024]{2,1,0:T(8,128)(2,1)S(1)}, u32[]{:S(2)}, u32[]{:S(2)}) async-start(bf16[32,16,1024]{2,1,0:T(8,128)(2,1)} %broadcast_in_dim.37), calls=%async_computation.5 | async-start | bytes 2097152 | tf_op jit(solution)/shard_map/spread_xy/all_to_all | solution.py:37
  149.7 16.4 %all-to-all-done.5 = bf16[32,16,1024]{2,1,0:T(8,128)(2,1)S(1)} async-done(((bf16[32,16,1024]{2,1,0:T(8,128)(2,1)}), bf16[32,16,1024]{2,1,0:T(8,128)(2,1)S(1)}, u32[]{:S(2)}, u32[]{:S(2)}) %all-to-all-start.5) | async-done | bytes 1048608 | tf_op jit(solution)/shard_map/spread_xy/all_to_all | solution.py:37
  166.1 1.8 %convolution_convert_fusion = bf16[256,1024]{1,0:T(8,128)(2,1)} fusion(bf16[512,1024]{1,0:T(8,128)(2,1)S(1)} %bitcast.24, bf16[256,512]{1,0:T(8,128)(2,1)S(1)} %copy-done, s32[512]{0:T(512)S(1)} %fusion.19), kind=kOutput, calls=%fused_computation | convolution fusion | flops 403570688 | bytes 1837056 | tf_op jit(solution)/shard_map/decode/dot_general | solution.py:177
  (29 shorter events, 5.5 us)
Async XLA Ops:
  0.6 1.0 copy-start
  2.0 13.5 %collective-permute-start.3 = (bf16[32,256]{1,0:T(8,128)(2,1)S(1)}, bf16[32,256]{1,0:T(8,128)(2,1)S(1)}, u32[]{:S(2)}, u32[]{:S(2)}) collective-permute-start(bf16[32,256]{1,0:T(8,128)(2,1)S(1)} %broadcast_select_fusion), channel_id=1, source_target_pairs={{0,1},{1,0},{2,3},{3,2},{4,5},{5,4},{6,7},{7,6},{8,9},{9,8},{10,11... | collective-permute-start | bytes 49160 | tf_op jit(solution)/shard_map/gather_core/ppermute | solution.py:142
  10.8 1.6 copy-start.1
  12.4 0.9 copy-start.2
  16.2 24.0 %all-to-all-start = ((bf16[16,32,256]{2,1,0:T(8,128)(2,1)}), bf16[16,32,256]{2,1,0:T(8,128)(2,1)S(1)}, u32[]{:S(2)}, u32[]{:S(2)}) async-start(bf16[16,32,256]{2,1,0:T(8,128)(2,1)} %broadcast_in_dim.15), calls=%async_computation | async-start | bytes 524288 | tf_op jit(solution)/shard_map/gather_z/all_to_all | solution.py:37
  25.8 22.2 %collective-permute-start = (bf16[128,3072]{1,0:T(8,128)(2,1)}, bf16[128,3072]{1,0:T(8,128)(2,1)S(1)}, u32[]{:S(2)}, u32[]{:S(2)}) collective-permute-start(bf16[128,3072]{1,0:T(8,128)(2,1)} %get-tuple-element.8.refs_1_), channel_id=1, source_target_pairs={{0,32},{32,64},{64,96},{96,0},{1,33},{33,65},{65,97},{97,1},{2,34}... | collective-permute-start | bytes 2359304 | tf_op jit(solution)/shard_map/tokens_x/ppermute | solution.py:147
  28.9 20.7 %collective-permute-start.1 = (bf16[128,3072]{1,0:T(8,128)(2,1)}, bf16[128,3072]{1,0:T(8,128)(2,1)}, u32[]{:S(2)}, u32[]{:S(2)}) collective-permute-start(bf16[128,3072]{1,0:T(8,128)(2,1)} %get-tuple-element.9), channel_id=1, source_target_pairs={{0,96},{32,0},{64,32},{96,64},{1,97},{33,1},{65,33},{97,65},{2,98}... | collective-permute-start | bytes 2359304 | tf_op jit(solution)/shard_map/tokens_x/ppermute | solution.py:147
  32.3 33.6 %collective-permute-start.2 = (bf16[128,3072]{1,0:T(8,128)(2,1)}, bf16[128,3072]{1,0:T(8,128)(2,1)}, u32[]{:S(2)}, u32[]{:S(2)}) collective-permute-start(bf16[128,3072]{1,0:T(8,128)(2,1)} %get-tuple-element.10), channel_id=1, source_target_pairs={{0,64},{32,96},{64,0},{96,32},{1,65},{33,97},{65,1},{97,33},{2,66}... | collective-permute-start | bytes 2359304 | tf_op jit(solution)/shard_map/tokens_x/ppermute | solution.py:147
  41.3 24.6 %all-to-all-start.1 = ((bf16[4,512,256]{2,1,0:T(8,128)(2,1)}), bf16[4,512,256]{2,1,0:T(8,128)(2,1)S(1)}, u32[]{:S(2)}, u32[]{:S(2)}) async-start(bf16[4,512,256]{2,1,0:T(8,128)(2,1)} %broadcast_in_dim.34), calls=%async_computation.1 | async-start | bytes 2097152 | tf_op jit(solution)/shard_map/gather_y/all_to_all | solution.py:37
  67.5 8.5 %collective-permute-start.4 = (bf16[512,3072]{1,0:T(8,128)(2,1)S(1)}, bf16[512,3072]{1,0:T(8,128)(2,1)S(1)}, u32[]{:S(2)}, u32[]{:S(2)}) collective-permute-start(bf16[512,3072]{1,0:T(8,128)(2,1)S(1)} %join.3.refs_0_), channel_id=1, source_target_pairs={{0,1},{1,0},{2,3},{3,2},{4,5},{5,4},{6,7},{7,6},{8,9},{9,8},{10,11... | collective-permute-start | bytes 9437192 | tf_op jit(solution)/shard_map/tokens_core/ppermute | solution.py:155
  78.4 35.4 %copy-start.4 = (f32[1,1024]{1,0:T(1,128)S(1)}, f32[1,1024]{1,0:T(1,128)}, u32[]{:S(2)}) copy-start(f32[1,1024]{1,0:T(1,128)} %param.8) | copy-start | bytes 12292
  78.4 35.4 %copy-start.3 = (f32[1,1024]{1,0:T(1,128)S(1)}, f32[1,1024]{1,0:T(1,128)}, u32[]{:S(2)}) copy-start(f32[1,1024]{1,0:T(1,128)} %param.9) | copy-start | bytes 12292
  102.3 23.1 %all-to-all-start.3 = ((f32[16,8,128]{2,1,0:T(8,128)}), f32[16,8,128]{2,1,0:T(8,128)S(1)}, u32[]{:S(2)}, u32[]{:S(2)}) async-start(f32[16,8,128]{2,1,0:T(8,128)} %bitcast.11), calls=%async_computation.3 | async-start | bytes 131072 | tf_op jit(solution)/shard_map/reduce_z/all_to_all | solution.py:37
  140.8 25.3 %all-to-all-start.5 = ((bf16[32,16,1024]{2,1,0:T(8,128)(2,1)}), bf16[32,16,1024]{2,1,0:T(8,128)(2,1)S(1)}, u32[]{:S(2)}, u32[]{:S(2)}) async-start(bf16[32,16,1024]{2,1,0:T(8,128)(2,1)} %broadcast_in_dim.37), calls=%async_computation.5 | async-start | bytes 2097152 | tf_op jit(solution)/shard_map/spread_xy/all_to_all | solution.py:37

commit v5 on v4

--- a/solution.py
+++ b/solution.py
@@ -2,6 +2,7 @@
 
 import jax
 import jax.numpy as jnp
+import numpy as np
 from jax import lax
 from jax.experimental import pallas as pl
 from jax.experimental.pallas import tpu as pltpu
@@ -129,25 +130,72 @@
     )(*pieces, whole)
 
 
+def adam_kernel(parts_ref, first_hbm, second_hbm, new_first_ref, new_second_ref, normalized_ref,
+                first_ref, second_ref, step_ref, semaphores):
+    fetches = [
+        pltpu.make_async_copy(first_hbm, first_ref, semaphores.at[0]),
+        pltpu.make_async_copy(second_hbm, second_ref, semaphores.at[1]),
+    ]
+    for fetch in fetches:
+        fetch.start()
+    shares = jnp.sum(parts_ref[...], axis=0) * (1.0 / math.sqrt(TOKENS))
+    for fetch in fetches:
+        fetch.wait()
+    corr_first = 1.0 - beta_first**STEP
+    corr_second = 1.0 - beta_second**STEP
+    for n in range(8):
+        columns = slice(n * 128, n * 128 + 128)
+        share = shares[n : n + 1]
+        new_first = beta_first * first_ref[:, columns] + (1.0 - beta_first) * share
+        new_second = beta_second * second_ref[:, columns] + (1.0 - beta_second) * share * share
+        new_first_ref[:, columns] = new_first
+        new_second_ref[:, columns] = new_second
+        step_ref[n : n + 1] = (
+            new_first / corr_first / (jnp.sqrt(new_second / corr_second) + adam_epsilon)
+        )
+    normalized_ref[...] = step_ref[...].astype(jnp.bfloat16)
+
+
+def adam(parts, first, second):
+    vmem, anywhere = pl.BlockSpec(memory_space=pltpu.VMEM), pl.BlockSpec(memory_space=pl.ANY)
+    row = jax.ShapeDtypeStruct((1, KVW), jnp.float32)
+    return pl.pallas_call(
+        adam_kernel,
+        in_specs=[vmem, anywhere, anywhere],
+        out_specs=[vmem] * 3,
+        out_shape=[row, row, jax.ShapeDtypeStruct((8, 128), jnp.bfloat16)],
+        scratch_shapes=[
+            pltpu.VMEM((1, KVW), jnp.float32),
+            pltpu.VMEM((1, KVW), jnp.float32),
+            pltpu.VMEM((8, 128), jnp.float32),
+            pltpu.SemaphoreType.DMA((2,)),
+        ],
+        compiler_params=pltpu.CompilerParams(vmem_limit_bytes=48 * 2**20),
+        cost_estimate=pl.CostEstimate(flops=2**14, bytes_accessed=2**16, transcendentals=2**10),
+        name="adam",
+    )(parts, first, second)
+
+
 def local(normed_input, value_cotangent, basis, first_moment, second_moment):
     x_at, z_lo_at, core_at = (lax.axis_index(a) for a in ("x", "z_lo", "core"))
     swap = [(0, 1), (1, 0)]
-    place = jnp.arange(RANK)
+    place = np.arange(RANK, dtype=np.int32)
     with jax.named_scope("order"):
         ranked = reorder(basis, owner_row(place >> 8, place >> 4 & 15, place & 15))
         decoder = reorder(basis, owner_row(place >> 4 & 1, place >> 5, place & 15))
-    with jax.named_scope("gather_core"):
-        rows = lax.dynamic_slice_in_dim(ranked, (x_at >> 1) * 128 + z_lo_at * 32, 32, 0)
-        low, high = rows[:, :256], rows[:, 256:]
-        theirs = lax.ppermute(jnp.where(core_at == 0, high, low), "core", swap)
-        chunk = jnp.where(core_at == (x_at & 1), jnp.where(core_at == 0, low, high), theirs)
     with jax.named_scope("tokens_x"):
         packed = pack(x_at, normed_input, value_cotangent)
         pieces = [packed[0]] + [
             lax.ppermute(packed[k], "x", [(i, (i + k) % 4) for i in range(4)]) for k in (1, 3, 2)
         ]
+    with jax.named_scope("gather_core"):
+        rows = lax.dynamic_slice_in_dim(ranked, (x_at >> 1) * 128 + z_lo_at * 32, 32, 0)
+        rows = join([rows], packed[1])
+        low, high = rows[:, :256], rows[:, 256:]
+        theirs = lax.ppermute(jnp.where(core_at == 0, high, low), "core", swap)
+        chunk = jnp.where(core_at == (x_at & 1), jnp.where(core_at == 0, low, high), theirs)
     with jax.named_scope("gather_z"):
-        line = spread(join([chunk], packed[1]), Z, 16).reshape(512, 256)
+        line = spread(chunk, Z, 16).reshape(512, 256)
     with jax.named_scope("gather_y"):
         whole = spread(line, "y", 4).reshape(QUARTER, 256)
     with jax.named_scope("tokens_core"):
@@ -158,24 +206,16 @@
     with jax.named_scope("reduce_xy"):
         summed = jnp.sum(exchange(partial.reshape(16, 16, KVW), ("x", "y")), axis=0)
     with jax.named_scope("reduce_z"):
-        share = jnp.sum(exchange(summed.reshape(16, 8, 128), Z), axis=0)
-        share = share * (1.0 / math.sqrt(TOKENS))
+        parts = exchange(summed.reshape(16, 8, 128), Z)
     with jax.named_scope("adam"):
-        first, second = first_moment.reshape(8, 128), second_moment.reshape(8, 128)
-        new_first = beta_first * first + (1.0 - beta_first) * share
-        new_second = beta_second * second + (1.0 - beta_second) * share * share
-        corr_first = 1.0 - beta_first**STEP
-        corr_second = 1.0 - beta_second**STEP
-        normalized = (
-            new_first / corr_first / (jnp.sqrt(new_second / corr_second) + adam_epsilon)
-        ).astype(jnp.bfloat16)
+        new_first, new_second, normalized = adam(parts, first_moment, second_moment)
     with jax.named_scope("spread_z"):
         column = spread(normalized, Z, 16).reshape(16, KVW)
     with jax.named_scope("spread_xy"):
         step = spread(column, ("x", "y", "core"), 32).reshape(RANK, KVW)
     with jax.named_scope("decode"):
         update = jnp.dot(decoder, step, preferred_element_type=jnp.float32).astype(jnp.bfloat16)
-    return new_first.reshape(1, KVW), new_second.reshape(1, KVW), update
+    return new_first, new_second, update
 
 
 def solution(mesh):

time: 169 us -> 169 us (level)
  blocking collectives: 37.4 us -> 85.3 us
  waiting for transfers between devices: 58.2 us -> 30.6 us
  starting transfers between devices: 55.4 us -> 36.1 us
    all_to_all x2 -> x4, blocking collectives: 37.4 us -> 85.3 us  [exchange(): return lax.all_to_all(blocks, axes, 0, 0, tiled=True)]
    all_to_all x4 -> x2, waiting for transfers between devices: 32.5 us -> 4.08 us  [exchange(): return lax.all_to_all(blocks, axes, 0, 0, tiled=True)]
    all_to_all x4 -> x2, starting transfers between devices: 33.4 us -> 13.7 us  [exchange(): return lax.all_to_all(blocks, axes, 0, 0, tiled=True)]
    unnamed x12 -> x14, local copies, waits for them, and re-layouts: 4.12 us -> 3.51 us
  transfers between devices with their start and end apart: 9 -> 7, of which waited for: 7 -> 5; matrix products, arithmetic and copies ran while one was open for 1% -> 1% of each run, Pallas kernels for 1% -> 0%
where the time goes in v5:
time: 169 us; the launch traced here: 168 us
  blocking collectives  85.3 us (50%)
  starting transfers between devices  36.1 us (21%)
  waiting for transfers between devices  30.6 us (18%)
  Pallas kernels  6.79 us (4%)
  local copies, waits for them, and re-layouts  5.43 us (3%)
  matrix products  2.88 us (2%)
    all_to_all x4, blocking collectives, exchange(): return lax.all_to_all(blocks, axes, 0, 0, tiled=True)  85.3 us
    ppermute x3, waiting for transfers between devices, local(): lax.ppermute(packed[k], 'x', [(i, (i + k) % 4) for i in range(4)])  20.5 us
    all_to_all x2, starting transfers between devices, exchange(): return lax.all_to_all(blocks, axes, 0, 0, tiled=True)  13.7 us
    ppermute x3, starting transfers between devices, local(): lax.ppermute(packed[k], 'x', [(i, (i + k) % 4) for i in range(4)])  9.93 us
    ppermute x1, starting transfers between devices, local(): theirs = lax.ppermute(jnp.where(core_at == 0, high, low), 'core', swap)  8.79 us
    ppermute x1, waiting for transfers between devices, local(): held = [held, lax.ppermute(held, 'core', swap)]  5.26 us
    all_to_all x2, waiting for transfers between devices, exchange(): return lax.all_to_all(blocks, axes, 0, 0, tiled=True)  4.08 us
    ppermute x1, starting transfers between devices, local(): held = [held, lax.ppermute(held, 'core', swap)]  3.63 us
  transfers between devices with their start and end apart: 7, of which 5 were waited for; matrix products, arithmetic and copies ran while one was open for 1% of the time, Pallas kernels for 0%

profile of v5, /device:TPU:1, one launch (start us, length us, event | category | flops | bytes accessed | tf_op | source)
XLA Modules:
  0.0 168.0 jit_solution(4628047454119233616)
XLA Ops:
  0.7 0.9 copy-done
  1.6 1.0 fusion
  2.7 1.6 copy-done.1
  4.3 0.9 copy-done.2
  5.2 2.1 %pack.1 = (bf16[128,3072]{1,0:T(8,128)(2,1)S(1)}, bf16[128,3072]{1,0:T(8,128)(2,1)}, bf16[128,3072]{1,0:T(8,128)(2,1)}, bf16[128,3072]{1,0:T(8,128)(2,1)}) custom-call(s32[1]{0:T(128)} %bitcast.x_ref, bf16[128,8192]{1,0:T(8,128)(2,1)S(1)} %copy-done.1, bf16[128,1024]{1,0:T(8,128)(2,1)S(1)} %copy-done.2), custom_call_target="tpu_custom_call" | custom-call | bytes 6291456 | tf_op jit(solution)/shard_map/tokens_x/pack/pallas_call | solution.py:58
  7.3 8.8 %collective-permute-start.3 = (bf16[32,256]{1,0:T(8,128)(2,1)S(1)}, bf16[32,256]{1,0:T(8,128)(2,1)S(1)}, u32[]{:S(2)}, u32[]{:S(2)}) collective-permute-start(bf16[32,256]{1,0:T(8,128)(2,1)S(1)} %broadcast_select_fusion), channel_id=1, source_target_pairs={{0,1},{1,0},{2,3},{3,2},{4,5},{5,4},{6,7},{7,6},{8,9},{9,8},{10,11... | collective-permute-start | bytes 49160 | tf_op jit(solution)/shard_map/gather_core/ppermute | solution.py:195
  17.7 9.5 %all-to-all-start = ((bf16[16,32,256]{2,1,0:T(8,128)(2,1)}), bf16[16,32,256]{2,1,0:T(8,128)(2,1)S(1)}, u32[]{:S(2)}, u32[]{:S(2)}) async-start(bf16[16,32,256]{2,1,0:T(8,128)(2,1)} %broadcast_in_dim.30), calls=%async_computation | async-start | bytes 524288 | tf_op jit(solution)/shard_map/gather_z/all_to_all | solution.py:38
  27.2 3.1 %collective-permute-start = (bf16[128,3072]{1,0:T(8,128)(2,1)}, bf16[128,3072]{1,0:T(8,128)(2,1)S(1)}, u32[]{:S(2)}, u32[]{:S(2)}) collective-permute-start(bf16[128,3072]{1,0:T(8,128)(2,1)} %get-tuple-element.11.refs_1_), channel_id=1, source_target_pairs={{0,32},{32,64},{64,96},{96,0},{1,33},{33,65},{65,97},{97,1},{2,34}... | collective-permute-start | bytes 2359304 | tf_op jit(solution)/shard_map/tokens_x/ppermute | solution.py:189
  30.4 3.4 %collective-permute-start.1 = (bf16[128,3072]{1,0:T(8,128)(2,1)}, bf16[128,3072]{1,0:T(8,128)(2,1)}, u32[]{:S(2)}, u32[]{:S(2)}) collective-permute-start(bf16[128,3072]{1,0:T(8,128)(2,1)} %get-tuple-element.12), channel_id=1, source_target_pairs={{0,96},{32,0},{64,32},{96,64},{1,97},{33,1},{65,33},{97,65},{2,98}... | collective-permute-start | bytes 2359304 | tf_op jit(solution)/shard_map/tokens_x/ppermute | solution.py:189
  33.7 3.4 %collective-permute-start.2 = (bf16[128,3072]{1,0:T(8,128)(2,1)}, bf16[128,3072]{1,0:T(8,128)(2,1)}, u32[]{:S(2)}, u32[]{:S(2)}) collective-permute-start(bf16[128,3072]{1,0:T(8,128)(2,1)} %get-tuple-element.13), channel_id=1, source_target_pairs={{0,64},{32,96},{64,0},{96,32},{1,65},{33,97},{65,1},{97,33},{2,66}... | collective-permute-start | bytes 2359304 | tf_op jit(solution)/shard_map/tokens_x/ppermute | solution.py:189
  37.2 4.1 %all-to-all-done = bf16[16,32,256]{2,1,0:T(8,128)(2,1)S(1)} async-done(((bf16[16,32,256]{2,1,0:T(8,128)(2,1)}), bf16[16,32,256]{2,1,0:T(8,128)(2,1)S(1)}, u32[]{:S(2)}, u32[]{:S(2)}) %all-to-all-start) | async-done | bytes 262176 | tf_op jit(solution)/shard_map/gather_z/all_to_all | solution.py:38
  41.3 1.1 broadcast_in_dim.32
  42.3 4.2 %all-to-all-start.1 = ((bf16[4,512,256]{2,1,0:T(8,128)(2,1)}), bf16[4,512,256]{2,1,0:T(8,128)(2,1)S(1)}, u32[]{:S(2)}, u32[]{:S(2)}) async-start(bf16[4,512,256]{2,1,0:T(8,128)(2,1)} %broadcast_in_dim.32), calls=%async_computation.1 | async-start | bytes 2097152 | tf_op jit(solution)/shard_map/gather_y/all_to_all | solution.py:38
  46.5 4.2 %collective-permute-done.1.refs_2_ = bf16[128,3072]{1,0:T(8,128)(2,1)} collective-permute-done((bf16[128,3072]{1,0:T(8,128)(2,1)}, bf16[128,3072]{1,0:T(8,128)(2,1)}, u32[]{:S(2)}, u32[]{:S(2)}) %collective-permute-start.1) | collective-permute-done | bytes 786464 | tf_op jit(solution)/shard_map/tokens_x/ppermute | solution.py:189
  50.7 16.2 %collective-permute-done.2.refs_3_ = bf16[128,3072]{1,0:T(8,128)(2,1)} collective-permute-done((bf16[128,3072]{1,0:T(8,128)(2,1)}, bf16[128,3072]{1,0:T(8,128)(2,1)}, u32[]{:S(2)}, u32[]{:S(2)}) %collective-permute-start.2) | collective-permute-done | bytes 786464 | tf_op jit(solution)/shard_map/tokens_x/ppermute | solution.py:189
  67.0 1.6 join.3.refs_0_
  68.5 3.6 %collective-permute-start.4 = (bf16[512,3072]{1,0:T(8,128)(2,1)S(1)}, bf16[512,3072]{1,0:T(8,128)(2,1)S(1)}, u32[]{:S(2)}, u32[]{:S(2)}) collective-permute-start(bf16[512,3072]{1,0:T(8,128)(2,1)S(1)} %join.3.refs_0_), channel_id=1, source_target_pairs={{0,1},{1,0},{2,3},{3,2},{4,5},{5,4},{6,7},{7,6},{8,9},{9,8},{10,11... | collective-permute-start | bytes 9437192 | tf_op jit(solution)/shard_map/tokens_core/ppermute | solution.py:203
  72.2 5.3 %collective-permute-done.4.refs_1_ = bf16[512,3072]{1,0:T(8,128)(2,1)S(1)} collective-permute-done((bf16[512,3072]{1,0:T(8,128)(2,1)S(1)}, bf16[512,3072]{1,0:T(8,128)(2,1)S(1)}, u32[]{:S(2)}, u32[]{:S(2)}) %collective-permute-start.4) | collective-permute-done | bytes 3145760 | tf_op jit(solution)/shard_map/tokens_core/ppermute | solution.py:203
  77.4 2.5 %project.1 = f32[256,1024]{1,0:T(8,128)S(1)} custom-call(bf16[512,3072]{1,0:T(8,128)(2,1)S(1)} %join.3.refs_0_, bf16[512,3072]{1,0:T(8,128)(2,1)S(1)} %collective-permute-done.4.refs_1_, bf16[2048,256]{1,0:T(8,128)(2,1)S(1)} %bitcast.17), custom_call_target="tpu_custom_call" | custom-call | flops 2147483648 | bytes 8388608 | tf_op jit(solution)/shard_map/project/project/pallas_call | solution.py:119
  79.9 23.3 %all_to_all.30 = f32[16,16,1024]{2,1,0:T(8,128)S(1)} all-to-all(f32[16,16,1024]{2,1,0:T(8,128)S(1)} %bitcast.18), channel_id=1, replica_groups=mesh['z_lo'=4,'x'=4,'y'=4,'z_hi'=4,'core'=2] {'x','y'}, dimensions={0} | all-to-all | bytes 2097152 | tf_op jit(solution)/shard_map/reduce_xy/all_to_all | solution.py:38
  103.3 22.9 %all_to_all.31.parts_ref = f32[16,8,128]{2,1,0:T(8,128)S(1)} all-to-all(f32[16,8,128]{2,1,0:T(8,128)S(1)} %bitcast.22), channel_id=1, replica_groups=mesh['z_lo'=4,'x'=4,'y'=4,'z_hi'=4,'core'=2] {'z_hi','z_lo'}, dimensions={0} | all-to-all | bytes 131072 | tf_op jit(solution)/shard_map/reduce_z/all_to_all | solution.py:38
  126.9 14.2 %all_to_all.32 = bf16[16,8,128]{2,1,0:T(8,128)(2,1)S(1)} all-to-all(bf16[16,8,128]{2,1,0:T(8,128)(2,1)S(1)} %broadcast_in_dim.33), channel_id=1, replica_groups=mesh['z_lo'=4,'x'=4,'y'=4,'z_hi'=4,'core'=2] {'z_hi','z_lo'}, dimensions={0} | all-to-all | bytes 65536 | tf_op jit(solution)/shard_map/spread_z/all_to_all | solution.py:38
  141.2 24.9 %all_to_all.33 = bf16[32,16,1024]{2,1,0:T(8,128)(2,1)S(1)} all-to-all(bf16[32,16,1024]{2,1,0:T(8,128)(2,1)S(1)} %broadcast_in_dim.35), channel_id=1, replica_groups=mesh['z_lo'=4,'x'=4,'y'=4,'z_hi'=4,'core'=2] {'x','y','core'}, dimensions={0} | all-to-all | bytes 2097152 | tf_op jit(solution)/shard_map/spread_xy/all_to_all | solution.py:38
  166.1 1.8 %convolution_convert_fusion = bf16[256,1024]{1,0:T(8,128)(2,1)} fusion(bf16[512,1024]{1,0:T(8,128)(2,1)S(1)} %bitcast.20, bf16[256,512]{1,0:T(8,128)(2,1)S(1)} %copy-done, s32[512]{0:T(512)S(1)} %copy-done.5), kind=kOutput, calls=%fused_computation | convolution fusion | flops 403570688 | bytes 1837056 | tf_op jit(solution)/shard_map/decode/dot_general | solution.py:217
  (23 shorter events, 2.5 us)
Async XLA Ops:
  0.6 1.0 copy-start
  2.7 1.6 copy-start.1
  4.3 0.9 copy-start.2
  7.3 9.6 %collective-permute-start.3 = (bf16[32,256]{1,0:T(8,128)(2,1)S(1)}, bf16[32,256]{1,0:T(8,128)(2,1)S(1)}, u32[]{:S(2)}, u32[]{:S(2)}) collective-permute-start(bf16[32,256]{1,0:T(8,128)(2,1)S(1)} %broadcast_select_fusion), channel_id=1, source_target_pairs={{0,1},{1,0},{2,3},{3,2},{4,5},{5,4},{6,7},{7,6},{8,9},{9,8},{10,11... | collective-permute-start | bytes 49160 | tf_op jit(solution)/shard_map/gather_core/ppermute | solution.py:195
  17.7 23.6 %all-to-all-start = ((bf16[16,32,256]{2,1,0:T(8,128)(2,1)}), bf16[16,32,256]{2,1,0:T(8,128)(2,1)S(1)}, u32[]{:S(2)}, u32[]{:S(2)}) async-start(bf16[16,32,256]{2,1,0:T(8,128)(2,1)} %broadcast_in_dim.30), calls=%async_computation | async-start | bytes 524288 | tf_op jit(solution)/shard_map/gather_z/all_to_all | solution.py:38
  27.2 39.7 %collective-permute-start = (bf16[128,3072]{1,0:T(8,128)(2,1)}, bf16[128,3072]{1,0:T(8,128)(2,1)S(1)}, u32[]{:S(2)}, u32[]{:S(2)}) collective-permute-start(bf16[128,3072]{1,0:T(8,128)(2,1)} %get-tuple-element.11.refs_1_), channel_id=1, source_target_pairs={{0,32},{32,64},{64,96},{96,0},{1,33},{33,65},{65,97},{97,1},{2,34}... | collective-permute-start | bytes 2359304 | tf_op jit(solution)/shard_map/tokens_x/ppermute | solution.py:189
  30.4 20.4 %collective-permute-start.1 = (bf16[128,3072]{1,0:T(8,128)(2,1)}, bf16[128,3072]{1,0:T(8,128)(2,1)}, u32[]{:S(2)}, u32[]{:S(2)}) collective-permute-start(bf16[128,3072]{1,0:T(8,128)(2,1)} %get-tuple-element.12), channel_id=1, source_target_pairs={{0,96},{32,0},{64,32},{96,64},{1,97},{33,1},{65,33},{97,65},{2,98}... | collective-permute-start | bytes 2359304 | tf_op jit(solution)/shard_map/tokens_x/ppermute | solution.py:189
  33.7 33.2 %collective-permute-start.2 = (bf16[128,3072]{1,0:T(8,128)(2,1)}, bf16[128,3072]{1,0:T(8,128)(2,1)}, u32[]{:S(2)}, u32[]{:S(2)}) collective-permute-start(bf16[128,3072]{1,0:T(8,128)(2,1)} %get-tuple-element.13), channel_id=1, source_target_pairs={{0,64},{32,96},{64,0},{96,32},{1,65},{33,97},{65,1},{97,33},{2,66}... | collective-permute-start | bytes 2359304 | tf_op jit(solution)/shard_map/tokens_x/ppermute | solution.py:189
  42.3 24.6 %all-to-all-start.1 = ((bf16[4,512,256]{2,1,0:T(8,128)(2,1)}), bf16[4,512,256]{2,1,0:T(8,128)(2,1)S(1)}, u32[]{:S(2)}, u32[]{:S(2)}) async-start(bf16[4,512,256]{2,1,0:T(8,128)(2,1)} %broadcast_in_dim.32), calls=%async_computation.1 | async-start | bytes 2097152 | tf_op jit(solution)/shard_map/gather_y/all_to_all | solution.py:38
  68.5 8.9 %collective-permute-start.4 = (bf16[512,3072]{1,0:T(8,128)(2,1)S(1)}, bf16[512,3072]{1,0:T(8,128)(2,1)S(1)}, u32[]{:S(2)}, u32[]{:S(2)}) collective-permute-start(bf16[512,3072]{1,0:T(8,128)(2,1)S(1)} %join.3.refs_0_), channel_id=1, source_target_pairs={{0,1},{1,0},{2,3},{3,2},{4,5},{5,4},{6,7},{7,6},{8,9},{9,8},{10,11... | collective-permute-start | bytes 9437192 | tf_op jit(solution)/shard_map/tokens_core/ppermute | solution.py:203
  79.9 46.3 %copy-start.3 = (f32[1,1024]{1,0:T(1,128)S(1)}, f32[1,1024]{1,0:T(1,128)}, u32[]{:S(2)}) copy-start(f32[1,1024]{1,0:T(1,128)} %first_hbm.1) | copy-start | bytes 12292
  79.9 46.3 %copy-start.4 = (f32[1,1024]{1,0:T(1,128)S(1)}, f32[1,1024]{1,0:T(1,128)}, u32[]{:S(2)}) copy-start(f32[1,1024]{1,0:T(1,128)} %second_hbm.1) | copy-start | bytes 12292
  79.9 86.2 %copy-start.5 = (s32[512]{0:T(512)S(1)}, s32[512]{0:T(512)}, u32[]{:S(2)}) copy-start(s32[512]{0:T(512)} %constant.37) | copy-start | bytes 6148

commit v6 on v5

--- a/solution.py
+++ b/solution.py
@@ -188,16 +188,22 @@
         pieces = [packed[0]] + [
             lax.ppermute(packed[k], "x", [(i, (i + k) % 4) for i in range(4)]) for k in (1, 3, 2)
         ]
-    with jax.named_scope("gather_core"):
+    def gather(rows):
+        with jax.named_scope("gather_core"):
+            low, high = rows[:, :256], rows[:, 256:]
+            theirs = lax.ppermute(jnp.where(core_at == 0, high, low), "core", swap)
+            chunk = jnp.where(core_at == (x_at & 1), jnp.where(core_at == 0, low, high), theirs)
+        with jax.named_scope("gather_z"):
+            line = spread(chunk, Z, 16).reshape(512, 256)
+        with jax.named_scope("gather_y"):
+            return spread(line, "y", 4).reshape(QUARTER, 256)
+
+    with jax.named_scope("gather"):
         rows = lax.dynamic_slice_in_dim(ranked, (x_at >> 1) * 128 + z_lo_at * 32, 32, 0)
-        rows = join([rows], packed[1])
-        low, high = rows[:, :256], rows[:, 256:]
-        theirs = lax.ppermute(jnp.where(core_at == 0, high, low), "core", swap)
-        chunk = jnp.where(core_at == (x_at & 1), jnp.where(core_at == 0, low, high), theirs)
-    with jax.named_scope("gather_z"):
-        line = spread(chunk, Z, 16).reshape(512, 256)
-    with jax.named_scope("gather_y"):
-        whole = spread(line, "y", 4).reshape(QUARTER, 256)
+        whole = lax.cond(
+            x_at < 4, gather, lambda rows: jnp.zeros((QUARTER, 256), jnp.bfloat16),
+            join([rows], packed[1]),
+        )
     with jax.named_scope("tokens_core"):
         held = join(pieces, whole)
         held = [held, lax.ppermute(held, "core", swap)]

time: 169 us -> 164 us (0.970)
  blocking collectives: 85.3 us -> 120 us
  waiting for transfers between devices: 30.6 us -> 6.08 us
  starting transfers between devices: 36.1 us -> 25.1 us
  local copies, waits for them, and re-layouts: 5.43 us -> 2.86 us
    all_to_all x4 -> x6, blocking collectives: 85.3 us -> 120 us  [exchange(): return lax.all_to_all(blocks, axes, 0, 0, tiled=True)]
    ppermute x3, waiting for transfers between devices: 20.5 us -> 0.01 us  [local(): lax.ppermute(packed[k], 'x', [(i, (i + k) % 4) for i in range(4)])]
    all_to_all x2 -> x0, starting transfers between devices: 13.7 us -> none  [exchange(): return lax.all_to_all(blocks, axes, 0, 0, tiled=True)]
    ppermute x1, starting transfers between devices: 3.63 us -> 8.6 us  [local(): held = [held, lax.ppermute(held, 'core', swap)]]
    all_to_all x2 -> x0, waiting for transfers between devices: 4.08 us -> none  [exchange(): return lax.all_to_all(blocks, axes, 0, 0, tiled=True)]
    ppermute x1, starting transfers between devices: 8.79 us -> 6.39 us  [gather(): theirs = lax.ppermute(jnp.where(core_at == 0, high, low), 'core', swap)]
    broadcast_in_dim x4, local copies, waits for them, and re-layouts: 1.91 us -> 0.21 us  [spread(): return exchange(jnp.broadcast_to(block[None], (count, *block.shape)), axes)]
    unnamed x14 -> x16, local copies, waits for them, and re-layouts: 3.51 us -> 2.63 us
  transfers between devices with their start and end apart: 7 -> 5, of which waited for: 5 -> 2; matrix products, arithmetic and copies ran while one was open for 1% -> 1% of each run, Pallas kernels for 0% -> 0%
where the time goes in v6:
time: 164 us; the launch traced here: 163 us
  blocking collectives  120 us (73%)
  starting transfers between devices  25.1 us (15%)
  waiting for transfers between devices  6.08 us (4%)
  Pallas kernels  5.38 us (3%)
  matrix products  2.88 us (2%)
  local copies, waits for them, and re-layouts  2.86 us (2%)
    all_to_all x6, blocking collectives, exchange(): return lax.all_to_all(blocks, axes, 0, 0, tiled=True)  120 us
    ppermute x3, starting transfers between devices, local(): lax.ppermute(packed[k], 'x', [(i, (i + k) % 4) for i in range(4)])  10.1 us
    ppermute x1, starting transfers between devices, local(): held = [held, lax.ppermute(held, 'core', swap)]  8.6 us
    ppermute x1, starting transfers between devices, gather(): theirs = lax.ppermute(jnp.where(core_at == 0, high, low), 'core', swap)  6.39 us
    ppermute x1, waiting for transfers between devices, local(): held = [held, lax.ppermute(held, 'core', swap)]  5.26 us
  transfers between devices with their start and end apart: 5, of which 2 were waited for; matrix products, arithmetic and copies ran while one was open for 1% of the time, Pallas kernels for 0%

profile of v6, /device:TPU:1, one launch (start us, length us, event | category | flops | bytes accessed | tf_op | source)
XLA Modules:
  0.0 163.3 jit_solution(10742395315029691695)
XLA Ops:
  0.7 1.6 copy-done.1
  2.3 0.9 copy-done.2
  3.2 2.1 %pack.1 = (bf16[128,3072]{1,0:T(8,128)(2,1)S(1)}, bf16[128,3072]{1,0:T(8,128)(2,1)}, bf16[128,3072]{1,0:T(8,128)(2,1)}, bf16[128,3072]{1,0:T(8,128)(2,1)}) custom-call(s32[1]{0:T(128)} %bitcast.2.x_ref, bf16[128,8192]{1,0:T(8,128)(2,1)S(1)} %copy-done.1, bf16[128,1024]{1,0:T(8,128)(2,1)S(1)} %copy-done.2), custom_call_target="tpu_custom_call" | custom-call | bytes 6291456 | tf_op jit(solution)/shard_map/tokens_x/pack/pallas_call | solution.py:58
  5.3 5.2 %collective-permute-start.2 = (bf16[128,3072]{1,0:T(8,128)(2,1)}, bf16[128,3072]{1,0:T(8,128)(2,1)S(1)}, u32[]{:S(2)}, u32[]{:S(2)}) collective-permute-start(bf16[128,3072]{1,0:T(8,128)(2,1)} %get-tuple-element.24), channel_id=1, source_target_pairs={{0,96},{32,0},{64,32},{96,64},{1,97},{33,1},{65,33},{97,65},{2,98}... | collective-permute-start | bytes 2359304 | tf_op jit(solution)/shard_map/tokens_x/ppermute | solution.py:189
  10.5 2.4 %collective-permute-start.3 = (bf16[128,3072]{1,0:T(8,128)(2,1)}, bf16[128,3072]{1,0:T(8,128)(2,1)S(1)}, u32[]{:S(2)}, u32[]{:S(2)}) collective-permute-start(bf16[128,3072]{1,0:T(8,128)(2,1)} %get-tuple-element.25), channel_id=1, source_target_pairs={{0,64},{32,96},{64,0},{96,32},{1,65},{33,97},{65,1},{97,33},{2,66}... | collective-permute-start | bytes 2359304 | tf_op jit(solution)/shard_map/tokens_x/ppermute | solution.py:189
  12.9 2.5 %collective-permute-start.1 = (bf16[128,3072]{1,0:T(8,128)(2,1)}, bf16[128,3072]{1,0:T(8,128)(2,1)S(1)}, u32[]{:S(2)}, u32[]{:S(2)}) collective-permute-start(bf16[128,3072]{1,0:T(8,128)(2,1)} %get-tuple-element.23.refs_1_), channel_id=1, source_target_pairs={{0,32},{32,64},{64,96},{96,0},{1,33},{33,65},{65,97},{97,1},{2,34}... | collective-permute-start | bytes 2359304 | tf_op jit(solution)/shard_map/tokens_x/ppermute | solution.py:189
  15.5 1.1 fusion
  16.6 47.0 %conditional.1 = (bf16[2048,256]{1,0:T(8,128)(2,1)}) conditional(s32[]{:T(128)} %convert_element_type.16, () %tuple.14, (s32[]{:T(128)}, s32[]{:T(128)}, bf16[32,512]{1,0:T(8,128)(2,1)S(1)}) %tuple.15), branch_computations={%region_0.0_spmd, %region_1.2_spmd} | conditional | flops 24579 | bytes 4390993 | solution.py:203
  16.6 6.4 %collective-permute-start = (bf16[32,256]{1,0:T(8,128)(2,1)S(1)}, bf16[32,256]{1,0:T(8,128)(2,1)S(1)}, u32[]{:S(2)}, u32[]{:S(2)}) collective-permute-start(bf16[32,256]{1,0:T(8,128)(2,1)S(1)} %broadcast_select_fusion), channel_id=1, source_target_pairs={{0,1},{1,0},{2,3},{3,2},{4,5},{5,4},{6,7},{7,6},{8,9},{9,8},{10,11... | collective-permute-start | bytes 49160 | tf_op jit(solution)/shard_map/gather/cond/branch_1_fun/gather_core/ppermute | solution.py:194
  23.0 0.8 collective-permute-done
  23.9 25.8 %all_to_all.28 = bf16[16,32,256]{2,1,0:T(8,128)(2,1)S(1)} all-to-all(bf16[16,32,256]{2,1,0:T(8,128)(2,1)S(1)} %broadcast_in_dim.7), channel_id=1, replica_groups=mesh['z_lo'=4,'x'=4,'y'=4,'z_hi'=4,'core'=2] {'z_hi','z_lo'}, dimensions={0} | all-to-all | bytes 524288 | tf_op jit(solution)/shard_map/gather/cond/branch_1_fun/gather_z/all_to_all | solution.py:38
  49.6 0.1 broadcast_in_dim.16
  49.7 13.8 %all_to_all.29 = bf16[4,512,256]{2,1,0:T(8,128)(2,1)} all-to-all(bf16[4,512,256]{2,1,0:T(8,128)(2,1)S(1)} %broadcast_in_dim.16), channel_id=1, replica_groups=mesh['z_lo'=4,'x'=4,'y'=4,'z_hi'=4,'core'=2] {'y'}, dimensions={0} | all-to-all | bytes 2097152 | tf_op jit(solution)/shard_map/gather/cond/branch_1_fun/gather_y/all_to_all | solution.py:38
  63.6 0.2 join.3.refs_0_
  63.8 8.6 %collective-permute-start.4 = (bf16[512,3072]{1,0:T(8,128)(2,1)S(1)}, bf16[512,3072]{1,0:T(8,128)(2,1)S(1)}, u32[]{:S(2)}, u32[]{:S(2)}) collective-permute-start(bf16[512,3072]{1,0:T(8,128)(2,1)S(1)} %join.3.refs_0_), channel_id=1, source_target_pairs={{0,1},{1,0},{2,3},{3,2},{4,5},{5,4},{6,7},{7,6},{8,9},{9,8},{10,11... | collective-permute-start | bytes 9437192 | tf_op jit(solution)/shard_map/tokens_core/ppermute | solution.py:209
  72.4 5.3 %collective-permute-done.4.refs_1_ = bf16[512,3072]{1,0:T(8,128)(2,1)S(1)} collective-permute-done((bf16[512,3072]{1,0:T(8,128)(2,1)S(1)}, bf16[512,3072]{1,0:T(8,128)(2,1)S(1)}, u32[]{:S(2)}, u32[]{:S(2)}) %collective-permute-start.4) | collective-permute-done | bytes 3145760 | tf_op jit(solution)/shard_map/tokens_core/ppermute | solution.py:209
  77.7 2.5 %project.1 = f32[256,1024]{1,0:T(8,128)S(1)} custom-call(bf16[512,3072]{1,0:T(8,128)(2,1)S(1)} %join.3.refs_0_, bf16[512,3072]{1,0:T(8,128)(2,1)S(1)} %collective-permute-done.4.refs_1_, bf16[2048,256]{1,0:T(8,128)(2,1)S(1)} %copy-done.5), custom_call_target="tpu_custom_call" | custom-call | flops 2147483648 | bytes 8388608 | tf_op jit(solution)/shard_map/project/project/pallas_call | solution.py:119
  80.2 19.9 %all_to_all.30 = f32[16,16,1024]{2,1,0:T(8,128)S(1)} all-to-all(f32[16,16,1024]{2,1,0:T(8,128)S(1)} %bitcast.16), channel_id=1, replica_groups=mesh['z_lo'=4,'x'=4,'y'=4,'z_hi'=4,'core'=2] {'x','y'}, dimensions={0} | all-to-all | bytes 2097152 | tf_op jit(solution)/shard_map/reduce_xy/all_to_all | solution.py:38
  100.2 21.3 %all_to_all.31.parts_ref = f32[16,8,128]{2,1,0:T(8,128)S(1)} all-to-all(f32[16,8,128]{2,1,0:T(8,128)S(1)} %bitcast.21), channel_id=1, replica_groups=mesh['z_lo'=4,'x'=4,'y'=4,'z_hi'=4,'core'=2] {'z_hi','z_lo'}, dimensions={0} | all-to-all | bytes 131072 | tf_op jit(solution)/shard_map/reduce_z/all_to_all | solution.py:38
  121.5 0.7 adam.1
  122.2 14.3 %all_to_all.32 = bf16[16,8,128]{2,1,0:T(8,128)(2,1)S(1)} all-to-all(bf16[16,8,128]{2,1,0:T(8,128)(2,1)S(1)} %broadcast_in_dim.30), channel_id=1, replica_groups=mesh['z_lo'=4,'x'=4,'y'=4,'z_hi'=4,'core'=2] {'z_hi','z_lo'}, dimensions={0} | all-to-all | bytes 65536 | tf_op jit(solution)/shard_map/spread_z/all_to_all | solution.py:38
  136.5 0.1 broadcast_in_dim.32
  136.6 24.9 %all_to_all.33 = bf16[32,16,1024]{2,1,0:T(8,128)(2,1)S(1)} all-to-all(bf16[32,16,1024]{2,1,0:T(8,128)(2,1)S(1)} %broadcast_in_dim.32), channel_id=1, replica_groups=mesh['z_lo'=4,'x'=4,'y'=4,'z_hi'=4,'core'=2] {'x','y','core'}, dimensions={0} | all-to-all | bytes 2097152 | tf_op jit(solution)/shard_map/spread_xy/all_to_all | solution.py:38
  161.5 1.8 %convolution_convert_fusion = bf16[256,1024]{1,0:T(8,128)(2,1)} fusion(bf16[512,1024]{1,0:T(8,128)(2,1)S(1)} %bitcast.19, bf16[256,512]{1,0:T(8,128)(2,1)S(1)} %copy-done, s32[512]{0:T(512)S(1)} %copy-done.6), kind=kOutput, calls=%fused_computation.2 | convolution fusion | flops 403570688 | bytes 1837056 | tf_op jit(solution)/shard_map/decode/dot_general | solution.py:223
  (24 shorter events, 0.2 us)
Async XLA Ops:
  0.6 14.8 %copy-start = (bf16[256,512]{1,0:T(8,128)(2,1)S(1)}, bf16[256,512]{1,0:T(8,128)(2,1)}, u32[]{:S(2)}) copy-start(bf16[256,512]{1,0:T(8,128)(2,1)} %param.11) | copy-start | bytes 786436
  0.7 1.6 copy-start.1
  2.3 0.9 copy-start.2
  5.3 58.3 %collective-permute-start.2 = (bf16[128,3072]{1,0:T(8,128)(2,1)}, bf16[128,3072]{1,0:T(8,128)(2,1)S(1)}, u32[]{:S(2)}, u32[]{:S(2)}) collective-permute-start(bf16[128,3072]{1,0:T(8,128)(2,1)} %get-tuple-element.24), channel_id=1, source_target_pairs={{0,96},{32,0},{64,32},{96,64},{1,97},{33,1},{65,33},{97,65},{2,98}... | collective-permute-start | bytes 2359304 | tf_op jit(solution)/shard_map/tokens_x/ppermute | solution.py:189
  10.5 53.0 %collective-permute-start.3 = (bf16[128,3072]{1,0:T(8,128)(2,1)}, bf16[128,3072]{1,0:T(8,128)(2,1)S(1)}, u32[]{:S(2)}, u32[]{:S(2)}) collective-permute-start(bf16[128,3072]{1,0:T(8,128)(2,1)} %get-tuple-element.25), channel_id=1, source_target_pairs={{0,64},{32,96},{64,0},{96,32},{1,65},{33,97},{65,1},{97,33},{2,66}... | collective-permute-start | bytes 2359304 | tf_op jit(solution)/shard_map/tokens_x/ppermute | solution.py:189
  12.9 50.6 %collective-permute-start.1 = (bf16[128,3072]{1,0:T(8,128)(2,1)}, bf16[128,3072]{1,0:T(8,128)(2,1)S(1)}, u32[]{:S(2)}, u32[]{:S(2)}) collective-permute-start(bf16[128,3072]{1,0:T(8,128)(2,1)} %get-tuple-element.23.refs_1_), channel_id=1, source_target_pairs={{0,32},{32,64},{64,96},{96,0},{1,33},{33,65},{65,97},{97,1},{2,34}... | collective-permute-start | bytes 2359304 | tf_op jit(solution)/shard_map/tokens_x/ppermute | solution.py:189
  16.6 7.2 %collective-permute-start = (bf16[32,256]{1,0:T(8,128)(2,1)S(1)}, bf16[32,256]{1,0:T(8,128)(2,1)S(1)}, u32[]{:S(2)}, u32[]{:S(2)}) collective-permute-start(bf16[32,256]{1,0:T(8,128)(2,1)S(1)} %broadcast_select_fusion), channel_id=1, source_target_pairs={{0,1},{1,0},{2,3},{3,2},{4,5},{5,4},{6,7},{7,6},{8,9},{9,8},{10,11... | collective-permute-start | bytes 49160 | tf_op jit(solution)/shard_map/gather/cond/branch_1_fun/gather_core/ppermute | solution.py:194
  63.6 14.1 %copy-start.5 = (bf16[2048,256]{1,0:T(8,128)(2,1)S(1)}, bf16[2048,256]{1,0:T(8,128)(2,1)}, u32[]{:S(2)}) copy-start(bf16[2048,256]{1,0:T(8,128)(2,1)} %get-tuple-element.29.refs_4_.refs_2_) | copy-start | bytes 3145732
  63.8 13.9 %collective-permute-start.4 = (bf16[512,3072]{1,0:T(8,128)(2,1)S(1)}, bf16[512,3072]{1,0:T(8,128)(2,1)S(1)}, u32[]{:S(2)}, u32[]{:S(2)}) collective-permute-start(bf16[512,3072]{1,0:T(8,128)(2,1)S(1)} %join.3.refs_0_), channel_id=1, source_target_pairs={{0,1},{1,0},{2,3},{3,2},{4,5},{5,4},{6,7},{7,6},{8,9},{9,8},{10,11... | collective-permute-start | bytes 9437192 | tf_op jit(solution)/shard_map/tokens_core/ppermute | solution.py:209
  80.1 41.4 %copy-start.3 = (f32[1,1024]{1,0:T(1,128)S(1)}, f32[1,1024]{1,0:T(1,128)}, u32[]{:S(2)}) copy-start(f32[1,1024]{1,0:T(1,128)} %first_hbm.1) | copy-start | bytes 12292
  80.1 41.4 %copy-start.4 = (f32[1,1024]{1,0:T(1,128)S(1)}, f32[1,1024]{1,0:T(1,128)}, u32[]{:S(2)}) copy-start(f32[1,1024]{1,0:T(1,128)} %second_hbm.1) | copy-start | bytes 12292
  80.1 81.3 %copy-start.6 = (s32[512]{0:T(512)S(1)}, s32[512]{0:T(512)}, u32[]{:S(2)}) copy-start(s32[512]{0:T(512)} %constant.45) | copy-start | bytes 6148

commit v7 on v6

--- a/solution.py
+++ b/solution.py
@@ -42,7 +42,7 @@
     return exchange(jnp.broadcast_to(block[None], (count, *block.shape)), axes)
 
 
-def pack_kernel(x_ref, tokens_ref, cotangent_ref, *out_refs):
+def pack_kernel(x_ref, tokens_ref, cotangent_ref, _, *out_refs):
     for k, out_ref in enumerate(out_refs):
         at = (x_ref[0] + k) & 3
         offset = pl.multiple_of((at & 1) * 256 + (at >> 1) * 128, 128)
@@ -53,7 +53,7 @@
         out_ref[:, QUARTER:] = cotangent_ref[...]
 
 
-def pack(x_at, tokens, cotangent):
+def pack(x_at, tokens, cotangent, other):
     rows = 32
     return pl.pallas_call(
         pack_kernel,
@@ -62,13 +62,14 @@
             pl.BlockSpec(memory_space=pltpu.SMEM),
             pl.BlockSpec((rows, 8192), lambda i: (i, 0)),
             pl.BlockSpec((rows, KVW), lambda i: (i, 0)),
+            pl.BlockSpec(memory_space=pl.ANY),
         ],
         out_specs=[pl.BlockSpec((rows, QUARTER + KVW), lambda i: (i, 0))] * 4,
         out_shape=[jax.ShapeDtypeStruct((128, QUARTER + KVW), jnp.bfloat16)] * 4,
-        compiler_params=pltpu.CompilerParams(vmem_limit_bytes=32 * 2**20),
+        compiler_params=pltpu.CompilerParams(vmem_limit_bytes=60 * 2**20),
         cost_estimate=pl.CostEstimate(flops=0, bytes_accessed=6 * 2**20, transcendentals=0),
         name="pack",
-    )(x_at[None], tokens, cotangent)
+    )(x_at[None], tokens, cotangent, other)
 
 
 def join_kernel(*refs):
@@ -92,42 +93,62 @@
     )(*pieces, other)
 
 
-def project_kernel(*refs):
-    *pieces, whole_ref, out_ref, split_ref = refs
-    whole = whole_ref[...]
-    at, tokens = 0, split_ref.shape[0] // 2
-    for piece in pieces:
-        rows = piece.shape[0]
-        reduced = jnp.dot(piece[:, :QUARTER], whole, preferred_element_type=jnp.float32)
-        high = reduced.astype(jnp.bfloat16)
-        low = (reduced - high.astype(jnp.float32)).astype(jnp.bfloat16)
-        split_ref[at : at + rows] = high
-        split_ref[tokens + at : tokens + at + rows] = low
-        at += rows
+def project_kernel(tokens_ref, whole_ref, *refs):
+    *before, out_ref, split_ref = refs
+    rows = tokens_ref.shape[0]
+    reduced = jnp.dot(
+        tokens_ref[:, :QUARTER], whole_ref[...], preferred_element_type=jnp.float32
+    )
+    high = reduced.astype(jnp.bfloat16)
+    split_ref[:rows] = high
+    split_ref[rows:] = (reduced - high.astype(jnp.float32)).astype(jnp.bfloat16)
     for n in range(0, KVW, 256):
-        columns = [piece[:, QUARTER + n : QUARTER + n + 256] for piece in pieces]
-        out_ref[:, n : n + 256] = lax.dot_general(
+        cotangent = tokens_ref[:, QUARTER + n : QUARTER + n + 256]
+        total = lax.dot_general(
             split_ref[...],
-            jnp.concatenate(columns + columns, axis=0),
+            jnp.concatenate([cotangent, cotangent], axis=0),
             (((0,), (0,)), ((), ())),
             preferred_element_type=jnp.float32,
         )
-
-
-def project(pieces, whole):
+        for part in before:
+            total += part[:, n : n + 256]
+        out_ref[:, n : n + 256] = total
+
+
+def project(tokens, whole, *before):
     vmem = pl.BlockSpec(memory_space=pltpu.VMEM)
     return pl.pallas_call(
         project_kernel,
-        in_specs=[vmem] * (len(pieces) + 1),
+        in_specs=[vmem] * (2 + len(before)),
         out_specs=vmem,
         out_shape=jax.ShapeDtypeStruct((256, KVW), jnp.float32),
-        scratch_shapes=[pltpu.VMEM((2048, 256), jnp.bfloat16)],
-        compiler_params=pltpu.CompilerParams(vmem_limit_bytes=40 * 2**20),
-        cost_estimate=pl.CostEstimate(
-            flops=2 * 2**30, bytes_accessed=8 * 2**20, transcendentals=0
-        ),
+        scratch_shapes=[pltpu.VMEM((1024, 256), jnp.bfloat16)],
+        compiler_params=pltpu.CompilerParams(vmem_limit_bytes=24 * 2**20),
+        cost_estimate=pl.CostEstimate(flops=2**30, bytes_accessed=6 * 2**20, transcendentals=0),
         name="project",
-    )(*pieces, whole)
+    )(tokens, whole, *before)
+
+
+def decode_kernel(core_ref, basis_ref, own_ref, other_ref, out_ref):
+    total = None
+    for at, rows_ref in ((core_ref[0], own_ref), (1 - core_ref[0], other_ref)):
+        half = basis_ref[:, pl.ds(pl.multiple_of(at * 256, 256), 256)]
+        term = jnp.dot(half, rows_ref[...], preferred_element_type=jnp.float32)
+        total = term if total is None else total + term
+    out_ref[...] = total.astype(jnp.bfloat16)
+
+
+def decode(core_at, basis, own, other):
+    vmem = pl.BlockSpec(memory_space=pltpu.VMEM)
+    return pl.pallas_call(
+        decode_kernel,
+        in_specs=[pl.BlockSpec(memory_space=pltpu.SMEM)] + [vmem] * 3,
+        out_specs=vmem,
+        out_shape=jax.ShapeDtypeStruct((256, KVW), jnp.bfloat16),
+        compiler_params=pltpu.CompilerParams(vmem_limit_bytes=16 * 2**20),
+        cost_estimate=pl.CostEstimate(flops=2**28, bytes_accessed=2**21, transcendentals=0),
+        name="decode",
+    )(core_at[None], basis, own, other)
 
 
 def adam_kernel(parts_ref, first_hbm, second_hbm, new_first_ref, new_second_ref, normalized_ref,
@@ -180,35 +201,35 @@
     x_at, z_lo_at, core_at = (lax.axis_index(a) for a in ("x", "z_lo", "core"))
     swap = [(0, 1), (1, 0)]
     place = np.arange(RANK, dtype=np.int32)
-    with jax.named_scope("order"):
-        ranked = reorder(basis, owner_row(place >> 8, place >> 4 & 15, place & 15))
-        decoder = reorder(basis, owner_row(place >> 4 & 1, place >> 5, place & 15))
+    by_core = owner_row(place >> 8, place >> 4 & 15, place & 15)
+    with jax.named_scope("gather_core"):
+        rows = lax.dynamic_slice_in_dim(basis, (x_at >> 1) * 128 + z_lo_at * 32, 32, 0)
+        rows = reorder(rows, by_core)
+        low, high = rows[:, :256], rows[:, 256:]
+        theirs = lax.ppermute(jnp.where(core_at == 0, high, low), "core", swap)
+        chunk = jnp.where(core_at == (x_at & 1), jnp.where(core_at == 0, low, high), theirs)
+
     with jax.named_scope("tokens_x"):
-        packed = pack(x_at, normed_input, value_cotangent)
+        packed = pack(x_at, normed_input, value_cotangent, theirs)
         pieces = [packed[0]] + [
             lax.ppermute(packed[k], "x", [(i, (i + k) % 4) for i in range(4)]) for k in (1, 3, 2)
         ]
-    def gather(rows):
-        with jax.named_scope("gather_core"):
-            low, high = rows[:, :256], rows[:, 256:]
-            theirs = lax.ppermute(jnp.where(core_at == 0, high, low), "core", swap)
-            chunk = jnp.where(core_at == (x_at & 1), jnp.where(core_at == 0, low, high), theirs)
+    def gather(chunk):
         with jax.named_scope("gather_z"):
             line = spread(chunk, Z, 16).reshape(512, 256)
         with jax.named_scope("gather_y"):
             return spread(line, "y", 4).reshape(QUARTER, 256)
 
     with jax.named_scope("gather"):
-        rows = lax.dynamic_slice_in_dim(ranked, (x_at >> 1) * 128 + z_lo_at * 32, 32, 0)
         whole = lax.cond(
-            x_at < 4, gather, lambda rows: jnp.zeros((QUARTER, 256), jnp.bfloat16),
-            join([rows], packed[1]),
+            x_at < 4, gather, lambda chunk: jnp.zeros((QUARTER, 256), jnp.bfloat16),
+            join([chunk], packed[1]),
         )
     with jax.named_scope("tokens_core"):
         held = join(pieces, whole)
-        held = [held, lax.ppermute(held, "core", swap)]
+        other_held = lax.ppermute(held, "core", swap)
     with jax.named_scope("project"):
-        partial = project(held, whole)
+        partial = project(other_held, whole, project(held, whole))
     with jax.named_scope("reduce_xy"):
         summed = jnp.sum(exchange(partial.reshape(16, 16, KVW), ("x", "y")), axis=0)
     with jax.named_scope("reduce_z"):
@@ -218,9 +239,11 @@
     with jax.named_scope("spread_z"):
         column = spread(normalized, Z, 16).reshape(16, KVW)
     with jax.named_scope("spread_xy"):
-        step = spread(column, ("x", "y", "core"), 32).reshape(RANK, KVW)
+        own = spread(column, ("x", "y"), 16).reshape(256, KVW)
+    with jax.named_scope("spread_core"):
+        other = lax.ppermute(own, "core", swap)
     with jax.named_scope("decode"):
-        update = jnp.dot(decoder, step, preferred_element_type=jnp.float32).astype(jnp.bfloat16)
+        update = decode(core_at, reorder(basis, by_core), own, other)
     return new_first, new_second, update
 
 

time: 164 us -> 162 us (0.988)
  blocking collectives: 120 us -> 106 us
  starting transfers between devices: 25.1 us -> 33.6 us
  Pallas kernels: 5.38 us -> 11.1 us
    all_to_all x6, blocking collectives: 120 us -> 106 us  [exchange(): return lax.all_to_all(blocks, axes, 0, 0, tiled=True)]
    ppermute x2 -> x3, starting transfers between devices: 15 us -> 25.1 us  [the longest x1 8.9 us: local(): other_held = lax.ppermute(held, 'core', swap)]
    pallas_call x1 -> x3, Pallas kernels: 2.46 us -> 6.02 us  [the longest x2 4.78 us: project(): pl.pallas_call(project_kernel, in_specs=[vmem] * (2 + len(before)), out_s...]
    pallas_call x1, Pallas kernels: 2.05 us -> 4.21 us  [pack(): pl.pallas_call(pack_kernel, grid=(128 // rows,), in_specs=[pl.BlockSpec(m...]
    dot_general x1 -> x0, matrix products: 1.83 us -> none  [local(): jnp.dot(decoder, step, preferred_element_type=jnp.float32)]
    ppermute x2 -> x3, waiting for transfers between devices: 6.07 us -> 4.8 us  [the longest x1 2.86 us: local(): other_held = lax.ppermute(held, 'core', swap)]
  transfers between devices with their start and end apart: 5 -> 6, of which waited for: 2 -> 3; matrix products, arithmetic and copies ran while one was open for 1% -> 1% of each run, Pallas kernels for 0% -> 1%
where the time goes in v7:
time: 162 us; the launch traced here: 161 us
  blocking collectives  106 us (65%)
  starting transfers between devices  33.6 us (21%)
  Pallas kernels  11.1 us (7%)
  waiting for transfers between devices  4.81 us (3%)
  local copies, waits for them, and re-layouts  2.87 us (2%)
    all_to_all x6, blocking collectives, exchange(): return lax.all_to_all(blocks, axes, 0, 0, tiled=True)  106 us
    ppermute x1, starting transfers between devices, local(): other_held = lax.ppermute(held, 'core', swap)  8.9 us
    ppermute x1, starting transfers between devices, local(): theirs = lax.ppermute(jnp.where(core_at == 0, high, low), 'core', swap)  8.79 us
    ppermute x3, starting transfers between devices, local(): lax.ppermute(packed[k], 'x', [(i, (i + k) % 4) for i in range(4)])  8.53 us
    ppermute x1, starting transfers between devices, local(): other = lax.ppermute(own, 'core', swap)  7.39 us
    pallas_call x2, Pallas kernels, project(): pl.pallas_call(project_kernel, in_specs=[vmem] * (2 + len(before)), out_s...  4.78 us
    pallas_call x1, Pallas kernels, pack(): pl.pallas_call(pack_kernel, grid=(128 // rows,), in_specs=[pl.BlockSpec(m...  4.21 us
  transfers between devices with their start and end apart: 6, of which 3 were waited for; matrix products, arithmetic and copies ran while one was open for 1% of the time, Pallas kernels for 1%

profile of v7, /device:TPU:1, one launch (start us, length us, event | category | flops | bytes accessed | tf_op | source)
XLA Modules:
  0.0 161.1 jit_solution(13968619290889569749)
XLA Ops:
  0.7 0.9 copy-done
  1.6 1.0 convolution_convert_fusion.1
  2.6 8.8 %collective-permute-start = (bf16[32,256]{1,0:T(8,128)(2,1)S(1)}, bf16[32,256]{1,0:T(8,128)(2,1)S(1)}, u32[]{:S(2)}, u32[]{:S(2)}) collective-permute-start(bf16[32,256]{1,0:T(8,128)(2,1)S(1)} %broadcast_select_fusion), channel_id=1, source_target_pairs={{0,1},{1,0},{2,3},{3,2},{4,5},{5,4},{6,7},{7,6},{8,9},{9,8},{10,11... | collective-permute-start | bytes 49160 | tf_op jit(solution)/shard_map/gather_core/ppermute | solution.py:209
  11.4 0.8 collective-permute-done._
  12.8 4.2 %pack.1 = (bf16[128,3072]{1,0:T(8,128)(2,1)}, bf16[128,3072]{1,0:T(8,128)(2,1)}, bf16[128,3072]{1,0:T(8,128)(2,1)}, bf16[128,3072]{1,0:T(8,128)(2,1)}) custom-call(s32[1]{0:T(128)} %bitcast.2.x_ref, bf16[128,8192]{1,0:T(8,128)(2,1)} %tokens_ref.1, bf16[128,1024]{1,0:T(8,128)(2,1)} %cotangent_ref.1, bf16[32,256]{1,0:T(8,128)(2,1)} %copy-done.6), custom_call_target="tpu_custom_call" | custom-call | bytes 6291456 | tf_op jit(solution)/shard_map/tokens_x/pack/pallas_call | solution.py:58
  17.0 2.0 %collective-permute-start.1 = (bf16[128,3072]{1,0:T(8,128)(2,1)}, bf16[128,3072]{1,0:T(8,128)(2,1)S(1)}, u32[]{:S(2)}, u32[]{:S(2)}) collective-permute-start(bf16[128,3072]{1,0:T(8,128)(2,1)} %get-tuple-element.15.refs_1_), channel_id=1, source_target_pairs={{0,32},{32,64},{64,96},{96,0},{1,33},{33,65},{65,97},{97,1},{2,34}... | collective-permute-start | bytes 2359304 | tf_op jit(solution)/shard_map/tokens_x/ppermute | solution.py:215
  19.0 4.6 %collective-permute-start.2 = (bf16[128,3072]{1,0:T(8,128)(2,1)}, bf16[128,3072]{1,0:T(8,128)(2,1)S(1)}, u32[]{:S(2)}, u32[]{:S(2)}) collective-permute-start(bf16[128,3072]{1,0:T(8,128)(2,1)} %get-tuple-element.16), channel_id=1, source_target_pairs={{0,96},{32,0},{64,32},{96,64},{1,97},{33,1},{65,33},{97,65},{2,98}... | collective-permute-start | bytes 2359304 | tf_op jit(solution)/shard_map/tokens_x/ppermute | solution.py:215
  23.6 1.9 %collective-permute-start.3 = (bf16[128,3072]{1,0:T(8,128)(2,1)}, bf16[128,3072]{1,0:T(8,128)(2,1)S(1)}, u32[]{:S(2)}, u32[]{:S(2)}) collective-permute-start(bf16[128,3072]{1,0:T(8,128)(2,1)} %get-tuple-element.17), channel_id=1, source_target_pairs={{0,64},{32,96},{64,0},{96,32},{1,65},{33,97},{65,1},{97,33},{2,66}... | collective-permute-start | bytes 2359304 | tf_op jit(solution)/shard_map/tokens_x/ppermute | solution.py:215
  25.6 0.7 select_select_fusion.refs_0_
  26.3 1.1 copy-done.2
  27.4 38.5 %conditional.1 = (bf16[2048,256]{1,0:T(8,128)(2,1)}) conditional(s32[]{:T(128)} %convert_element_type.14, () %tuple.14, bf16[32,256]{1,0:T(8,128)(2,1)S(1)} %join.2), branch_computations={%region_0.1_spmd, %region_1.2_spmd} | conditional | bytes 4210696 | solution.py:224
  27.5 24.6 %all_to_all.28 = bf16[16,32,256]{2,1,0:T(8,128)(2,1)S(1)} all-to-all(bf16[16,32,256]{2,1,0:T(8,128)(2,1)S(1)} %broadcast_in_dim.7), channel_id=1, replica_groups=mesh['z_lo'=4,'x'=4,'y'=4,'z_hi'=4,'core'=2] {'z_hi','z_lo'}, dimensions={0} | all-to-all | bytes 524288 | tf_op jit(solution)/shard_map/gather/cond/branch_1_fun/gather_z/all_to_all | solution.py:38
  52.1 13.8 %all_to_all.29 = bf16[4,512,256]{2,1,0:T(8,128)(2,1)} all-to-all(bf16[4,512,256]{2,1,0:T(8,128)(2,1)S(1)} %broadcast_in_dim.17), channel_id=1, replica_groups=mesh['z_lo'=4,'x'=4,'y'=4,'z_hi'=4,'core'=2] {'y'}, dimensions={0} | all-to-all | bytes 2097152 | tf_op jit(solution)/shard_map/gather/cond/branch_1_fun/gather_y/all_to_all | solution.py:38
  66.2 8.9 %collective-permute-start.4 = (bf16[512,3072]{1,0:T(8,128)(2,1)S(1)}, bf16[512,3072]{1,0:T(8,128)(2,1)S(1)}, u32[]{:S(2)}, u32[]{:S(2)}) collective-permute-start(bf16[512,3072]{1,0:T(8,128)(2,1)S(1)} %join.3.tokens_ref), channel_id=1, source_target_pairs={{0,1},{1,0},{2,3},{3,2},{4,5},{5,4},{6,7},{7,6},{8,9},{9,8},{10,11... | collective-permute-start | bytes 9437192 | tf_op jit(solution)/shard_map/tokens_core/ppermute | solution.py:230
  75.1 2.4 %project.2.refs_0_ = f32[256,1024]{1,0:T(8,128)S(1)} custom-call(bf16[512,3072]{1,0:T(8,128)(2,1)S(1)} %join.3.tokens_ref, bf16[2048,256]{1,0:T(8,128)(2,1)S(1)} %copy-done.5), custom_call_target="tpu_custom_call" | custom-call | flops 1073741824 | bytes 6291456 | tf_op jit(solution)/shard_map/project/project/pallas_call | solution.py:120
  77.5 2.9 %collective-permute-done.4.tokens_ref = bf16[512,3072]{1,0:T(8,128)(2,1)S(1)} collective-permute-done((bf16[512,3072]{1,0:T(8,128)(2,1)S(1)}, bf16[512,3072]{1,0:T(8,128)(2,1)S(1)}, u32[]{:S(2)}, u32[]{:S(2)}) %collective-permute-start.4) | collective-permute-done | bytes 3145760 | tf_op jit(solution)/shard_map/tokens_core/ppermute | solution.py:230
  80.4 2.4 %project.3 = f32[256,1024]{1,0:T(8,128)S(1)} custom-call(bf16[512,3072]{1,0:T(8,128)(2,1)S(1)} %collective-permute-done.4.tokens_ref, bf16[2048,256]{1,0:T(8,128)(2,1)S(1)} %copy-done.5, f32[256,1024]{1,0:T(8,128)S(1)} %project.2.refs_0_), custom_call_target="tpu_custom_call" | custom-call | flops 1073741824 | bytes 6291456 | tf_op jit(solution)/shard_map/project/project/pallas_call | solution.py:120
  82.8 19.3 %all_to_all.30 = f32[16,16,1024]{2,1,0:T(8,128)S(1)} all-to-all(f32[16,16,1024]{2,1,0:T(8,128)S(1)} %bitcast.15), channel_id=1, replica_groups=mesh['z_lo'=4,'x'=4,'y'=4,'z_hi'=4,'core'=2] {'x','y'}, dimensions={0} | all-to-all | bytes 2097152 | tf_op jit(solution)/shard_map/reduce_xy/all_to_all | solution.py:38
  102.2 21.3 %all_to_all.31.parts_ref = f32[16,8,128]{2,1,0:T(8,128)S(1)} all-to-all(f32[16,8,128]{2,1,0:T(8,128)S(1)} %bitcast.21), channel_id=1, replica_groups=mesh['z_lo'=4,'x'=4,'y'=4,'z_hi'=4,'core'=2] {'z_hi','z_lo'}, dimensions={0} | all-to-all | bytes 131072 | tf_op jit(solution)/shard_map/reduce_z/all_to_all | solution.py:38
  124.2 14.2 %all_to_all.32 = bf16[16,8,128]{2,1,0:T(8,128)(2,1)S(1)} all-to-all(bf16[16,8,128]{2,1,0:T(8,128)(2,1)S(1)} %broadcast_in_dim.34), channel_id=1, replica_groups=mesh['z_lo'=4,'x'=4,'y'=4,'z_hi'=4,'core'=2] {'z_hi','z_lo'}, dimensions={0} | all-to-all | bytes 65536 | tf_op jit(solution)/shard_map/spread_z/all_to_all | solution.py:38
  138.5 12.5 %all_to_all.33 = bf16[16,16,1024]{2,1,0:T(8,128)(2,1)S(1)} all-to-all(bf16[16,16,1024]{2,1,0:T(8,128)(2,1)S(1)} %broadcast_in_dim.36), channel_id=1, replica_groups=mesh['z_lo'=4,'x'=4,'y'=4,'z_hi'=4,'core'=2] {'x','y'}, dimensions={0} | all-to-all | bytes 1048576 | tf_op jit(solution)/shard_map/spread_xy/all_to_all | solution.py:38
  151.0 7.4 %collective-permute-start.5 = (bf16[256,1024]{1,0:T(8,128)(2,1)S(1)}, bf16[256,1024]{1,0:T(8,128)(2,1)S(1)}, u32[]{:S(2)}, u32[]{:S(2)}) collective-permute-start(bf16[256,1024]{1,0:T(8,128)(2,1)S(1)} %bitcast.16), channel_id=1, source_target_pairs={{0,1},{1,0},{2,3},{3,2},{4,5},{5,4},{6,7},{7,6},{8,9},{9,8},{10,11... | collective-permute-start | bytes 1572872 | tf_op jit(solution)/shard_map/spread_core/ppermute | solution.py:244
  158.7 1.1 collective-permute-done.5.other_ref
  159.9 1.2 decode.1
  (29 shorter events, 2.1 us)
Async XLA Ops:
  0.6 1.0 copy-start
  2.6 9.6 %collective-permute-start = (bf16[32,256]{1,0:T(8,128)(2,1)S(1)}, bf16[32,256]{1,0:T(8,128)(2,1)S(1)}, u32[]{:S(2)}, u32[]{:S(2)}) collective-permute-start(bf16[32,256]{1,0:T(8,128)(2,1)S(1)} %broadcast_select_fusion), channel_id=1, source_target_pairs={{0,1},{1,0},{2,3},{3,2},{4,5},{5,4},{6,7},{7,6},{8,9},{9,8},{10,11... | collective-permute-start | bytes 49160 | tf_op jit(solution)/shard_map/gather_core/ppermute | solution.py:209
  12.2 0.6 copy-start.6
  17.0 49.0 %copy-start.1 = (bf16[128,3072]{1,0:T(8,128)(2,1)S(1)}, bf16[128,3072]{1,0:T(8,128)(2,1)}, u32[]{:S(2)}) copy-start(bf16[128,3072]{1,0:T(8,128)(2,1)} %get-tuple-element.14.refs_0_) | copy-start | bytes 2359300
  17.0 49.0 %collective-permute-start.1 = (bf16[128,3072]{1,0:T(8,128)(2,1)}, bf16[128,3072]{1,0:T(8,128)(2,1)S(1)}, u32[]{:S(2)}, u32[]{:S(2)}) collective-permute-start(bf16[128,3072]{1,0:T(8,128)(2,1)} %get-tuple-element.15.refs_1_), channel_id=1, source_target_pairs={{0,32},{32,64},{64,96},{96,0},{1,33},{33,65},{65,97},{97,1},{2,34}... | collective-permute-start | bytes 2359304 | tf_op jit(solution)/shard_map/tokens_x/ppermute | solution.py:215
  19.0 46.9 %collective-permute-start.2 = (bf16[128,3072]{1,0:T(8,128)(2,1)}, bf16[128,3072]{1,0:T(8,128)(2,1)S(1)}, u32[]{:S(2)}, u32[]{:S(2)}) collective-permute-start(bf16[128,3072]{1,0:T(8,128)(2,1)} %get-tuple-element.16), channel_id=1, source_target_pairs={{0,96},{32,0},{64,32},{96,64},{1,97},{33,1},{65,33},{97,65},{2,98}... | collective-permute-start | bytes 2359304 | tf_op jit(solution)/shard_map/tokens_x/ppermute | solution.py:215
  23.6 42.4 %collective-permute-start.3 = (bf16[128,3072]{1,0:T(8,128)(2,1)}, bf16[128,3072]{1,0:T(8,128)(2,1)S(1)}, u32[]{:S(2)}, u32[]{:S(2)}) collective-permute-start(bf16[128,3072]{1,0:T(8,128)(2,1)} %get-tuple-element.17), channel_id=1, source_target_pairs={{0,64},{32,96},{64,0},{96,32},{1,65},{33,97},{65,1},{97,33},{2,66}... | collective-permute-start | bytes 2359304 | tf_op jit(solution)/shard_map/tokens_x/ppermute | solution.py:215
  26.3 1.1 copy-start.2
  66.0 9.1 %copy-start.5 = (bf16[2048,256]{1,0:T(8,128)(2,1)S(1)}, bf16[2048,256]{1,0:T(8,128)(2,1)}, u32[]{:S(2)}) copy-start(bf16[2048,256]{1,0:T(8,128)(2,1)} %get-tuple-element.21.refs_4_.whole_ref) | copy-start | bytes 3145732
  66.2 14.2 %collective-permute-start.4 = (bf16[512,3072]{1,0:T(8,128)(2,1)S(1)}, bf16[512,3072]{1,0:T(8,128)(2,1)S(1)}, u32[]{:S(2)}, u32[]{:S(2)}) collective-permute-start(bf16[512,3072]{1,0:T(8,128)(2,1)S(1)} %join.3.tokens_ref), channel_id=1, source_target_pairs={{0,1},{1,0},{2,3},{3,2},{4,5},{5,4},{6,7},{7,6},{8,9},{9,8},{10,11... | collective-permute-start | bytes 9437192 | tf_op jit(solution)/shard_map/tokens_core/ppermute | solution.py:230
  82.8 40.7 %copy-start.3 = (f32[1,1024]{1,0:T(1,128)S(1)}, f32[1,1024]{1,0:T(1,128)}, u32[]{:S(2)}) copy-start(f32[1,1024]{1,0:T(1,128)} %first_hbm.1) | copy-start | bytes 12292
  82.8 40.7 %copy-start.4 = (f32[1,1024]{1,0:T(1,128)S(1)}, f32[1,1024]{1,0:T(1,128)}, u32[]{:S(2)}) copy-start(f32[1,1024]{1,0:T(1,128)} %second_hbm.1) | copy-start | bytes 12292
  82.8 75.5 %copy-start.7 = (s32[512]{0:T(512)S(1)}, s32[512]{0:T(512)}, u32[]{:S(2)}) copy-start(s32[512]{0:T(512)} %constant.37) | copy-start | bytes 6148
  151.0 8.9 %collective-permute-start.5 = (bf16[256,1024]{1,0:T(8,128)(2,1)S(1)}, bf16[256,1024]{1,0:T(8,128)(2,1)S(1)}, u32[]{:S(2)}, u32[]{:S(2)}) collective-permute-start(bf16[256,1024]{1,0:T(8,128)(2,1)S(1)} %bitcast.16), channel_id=1, source_target_pairs={{0,1},{1,0},{2,3},{3,2},{4,5},{5,4},{6,7},{7,6},{8,9},{9,8},{10,11... | collective-permute-start | bytes 1572872 | tf_op jit(solution)/shard_map/spread_core/ppermute | solution.py:244

commit v8 on v6

--- a/solution.py
+++ b/solution.py
@@ -86,7 +86,7 @@
         in_specs=[vmem] * len(pieces) + [pl.BlockSpec(memory_space=pl.ANY)],
         out_specs=vmem,
         out_shape=jax.ShapeDtypeStruct((rows * len(pieces), columns), jnp.bfloat16),
-        compiler_params=pltpu.CompilerParams(vmem_limit_bytes=16 * 2**20),
+        compiler_params=pltpu.CompilerParams(vmem_limit_bytes=56 * 2**20),
         cost_estimate=pl.CostEstimate(flops=0, bytes_accessed=2**20, transcendentals=0),
         name="join",
     )(*pieces, other)
@@ -122,12 +122,34 @@
         out_specs=vmem,
         out_shape=jax.ShapeDtypeStruct((256, KVW), jnp.float32),
         scratch_shapes=[pltpu.VMEM((2048, 256), jnp.bfloat16)],
-        compiler_params=pltpu.CompilerParams(vmem_limit_bytes=40 * 2**20),
+        compiler_params=pltpu.CompilerParams(vmem_limit_bytes=56 * 2**20),
         cost_estimate=pl.CostEstimate(
             flops=2 * 2**30, bytes_accessed=8 * 2**20, transcendentals=0
         ),
         name="project",
     )(*pieces, whole)
+
+
+def decode_kernel(core_ref, basis_ref, own_ref, other_ref, out_ref):
+    total = None
+    for at, rows_ref in ((core_ref[0], own_ref), (1 - core_ref[0], other_ref)):
+        half = basis_ref[:, pl.ds(pl.multiple_of(at * 256, 256), 256)]
+        term = jnp.dot(half, rows_ref[...], preferred_element_type=jnp.float32)
+        total = term if total is None else total + term
+    out_ref[...] = total.astype(jnp.bfloat16)
+
+
+def decode(core_at, basis, own, other):
+    vmem = pl.BlockSpec(memory_space=pltpu.VMEM)
+    return pl.pallas_call(
+        decode_kernel,
+        in_specs=[pl.BlockSpec(memory_space=pltpu.SMEM)] + [vmem] * 3,
+        out_specs=vmem,
+        out_shape=jax.ShapeDtypeStruct((256, KVW), jnp.bfloat16),
+        compiler_params=pltpu.CompilerParams(vmem_limit_bytes=16 * 2**20),
+        cost_estimate=pl.CostEstimate(flops=2**28, bytes_accessed=2**21, transcendentals=0),
+        name="decode",
+    )(core_at[None], basis, own, other)
 
 
 def adam_kernel(parts_ref, first_hbm, second_hbm, new_first_ref, new_second_ref, normalized_ref,
@@ -180,35 +202,41 @@
     x_at, z_lo_at, core_at = (lax.axis_index(a) for a in ("x", "z_lo", "core"))
     swap = [(0, 1), (1, 0)]
     place = np.arange(RANK, dtype=np.int32)
-    with jax.named_scope("order"):
-        ranked = reorder(basis, owner_row(place >> 8, place >> 4 & 15, place & 15))
-        decoder = reorder(basis, owner_row(place >> 4 & 1, place >> 5, place & 15))
+    by_core = owner_row(place >> 8, place >> 4 & 15, place & 15)
     with jax.named_scope("tokens_x"):
         packed = pack(x_at, normed_input, value_cotangent)
         pieces = [packed[0]] + [
             lax.ppermute(packed[k], "x", [(i, (i + k) % 4) for i in range(4)]) for k in (1, 3, 2)
         ]
-    def gather(rows):
+
+    def gather_z(rows):
         with jax.named_scope("gather_core"):
             low, high = rows[:, :256], rows[:, 256:]
             theirs = lax.ppermute(jnp.where(core_at == 0, high, low), "core", swap)
             chunk = jnp.where(core_at == (x_at & 1), jnp.where(core_at == 0, low, high), theirs)
         with jax.named_scope("gather_z"):
-            line = spread(chunk, Z, 16).reshape(512, 256)
+            return spread(chunk, Z, 16).reshape(512, 256)
+
+    def gather_y(line):
         with jax.named_scope("gather_y"):
             return spread(line, "y", 4).reshape(QUARTER, 256)
 
+    def in_order(step, block, out_rows):
+        return lax.cond(
+            x_at < 4, step, lambda block: jnp.zeros((out_rows, 256), jnp.bfloat16), block
+        )
+
     with jax.named_scope("gather"):
-        rows = lax.dynamic_slice_in_dim(ranked, (x_at >> 1) * 128 + z_lo_at * 32, 32, 0)
-        whole = lax.cond(
-            x_at < 4, gather, lambda rows: jnp.zeros((QUARTER, 256), jnp.bfloat16),
-            join([rows], packed[1]),
-        )
+        rows = lax.dynamic_slice_in_dim(basis, (x_at >> 1) * 128 + z_lo_at * 32, 32, 0)
+        rows = reorder(rows, by_core)
+        line = in_order(gather_z, join([rows], packed[1]), 512)
     with jax.named_scope("tokens_core"):
-        held = join(pieces, whole)
-        held = [held, lax.ppermute(held, "core", swap)]
+        held = join(pieces, line)
+        other_held = lax.ppermute(held, "core", swap)
+    with jax.named_scope("gather"):
+        whole = in_order(gather_y, join([line], held), QUARTER)
     with jax.named_scope("project"):
-        partial = project(held, whole)
+        partial = project([held, other_held], whole)
     with jax.named_scope("reduce_xy"):
         summed = jnp.sum(exchange(partial.reshape(16, 16, KVW), ("x", "y")), axis=0)
     with jax.named_scope("reduce_z"):
@@ -218,9 +246,11 @@
     with jax.named_scope("spread_z"):
         column = spread(normalized, Z, 16).reshape(16, KVW)
     with jax.named_scope("spread_xy"):
-        step = spread(column, ("x", "y", "core"), 32).reshape(RANK, KVW)
+        own = spread(column, ("x", "y"), 16).reshape(256, KVW)
+    with jax.named_scope("spread_core"):
+        other = lax.ppermute(own, "core", swap)
     with jax.named_scope("decode"):
-        update = jnp.dot(decoder, step, preferred_element_type=jnp.float32).astype(jnp.bfloat16)
+        update = decode(core_at, reorder(basis, by_core), own, other)
     return new_first, new_second, update
 
 

time: 164 us -> 164 us (level)
  blocking collectives: 120 us -> 109 us
  Pallas kernels: 5.38 us -> 13.3 us
  starting transfers between devices: 25.1 us -> 33 us
  waiting for transfers between devices: 6.08 us -> 1.95 us
    all_to_all x6, blocking collectives: 120 us -> 109 us  [exchange(): return lax.all_to_all(blocks, axes, 0, 0, tiled=True)]
    ppermute x2 -> x3, starting transfers between devices: 15 us -> 22.2 us  [the longest x1 8.2 us: local(): other = lax.ppermute(own, 'core', swap)]
    pallas_call x2 -> x3, Pallas kernels: 0.21 us -> 4.49 us  [join(): pl.pallas_call(join_kernel, in_specs=[vmem] * len(pieces) + [pl.BlockSpec...]
    ppermute x2 -> x3, waiting for transfers between devices: 6.07 us -> 1.94 us  [the longest x1 1.13 us: local(): other = lax.ppermute(own, 'core', swap)]
    pallas_call x1, Pallas kernels: 2.46 us -> 6.31 us  [project(): pl.pallas_call(project_kernel, in_specs=[vmem] * (len(pieces) + 1), out_s...]
    dot_general x1 -> x0, matrix products: 1.83 us -> none  [local(): jnp.dot(decoder, step, preferred_element_type=jnp.float32)]
    unnamed x16 -> x18, local copies, waits for them, and re-layouts: 2.63 us -> 3.52 us
  transfers between devices with their start and end apart: 5 -> 6, of which waited for: 2 -> 2; matrix products, arithmetic and copies ran while one was open for 1% -> 1% of each run, Pallas kernels for 0% -> 0%
where the time goes in v8:
time: 164 us; the launch traced here: 163 us
  blocking collectives  109 us (66%)
  starting transfers between devices  33 us (20%)
  Pallas kernels  13.3 us (8%)
  local copies, waits for them, and re-layouts  3.67 us (2%)
  matrix products  1.97 us (1%)
  waiting for transfers between devices  1.95 us (1%)
    all_to_all x6, blocking collectives, exchange(): return lax.all_to_all(blocks, axes, 0, 0, tiled=True)  109 us
    ppermute x3, starting transfers between devices, local(): lax.ppermute(packed[k], 'x', [(i, (i + k) % 4) for i in range(4)])  10.8 us
    ppermute x1, starting transfers between devices, local(): other = lax.ppermute(own, 'core', swap)  8.2 us
    ppermute x1, starting transfers between devices, local(): other_held = lax.ppermute(held, 'core', swap)  7.03 us
    ppermute x1, starting transfers between devices, gather_z(): theirs = lax.ppermute(jnp.where(core_at == 0, high, low), 'core', swap)  7 us
    pallas_call x1, Pallas kernels, project(): pl.pallas_call(project_kernel, in_specs=[vmem] * (len(pieces) + 1), out_s...  6.31 us
    pallas_call x3, Pallas kernels, join(): pl.pallas_call(join_kernel, in_specs=[vmem] * len(pieces) + [pl.BlockSpec...  4.49 us
    unnamed x18, local copies, waits for them, and re-layouts  3.52 us
  transfers between devices with their start and end apart: 6, of which 2 were waited for; matrix products, arithmetic and copies ran while one was open for 1% of the time, Pallas kernels for 0%

profile of v8, /device:TPU:1, one launch (start us, length us, event | category | flops | bytes accessed | tf_op | source)
XLA Modules:
  0.0 163.3 jit_solution(1271253730603139408)
XLA Ops:
  0.7 1.6 copy-done.1
  2.3 0.9 copy-done.4
  3.9 0.9 copy-done.2
  4.8 3.9 %collective-permute-start.1 = (bf16[128,3072]{1,0:T(8,128)(2,1)S(1)}, bf16[128,3072]{1,0:T(8,128)(2,1)}, u32[]{:S(2)}, u32[]{:S(2)}) collective-permute-start(bf16[128,3072]{1,0:T(8,128)(2,1)S(1)} %get-tuple-element.27.refs_1_), channel_id=1, source_target_pairs={{0,32},{32,64},{64,96},{96,0},{1,33},{33,65},{65,97},{97,1},{2,34}... | collective-permute-start | bytes 2359304 | tf_op jit(solution)/shard_map/tokens_x/ppermute | solution.py:209
  8.7 3.2 %collective-permute-start.2 = (bf16[128,3072]{1,0:T(8,128)(2,1)S(1)}, bf16[128,3072]{1,0:T(8,128)(2,1)}, u32[]{:S(2)}, u32[]{:S(2)}) collective-permute-start(bf16[128,3072]{1,0:T(8,128)(2,1)S(1)} %get-tuple-element.28), channel_id=1, source_target_pairs={{0,96},{32,0},{64,32},{96,64},{1,97},{33,1},{65,33},{97,65},{2,98}... | collective-permute-start | bytes 2359304 | tf_op jit(solution)/shard_map/tokens_x/ppermute | solution.py:209
  11.9 3.6 %collective-permute-start.3 = (bf16[128,3072]{1,0:T(8,128)(2,1)S(1)}, bf16[128,3072]{1,0:T(8,128)(2,1)}, u32[]{:S(2)}, u32[]{:S(2)}) collective-permute-start(bf16[128,3072]{1,0:T(8,128)(2,1)S(1)} %get-tuple-element.29), channel_id=1, source_target_pairs={{0,64},{32,96},{64,0},{96,32},{1,65},{33,97},{65,1},{97,33},{2,66}... | collective-permute-start | bytes 2359304 | tf_op jit(solution)/shard_map/tokens_x/ppermute | solution.py:209
  15.6 1.6 convolution_convert_fusion.1.refs_0_
  17.2 0.8 join.3
  17.9 33.0 %conditional.2 = (bf16[512,256]{1,0:T(8,128)(2,1)S(1)}) conditional(s32[]{:T(128)} %convert_element_type.14, () %tuple.20, (s32[]{:T(128)}, s32[]{:T(128)}, bf16[32,512]{1,0:T(8,128)(2,1)S(1)}) %tuple.21), branch_computations={%region_0.0_spmd, %region_1.2_spmd} | conditional | flops 24579 | bytes 983121 | solution.py:225
  17.9 7.0 %collective-permute-start = (bf16[32,256]{1,0:T(8,128)(2,1)S(1)}, bf16[32,256]{1,0:T(8,128)(2,1)S(1)}, u32[]{:S(2)}, u32[]{:S(2)}) collective-permute-start(bf16[32,256]{1,0:T(8,128)(2,1)S(1)} %broadcast_select_fusion), channel_id=1, source_target_pairs={{0,1},{1,0},{2,3},{3,2},{4,5},{5,4},{6,7},{7,6},{8,9},{9,8},{10,11... | collective-permute-start | bytes 49160 | tf_op jit(solution)/shard_map/gather/cond/branch_1_fun/gather_core/ppermute | solution.py:215
  25.0 0.8 collective-permute-done
  25.8 25.2 %all_to_all.28 = bf16[16,32,256]{2,1,0:T(8,128)(2,1)S(1)} all-to-all(bf16[16,32,256]{2,1,0:T(8,128)(2,1)S(1)} %broadcast_in_dim.1), channel_id=1, replica_groups=mesh['z_lo'=4,'x'=4,'y'=4,'z_hi'=4,'core'=2] {'z_hi','z_lo'}, dimensions={0} | all-to-all | bytes 524288 | tf_op jit(solution)/shard_map/gather/cond/branch_1_fun/gather_z/all_to_all | solution.py:38
  51.0 3.7 %join.4.refs_1_.refs_0_ = bf16[512,3072]{1,0:T(8,128)(2,1)} custom-call(bf16[128,3072]{1,0:T(8,128)(2,1)} %copy-done.2, bf16[128,3072]{1,0:T(8,128)(2,1)} %collective-permute-done.1.refs_1_, bf16[128,3072]{1,0:T(8,128)(2,1)} %collective-permute-done.2.refs_2_, bf16[128,3072]{1,0:T(8,128)(2,1)} %collective-permute-done.3.refs_3_, ...), custom_call_target="tpu_custom_call" | custom-call | bytes 1048576 | tf_op jit(solution)/shard_map/tokens_core/join/pallas_call | solution.py:84
  54.7 7.0 %collective-permute-start.4 = (bf16[512,3072]{1,0:T(8,128)(2,1)}, bf16[512,3072]{1,0:T(8,128)(2,1)}, u32[]{:S(2)}, u32[]{:S(2)}) collective-permute-start(bf16[512,3072]{1,0:T(8,128)(2,1)} %join.4.refs_1_.refs_0_), channel_id=1, source_target_pairs={{0,1},{1,0},{2,3},{3,2},{4,5},{5,4},{6,7},{7,6},{8,9},{9,8},{10,11... | collective-permute-start | bytes 9437192 | tf_op jit(solution)/shard_map/tokens_core/ppermute | solution.py:235
  61.8 19.0 %conditional.3 = (bf16[2048,256]{1,0:T(8,128)(2,1)S(1)}) conditional(s32[]{:T(128)} %convert_element_type.14, () %tuple.22, bf16[512,256]{1,0:T(8,128)(2,1)S(1)} %join.5), branch_computations={%region_2.3_spmd, %region_3.4_spmd} | conditional | bytes 3407880 | solution.py:225
  61.8 18.9 %all_to_all.29 = bf16[4,512,256]{2,1,0:T(8,128)(2,1)S(1)} all-to-all(bf16[4,512,256]{2,1,0:T(8,128)(2,1)S(1)} %broadcast_in_dim.3), channel_id=1, replica_groups=mesh['z_lo'=4,'x'=4,'y'=4,'z_hi'=4,'core'=2] {'y'}, dimensions={0} | all-to-all | bytes 2097152 | tf_op jit(solution)/shard_map/gather/cond/branch_1_fun/gather_y/all_to_all | solution.py:38
  80.8 6.3 %project.1 = f32[256,1024]{1,0:T(8,128)} custom-call(bf16[512,3072]{1,0:T(8,128)(2,1)} %join.4.refs_1_.refs_0_, bf16[512,3072]{1,0:T(8,128)(2,1)} %collective-permute-done.4.refs_1_, bf16[2048,256]{1,0:T(8,128)(2,1)S(1)} %get-tuple-element.34.refs_2_), custom_call_target="tpu_custom_call" | custom-call | flops 2147483648 | bytes 8388608 | tf_op jit(solution)/shard_map/project/project/pallas_call | solution.py:119
  87.1 19.4 %all_to_all.30 = f32[16,16,1024]{2,1,0:T(8,128)S(1)} all-to-all(f32[16,16,1024]{2,1,0:T(8,128)} %bitcast.17), channel_id=1, replica_groups=mesh['z_lo'=4,'x'=4,'y'=4,'z_hi'=4,'core'=2] {'x','y'}, dimensions={0} | all-to-all | bytes 2097152 | tf_op jit(solution)/shard_map/reduce_xy/all_to_all | solution.py:38
  106.5 17.7 %all_to_all.31.parts_ref = f32[16,8,128]{2,1,0:T(8,128)S(1)} all-to-all(f32[16,8,128]{2,1,0:T(8,128)S(1)} %bitcast.21), channel_id=1, replica_groups=mesh['z_lo'=4,'x'=4,'y'=4,'z_hi'=4,'core'=2] {'z_hi','z_lo'}, dimensions={0} | all-to-all | bytes 131072 | tf_op jit(solution)/shard_map/reduce_z/all_to_all | solution.py:38
  124.9 14.3 %all_to_all.32 = bf16[16,8,128]{2,1,0:T(8,128)(2,1)S(1)} all-to-all(bf16[16,8,128]{2,1,0:T(8,128)(2,1)S(1)} %broadcast_in_dim.24), channel_id=1, replica_groups=mesh['z_lo'=4,'x'=4,'y'=4,'z_hi'=4,'core'=2] {'z_hi','z_lo'}, dimensions={0} | all-to-all | bytes 65536 | tf_op jit(solution)/shard_map/spread_z/all_to_all | solution.py:38
  139.3 13.1 %all_to_all.33 = bf16[16,16,1024]{2,1,0:T(8,128)(2,1)S(1)} all-to-all(bf16[16,16,1024]{2,1,0:T(8,128)(2,1)S(1)} %broadcast_in_dim.35), channel_id=1, replica_groups=mesh['z_lo'=4,'x'=4,'y'=4,'z_hi'=4,'core'=2] {'x','y'}, dimensions={0} | all-to-all | bytes 1048576 | tf_op jit(solution)/shard_map/spread_xy/all_to_all | solution.py:38
  152.4 8.2 %collective-permute-start.5 = (bf16[256,1024]{1,0:T(8,128)(2,1)S(1)}, bf16[256,1024]{1,0:T(8,128)(2,1)S(1)}, u32[]{:S(2)}, u32[]{:S(2)}) collective-permute-start(bf16[256,1024]{1,0:T(8,128)(2,1)S(1)} %bitcast.15), channel_id=1, source_target_pairs={{0,1},{1,0},{2,3},{3,2},{4,5},{5,4},{6,7},{7,6},{8,9},{9,8},{10,11... | collective-permute-start | bytes 1572872 | tf_op jit(solution)/shard_map/spread_core/ppermute | solution.py:251
  161.0 1.1 collective-permute-done.5.other_ref
  162.1 1.2 decode.1
  (30 shorter events, 1.9 us)
Async XLA Ops:
  0.6 14.9 %copy-start = (bf16[256,512]{1,0:T(8,128)(2,1)S(1)}, bf16[256,512]{1,0:T(8,128)(2,1)}, u32[]{:S(2)}) copy-start(bf16[256,512]{1,0:T(8,128)(2,1)} %param.13) | copy-start | bytes 786436
  0.7 1.6 copy-start.1
  2.3 0.9 copy-start.4
  3.9 0.9 copy-start.2
  4.8 12.4 %copy-start.3 = (bf16[128,3072]{1,0:T(8,128)(2,1)}, bf16[128,3072]{1,0:T(8,128)(2,1)S(1)}, u32[]{:S(2)}) copy-start(bf16[128,3072]{1,0:T(8,128)(2,1)S(1)} %get-tuple-element.27.refs_1_) | copy-start | bytes 2359300
  4.8 46.2 %collective-permute-start.1 = (bf16[128,3072]{1,0:T(8,128)(2,1)S(1)}, bf16[128,3072]{1,0:T(8,128)(2,1)}, u32[]{:S(2)}, u32[]{:S(2)}) collective-permute-start(bf16[128,3072]{1,0:T(8,128)(2,1)S(1)} %get-tuple-element.27.refs_1_), channel_id=1, source_target_pairs={{0,32},{32,64},{64,96},{96,0},{1,33},{33,65},{65,97},{97,1},{2,34}... | collective-permute-start | bytes 2359304 | tf_op jit(solution)/shard_map/tokens_x/ppermute | solution.py:209
  8.7 42.3 %collective-permute-start.2 = (bf16[128,3072]{1,0:T(8,128)(2,1)S(1)}, bf16[128,3072]{1,0:T(8,128)(2,1)}, u32[]{:S(2)}, u32[]{:S(2)}) collective-permute-start(bf16[128,3072]{1,0:T(8,128)(2,1)S(1)} %get-tuple-element.28), channel_id=1, source_target_pairs={{0,96},{32,0},{64,32},{96,64},{1,97},{33,1},{65,33},{97,65},{2,98}... | collective-permute-start | bytes 2359304 | tf_op jit(solution)/shard_map/tokens_x/ppermute | solution.py:209
  11.9 39.1 %collective-permute-start.3 = (bf16[128,3072]{1,0:T(8,128)(2,1)S(1)}, bf16[128,3072]{1,0:T(8,128)(2,1)}, u32[]{:S(2)}, u32[]{:S(2)}) collective-permute-start(bf16[128,3072]{1,0:T(8,128)(2,1)S(1)} %get-tuple-element.29), channel_id=1, source_target_pairs={{0,64},{32,96},{64,0},{96,32},{1,65},{33,97},{65,1},{97,33},{2,66}... | collective-permute-start | bytes 2359304 | tf_op jit(solution)/shard_map/tokens_x/ppermute | solution.py:209
  17.9 7.8 %collective-permute-start = (bf16[32,256]{1,0:T(8,128)(2,1)S(1)}, bf16[32,256]{1,0:T(8,128)(2,1)S(1)}, u32[]{:S(2)}, u32[]{:S(2)}) collective-permute-start(bf16[32,256]{1,0:T(8,128)(2,1)S(1)} %broadcast_select_fusion), channel_id=1, source_target_pairs={{0,1},{1,0},{2,3},{3,2},{4,5},{5,4},{6,7},{7,6},{8,9},{9,8},{10,11... | collective-permute-start | bytes 49160 | tf_op jit(solution)/shard_map/gather/cond/branch_1_fun/gather_core/ppermute | solution.py:215
  54.7 26.1 %collective-permute-start.4 = (bf16[512,3072]{1,0:T(8,128)(2,1)}, bf16[512,3072]{1,0:T(8,128)(2,1)}, u32[]{:S(2)}, u32[]{:S(2)}) collective-permute-start(bf16[512,3072]{1,0:T(8,128)(2,1)} %join.4.refs_1_.refs_0_), channel_id=1, source_target_pairs={{0,1},{1,0},{2,3},{3,2},{4,5},{5,4},{6,7},{7,6},{8,9},{9,8},{10,11... | collective-permute-start | bytes 9437192 | tf_op jit(solution)/shard_map/tokens_core/ppermute | solution.py:235
  87.1 37.2 %copy-start.5 = (f32[1,1024]{1,0:T(1,128)S(1)}, f32[1,1024]{1,0:T(1,128)}, u32[]{:S(2)}) copy-start(f32[1,1024]{1,0:T(1,128)} %first_hbm.1) | copy-start | bytes 12292
  87.1 37.2 %copy-start.6 = (f32[1,1024]{1,0:T(1,128)S(1)}, f32[1,1024]{1,0:T(1,128)}, u32[]{:S(2)}) copy-start(f32[1,1024]{1,0:T(1,128)} %second_hbm.1) | copy-start | bytes 12292
  87.1 73.5 %copy-start.7 = (s32[512]{0:T(512)S(1)}, s32[512]{0:T(512)}, u32[]{:S(2)}) copy-start(s32[512]{0:T(512)} %constant.43) | copy-start | bytes 6148
  152.4 9.7 %collective-permute-start.5 = (bf16[256,1024]{1,0:T(8,128)(2,1)S(1)}, bf16[256,1024]{1,0:T(8,128)(2,1)S(1)}, u32[]{:S(2)}, u32[]{:S(2)}) collective-permute-start(bf16[256,1024]{1,0:T(8,128)(2,1)S(1)} %bitcast.15), channel_id=1, source_target_pairs={{0,1},{1,0},{2,3},{3,2},{4,5},{5,4},{6,7},{7,6},{8,9},{9,8},{10,11... | collective-permute-start | bytes 1572872 | tf_op jit(solution)/shard_map/spread_core/ppermute | solution.py:251

commit v9 on v8

--- a/solution.py
+++ b/solution.py
@@ -86,7 +86,7 @@
         in_specs=[vmem] * len(pieces) + [pl.BlockSpec(memory_space=pl.ANY)],
         out_specs=vmem,
         out_shape=jax.ShapeDtypeStruct((rows * len(pieces), columns), jnp.bfloat16),
-        compiler_params=pltpu.CompilerParams(vmem_limit_bytes=56 * 2**20),
+        compiler_params=pltpu.CompilerParams(vmem_limit_bytes=16 * 2**20),
         cost_estimate=pl.CostEstimate(flops=0, bytes_accessed=2**20, transcendentals=0),
         name="join",
     )(*pieces, other)
@@ -122,7 +122,7 @@
         out_specs=vmem,
         out_shape=jax.ShapeDtypeStruct((256, KVW), jnp.float32),
         scratch_shapes=[pltpu.VMEM((2048, 256), jnp.bfloat16)],
-        compiler_params=pltpu.CompilerParams(vmem_limit_bytes=56 * 2**20),
+        compiler_params=pltpu.CompilerParams(vmem_limit_bytes=40 * 2**20),
         cost_estimate=pl.CostEstimate(
             flops=2 * 2**30, bytes_accessed=8 * 2**20, transcendentals=0
         ),
@@ -208,35 +208,28 @@
         pieces = [packed[0]] + [
             lax.ppermute(packed[k], "x", [(i, (i + k) % 4) for i in range(4)]) for k in (1, 3, 2)
         ]
-
-    def gather_z(rows):
+    def gather(rows):
         with jax.named_scope("gather_core"):
             low, high = rows[:, :256], rows[:, 256:]
             theirs = lax.ppermute(jnp.where(core_at == 0, high, low), "core", swap)
             chunk = jnp.where(core_at == (x_at & 1), jnp.where(core_at == 0, low, high), theirs)
         with jax.named_scope("gather_z"):
-            return spread(chunk, Z, 16).reshape(512, 256)
-
-    def gather_y(line):
+            line = spread(chunk, Z, 16).reshape(512, 256)
         with jax.named_scope("gather_y"):
             return spread(line, "y", 4).reshape(QUARTER, 256)
-
-    def in_order(step, block, out_rows):
-        return lax.cond(
-            x_at < 4, step, lambda block: jnp.zeros((out_rows, 256), jnp.bfloat16), block
-        )
 
     with jax.named_scope("gather"):
         rows = lax.dynamic_slice_in_dim(basis, (x_at >> 1) * 128 + z_lo_at * 32, 32, 0)
         rows = reorder(rows, by_core)
-        line = in_order(gather_z, join([rows], packed[1]), 512)
+        whole = lax.cond(
+            x_at < 4, gather, lambda rows: jnp.zeros((QUARTER, 256), jnp.bfloat16),
+            join([rows], packed[1]),
+        )
     with jax.named_scope("tokens_core"):
-        held = join(pieces, line)
-        other_held = lax.ppermute(held, "core", swap)
-    with jax.named_scope("gather"):
-        whole = in_order(gather_y, join([line], held), QUARTER)
+        held = join(pieces, whole)
+        held = [held, lax.ppermute(held, "core", swap)]
     with jax.named_scope("project"):
-        partial = project([held, other_held], whole)
+        partial = project(held, whole)
     with jax.named_scope("reduce_xy"):
         summed = jnp.sum(exchange(partial.reshape(16, 16, KVW), ("x", "y")), axis=0)
     with jax.named_scope("reduce_z"):

time: 164 us -> 160 us (0.976)
  Pallas kernels: 13.3 us -> 6.66 us
  waiting for transfers between devices: 1.95 us -> 7.21 us
  blocking collectives: 109 us -> 106 us
    ppermute x2, waiting for transfers between devices: 0.81 us -> 6.07 us  [the longest x1 5.26 us: local(): held = [held, lax.ppermute(held, 'core', swap)]]
    pallas_call x3 -> x2, Pallas kernels: 4.49 us -> 0.21 us  [join(): pl.pallas_call(join_kernel, in_specs=[vmem] * len(pieces) + [pl.BlockSpec...]
    pallas_call x1, Pallas kernels: 6.31 us -> 2.46 us  [project(): pl.pallas_call(project_kernel, in_specs=[vmem] * (len(pieces) + 1), out_s...]
    all_to_all x6, blocking collectives: 109 us -> 106 us  [exchange(): return lax.all_to_all(blocks, axes, 0, 0, tiled=True)]
    unnamed x18 -> x16, local copies, waits for them, and re-layouts: 3.52 us -> 2.63 us
  transfers between devices with their start and end apart: 6 -> 6, of which waited for: 2 -> 3; matrix products, arithmetic and copies ran while one was open for 1% -> 1% of each run, Pallas kernels for 0% -> 0%
where the time goes in v9:
time: 160 us; the launch traced here: 159 us
  blocking collectives  106 us (66%)
  starting transfers between devices  33.7 us (21%)
  waiting for transfers between devices  7.21 us (5%)
  Pallas kernels  6.66 us (4%)
  local copies, waits for them, and re-layouts  2.78 us (2%)
    all_to_all x6, blocking collectives, exchange(): return lax.all_to_all(blocks, axes, 0, 0, tiled=True)  106 us
    ppermute x3, starting transfers between devices, local(): lax.ppermute(packed[k], 'x', [(i, (i + k) % 4) for i in range(4)])  10.8 us
    ppermute x1, starting transfers between devices, local(): held = [held, lax.ppermute(held, 'core', swap)]  8.6 us
    ppermute x1, starting transfers between devices, local(): other = lax.ppermute(own, 'core', swap)  7.39 us
    ppermute x1, starting transfers between devices, gather(): theirs = lax.ppermute(jnp.where(core_at == 0, high, low), 'core', swap)  7 us
    ppermute x1, waiting for transfers between devices, local(): held = [held, lax.ppermute(held, 'core', swap)]  5.26 us
  transfers between devices with their start and end apart: 6, of which 3 were waited for; matrix products, arithmetic and copies ran while one was open for 1% of the time, Pallas kernels for 0%

profile of v9, /device:TPU:1, one launch (start us, length us, event | category | flops | bytes accessed | tf_op | source)
XLA Modules:
  0.0 159.1 jit_solution(10899136354142582086)
XLA Ops:
  0.7 1.6 %copy-done.1 = bf16[128,8192]{1,0:T(8,128)(2,1)S(1)} copy-done((bf16[128,8192]{1,0:T(8,128)(2,1)S(1)}, bf16[128,8192]{1,0:T(8,128)(2,1)}, u32[]{:S(2)}) %copy-start.1) | copy-done | bytes 2097176
  2.3 0.9 copy-done.2
  3.2 2.1 %pack.1 = (bf16[128,3072]{1,0:T(8,128)(2,1)S(1)}, bf16[128,3072]{1,0:T(8,128)(2,1)}, bf16[128,3072]{1,0:T(8,128)(2,1)}, bf16[128,3072]{1,0:T(8,128)(2,1)}) custom-call(s32[1]{0:T(128)} %bitcast.2.x_ref, bf16[128,8192]{1,0:T(8,128)(2,1)S(1)} %copy-done.1, bf16[128,1024]{1,0:T(8,128)(2,1)S(1)} %copy-done.2), custom_call_target="tpu_custom_call" | custom-call | bytes 6291456 | tf_op jit(solution)/shard_map/tokens_x/pack/pallas_call | solution.py:58
  5.3 3.9 %collective-permute-start.1 = (bf16[128,3072]{1,0:T(8,128)(2,1)}, bf16[128,3072]{1,0:T(8,128)(2,1)S(1)}, u32[]{:S(2)}, u32[]{:S(2)}) collective-permute-start(bf16[128,3072]{1,0:T(8,128)(2,1)} %get-tuple-element.23.refs_1_), channel_id=1, source_target_pairs={{0,32},{32,64},{64,96},{96,0},{1,33},{33,65},{65,97},{97,1},{2,34}... | collective-permute-start | bytes 2359304 | tf_op jit(solution)/shard_map/tokens_x/ppermute | solution.py:209
  9.3 3.2 %collective-permute-start.2 = (bf16[128,3072]{1,0:T(8,128)(2,1)}, bf16[128,3072]{1,0:T(8,128)(2,1)S(1)}, u32[]{:S(2)}, u32[]{:S(2)}) collective-permute-start(bf16[128,3072]{1,0:T(8,128)(2,1)} %get-tuple-element.24), channel_id=1, source_target_pairs={{0,96},{32,0},{64,32},{96,64},{1,97},{33,1},{65,33},{97,65},{2,98}... | collective-permute-start | bytes 2359304 | tf_op jit(solution)/shard_map/tokens_x/ppermute | solution.py:209
  12.5 3.6 %collective-permute-start.3 = (bf16[128,3072]{1,0:T(8,128)(2,1)}, bf16[128,3072]{1,0:T(8,128)(2,1)S(1)}, u32[]{:S(2)}, u32[]{:S(2)}) collective-permute-start(bf16[128,3072]{1,0:T(8,128)(2,1)} %get-tuple-element.25), channel_id=1, source_target_pairs={{0,64},{32,96},{64,0},{96,32},{1,65},{33,97},{65,1},{97,33},{2,66}... | collective-permute-start | bytes 2359304 | tf_op jit(solution)/shard_map/tokens_x/ppermute | solution.py:209
  16.1 1.0 convolution_convert_fusion.1.refs_0_
  17.1 47.0 %conditional.1 = (bf16[2048,256]{1,0:T(8,128)(2,1)}) conditional(s32[]{:T(128)} %convert_element_type.13, () %tuple.14, (s32[]{:T(128)}, s32[]{:T(128)}, bf16[32,512]{1,0:T(8,128)(2,1)S(1)}) %tuple.15), branch_computations={%region_0.0_spmd, %region_1.2_spmd} | conditional | flops 24579 | bytes 4390993 | solution.py:224
  17.1 7.0 %collective-permute-start = (bf16[32,256]{1,0:T(8,128)(2,1)S(1)}, bf16[32,256]{1,0:T(8,128)(2,1)S(1)}, u32[]{:S(2)}, u32[]{:S(2)}) collective-permute-start(bf16[32,256]{1,0:T(8,128)(2,1)S(1)} %broadcast_select_fusion), channel_id=1, source_target_pairs={{0,1},{1,0},{2,3},{3,2},{4,5},{5,4},{6,7},{7,6},{8,9},{9,8},{10,11... | collective-permute-start | bytes 49160 | tf_op jit(solution)/shard_map/gather/cond/branch_1_fun/gather_core/ppermute | solution.py:214
  24.2 0.8 collective-permute-done
  25.0 25.2 %all_to_all.28 = bf16[16,32,256]{2,1,0:T(8,128)(2,1)S(1)} all-to-all(bf16[16,32,256]{2,1,0:T(8,128)(2,1)S(1)} %broadcast_in_dim.7), channel_id=1, replica_groups=mesh['z_lo'=4,'x'=4,'y'=4,'z_hi'=4,'core'=2] {'z_hi','z_lo'}, dimensions={0} | all-to-all | bytes 524288 | tf_op jit(solution)/shard_map/gather/cond/branch_1_fun/gather_z/all_to_all | solution.py:38
  50.3 13.8 %all_to_all.29 = bf16[4,512,256]{2,1,0:T(8,128)(2,1)} all-to-all(bf16[4,512,256]{2,1,0:T(8,128)(2,1)S(1)} %broadcast_in_dim.17), channel_id=1, replica_groups=mesh['z_lo'=4,'x'=4,'y'=4,'z_hi'=4,'core'=2] {'y'}, dimensions={0} | all-to-all | bytes 2097152 | tf_op jit(solution)/shard_map/gather/cond/branch_1_fun/gather_y/all_to_all | solution.py:38
  64.3 8.6 %collective-permute-start.4 = (bf16[512,3072]{1,0:T(8,128)(2,1)S(1)}, bf16[512,3072]{1,0:T(8,128)(2,1)S(1)}, u32[]{:S(2)}, u32[]{:S(2)}) collective-permute-start(bf16[512,3072]{1,0:T(8,128)(2,1)S(1)} %join.3.refs_0_), channel_id=1, source_target_pairs={{0,1},{1,0},{2,3},{3,2},{4,5},{5,4},{6,7},{7,6},{8,9},{9,8},{10,11... | collective-permute-start | bytes 9437192 | tf_op jit(solution)/shard_map/tokens_core/ppermute | solution.py:230
  72.9 5.3 %collective-permute-done.4.refs_1_ = bf16[512,3072]{1,0:T(8,128)(2,1)S(1)} collective-permute-done((bf16[512,3072]{1,0:T(8,128)(2,1)S(1)}, bf16[512,3072]{1,0:T(8,128)(2,1)S(1)}, u32[]{:S(2)}, u32[]{:S(2)}) %collective-permute-start.4) | collective-permute-done | bytes 3145760 | tf_op jit(solution)/shard_map/tokens_core/ppermute | solution.py:230
  78.2 2.5 %project.1 = f32[256,1024]{1,0:T(8,128)S(1)} custom-call(bf16[512,3072]{1,0:T(8,128)(2,1)S(1)} %join.3.refs_0_, bf16[512,3072]{1,0:T(8,128)(2,1)S(1)} %collective-permute-done.4.refs_1_, bf16[2048,256]{1,0:T(8,128)(2,1)S(1)} %copy-done.5), custom_call_target="tpu_custom_call" | custom-call | flops 2147483648 | bytes 8388608 | tf_op jit(solution)/shard_map/project/project/pallas_call | solution.py:119
  80.7 19.3 %all_to_all.30 = f32[16,16,1024]{2,1,0:T(8,128)S(1)} all-to-all(f32[16,16,1024]{2,1,0:T(8,128)S(1)} %bitcast.15), channel_id=1, replica_groups=mesh['z_lo'=4,'x'=4,'y'=4,'z_hi'=4,'core'=2] {'x','y'}, dimensions={0} | all-to-all | bytes 2097152 | tf_op jit(solution)/shard_map/reduce_xy/all_to_all | solution.py:38
  100.1 21.4 %all_to_all.31.parts_ref = f32[16,8,128]{2,1,0:T(8,128)S(1)} all-to-all(f32[16,8,128]{2,1,0:T(8,128)S(1)} %bitcast.21), channel_id=1, replica_groups=mesh['z_lo'=4,'x'=4,'y'=4,'z_hi'=4,'core'=2] {'z_hi','z_lo'}, dimensions={0} | all-to-all | bytes 131072 | tf_op jit(solution)/shard_map/reduce_z/all_to_all | solution.py:38
  121.5 0.7 adam.1
  122.2 14.2 %all_to_all.32 = bf16[16,8,128]{2,1,0:T(8,128)(2,1)S(1)} all-to-all(bf16[16,8,128]{2,1,0:T(8,128)(2,1)S(1)} %broadcast_in_dim.34), channel_id=1, replica_groups=mesh['z_lo'=4,'x'=4,'y'=4,'z_hi'=4,'core'=2] {'z_hi','z_lo'}, dimensions={0} | all-to-all | bytes 65536 | tf_op jit(solution)/shard_map/spread_z/all_to_all | solution.py:38
  136.5 12.5 %all_to_all.33 = bf16[16,16,1024]{2,1,0:T(8,128)(2,1)S(1)} all-to-all(bf16[16,16,1024]{2,1,0:T(8,128)(2,1)S(1)} %broadcast_in_dim.36), channel_id=1, replica_groups=mesh['z_lo'=4,'x'=4,'y'=4,'z_hi'=4,'core'=2] {'x','y'}, dimensions={0} | all-to-all | bytes 1048576 | tf_op jit(solution)/shard_map/spread_xy/all_to_all | solution.py:38
  149.0 7.4 %collective-permute-start.5 = (bf16[256,1024]{1,0:T(8,128)(2,1)S(1)}, bf16[256,1024]{1,0:T(8,128)(2,1)S(1)}, u32[]{:S(2)}, u32[]{:S(2)}) collective-permute-start(bf16[256,1024]{1,0:T(8,128)(2,1)S(1)} %bitcast.16), channel_id=1, source_target_pairs={{0,1},{1,0},{2,3},{3,2},{4,5},{5,4},{6,7},{7,6},{8,9},{9,8},{10,11... | collective-permute-start | bytes 1572872 | tf_op jit(solution)/shard_map/spread_core/ppermute | solution.py:244
  156.4 0.4 fusion.basis_ref
  156.8 1.1 collective-permute-done.5.other_ref
  157.9 1.2 decode.1
  (26 shorter events, 0.5 us)
Async XLA Ops:
  0.6 15.5 %copy-start = (bf16[256,512]{1,0:T(8,128)(2,1)S(1)}, bf16[256,512]{1,0:T(8,128)(2,1)}, u32[]{:S(2)}) copy-start(bf16[256,512]{1,0:T(8,128)(2,1)} %param.11) | copy-start | bytes 786436
  0.7 1.6 %copy-start.1 = (bf16[128,8192]{1,0:T(8,128)(2,1)S(1)}, bf16[128,8192]{1,0:T(8,128)(2,1)}, u32[]{:S(2)}) copy-start(bf16[128,8192]{1,0:T(8,128)(2,1)} %tokens_ref.1) | copy-start | bytes 6291460
  2.3 0.9 copy-start.2
  5.3 58.8 %collective-permute-start.1 = (bf16[128,3072]{1,0:T(8,128)(2,1)}, bf16[128,3072]{1,0:T(8,128)(2,1)S(1)}, u32[]{:S(2)}, u32[]{:S(2)}) collective-permute-start(bf16[128,3072]{1,0:T(8,128)(2,1)} %get-tuple-element.23.refs_1_), channel_id=1, source_target_pairs={{0,32},{32,64},{64,96},{96,0},{1,33},{33,65},{65,97},{97,1},{2,34}... | collective-permute-start | bytes 2359304 | tf_op jit(solution)/shard_map/tokens_x/ppermute | solution.py:209
  9.3 54.8 %collective-permute-start.2 = (bf16[128,3072]{1,0:T(8,128)(2,1)}, bf16[128,3072]{1,0:T(8,128)(2,1)S(1)}, u32[]{:S(2)}, u32[]{:S(2)}) collective-permute-start(bf16[128,3072]{1,0:T(8,128)(2,1)} %get-tuple-element.24), channel_id=1, source_target_pairs={{0,96},{32,0},{64,32},{96,64},{1,97},{33,1},{65,33},{97,65},{2,98}... | collective-permute-start | bytes 2359304 | tf_op jit(solution)/shard_map/tokens_x/ppermute | solution.py:209
  12.5 51.6 %collective-permute-start.3 = (bf16[128,3072]{1,0:T(8,128)(2,1)}, bf16[128,3072]{1,0:T(8,128)(2,1)S(1)}, u32[]{:S(2)}, u32[]{:S(2)}) collective-permute-start(bf16[128,3072]{1,0:T(8,128)(2,1)} %get-tuple-element.25), channel_id=1, source_target_pairs={{0,64},{32,96},{64,0},{96,32},{1,65},{33,97},{65,1},{97,33},{2,66}... | collective-permute-start | bytes 2359304 | tf_op jit(solution)/shard_map/tokens_x/ppermute | solution.py:209
  17.1 7.8 %collective-permute-start = (bf16[32,256]{1,0:T(8,128)(2,1)S(1)}, bf16[32,256]{1,0:T(8,128)(2,1)S(1)}, u32[]{:S(2)}, u32[]{:S(2)}) collective-permute-start(bf16[32,256]{1,0:T(8,128)(2,1)S(1)} %broadcast_select_fusion), channel_id=1, source_target_pairs={{0,1},{1,0},{2,3},{3,2},{4,5},{5,4},{6,7},{7,6},{8,9},{9,8},{10,11... | collective-permute-start | bytes 49160 | tf_op jit(solution)/shard_map/gather/cond/branch_1_fun/gather_core/ppermute | solution.py:214
  64.1 14.1 %copy-start.5 = (bf16[2048,256]{1,0:T(8,128)(2,1)S(1)}, bf16[2048,256]{1,0:T(8,128)(2,1)}, u32[]{:S(2)}) copy-start(bf16[2048,256]{1,0:T(8,128)(2,1)} %get-tuple-element.29.refs_4_.refs_2_) | copy-start | bytes 3145732
  64.3 13.9 %collective-permute-start.4 = (bf16[512,3072]{1,0:T(8,128)(2,1)S(1)}, bf16[512,3072]{1,0:T(8,128)(2,1)S(1)}, u32[]{:S(2)}, u32[]{:S(2)}) collective-permute-start(bf16[512,3072]{1,0:T(8,128)(2,1)S(1)} %join.3.refs_0_), channel_id=1, source_target_pairs={{0,1},{1,0},{2,3},{3,2},{4,5},{5,4},{6,7},{7,6},{8,9},{9,8},{10,11... | collective-permute-start | bytes 9437192 | tf_op jit(solution)/shard_map/tokens_core/ppermute | solution.py:230
  80.7 40.8 %copy-start.3 = (f32[1,1024]{1,0:T(1,128)S(1)}, f32[1,1024]{1,0:T(1,128)}, u32[]{:S(2)}) copy-start(f32[1,1024]{1,0:T(1,128)} %first_hbm.1) | copy-start | bytes 12292
  80.7 40.8 %copy-start.4 = (f32[1,1024]{1,0:T(1,128)S(1)}, f32[1,1024]{1,0:T(1,128)}, u32[]{:S(2)}) copy-start(f32[1,1024]{1,0:T(1,128)} %second_hbm.1) | copy-start | bytes 12292
  80.7 75.7 %copy-start.6 = (s32[512]{0:T(512)S(1)}, s32[512]{0:T(512)}, u32[]{:S(2)}) copy-start(s32[512]{0:T(512)} %constant.41) | copy-start | bytes 6148
  149.0 8.9 %collective-permute-start.5 = (bf16[256,1024]{1,0:T(8,128)(2,1)S(1)}, bf16[256,1024]{1,0:T(8,128)(2,1)S(1)}, u32[]{:S(2)}, u32[]{:S(2)}) collective-permute-start(bf16[256,1024]{1,0:T(8,128)(2,1)S(1)} %bitcast.16), channel_id=1, source_target_pairs={{0,1},{1,0},{2,3},{3,2},{4,5},{5,4},{6,7},{7,6},{8,9},{9,8},{10,11... | collective-permute-start | bytes 1572872 | tf_op jit(solution)/shard_map/spread_core/ppermute | solution.py:244

commit v10 on v9

--- a/solution.py
+++ b/solution.py
@@ -93,7 +93,7 @@
 
 
 def project_kernel(*refs):
-    *pieces, whole_ref, out_ref, split_ref = refs
+    *pieces, whole_ref, out_ref, split_ref, sum_ref = refs
     whole = whole_ref[...]
     at, tokens = 0, split_ref.shape[0] // 2
     for piece in pieces:
@@ -106,12 +106,19 @@
         at += rows
     for n in range(0, KVW, 256):
         columns = [piece[:, QUARTER + n : QUARTER + n + 256] for piece in pieces]
-        out_ref[:, n : n + 256] = lax.dot_general(
+        sum_ref[:, n : n + 256] = lax.dot_general(
             split_ref[...],
             jnp.concatenate(columns + columns, axis=0),
             (((0,), (0,)), ((), ())),
             preferred_element_type=jnp.float32,
         )
+    top = jnp.max(jnp.abs(sum_ref[...]), axis=1, keepdims=True)
+    exponent = jnp.ceil(jnp.log2(jnp.maximum(top, 1e-36))) + 1.0
+    exponent = jnp.broadcast_to(exponent, (256, 128))
+    scale = jnp.exp2(-exponent)
+    out_ref[:, 8] = exponent.reshape(16, 16, 128)
+    for n in range(8):
+        out_ref[:, n] = (sum_ref[:, n * 128 : n * 128 + 128] * scale).reshape(16, 16, 128)
 
 
 def project(pieces, whole):
@@ -120,8 +127,11 @@
         project_kernel,
         in_specs=[vmem] * (len(pieces) + 1),
         out_specs=vmem,
-        out_shape=jax.ShapeDtypeStruct((256, KVW), jnp.float32),
-        scratch_shapes=[pltpu.VMEM((2048, 256), jnp.bfloat16)],
+        out_shape=jax.ShapeDtypeStruct((16, 9, 16, 128), jnp.float32),
+        scratch_shapes=[
+            pltpu.VMEM((2048, 256), jnp.bfloat16),
+            pltpu.VMEM((256, KVW), jnp.float32),
+        ],
         compiler_params=pltpu.CompilerParams(vmem_limit_bytes=40 * 2**20),
         cost_estimate=pl.CostEstimate(
             flops=2 * 2**30, bytes_accessed=8 * 2**20, transcendentals=0
@@ -231,9 +241,10 @@
     with jax.named_scope("project"):
         partial = project(held, whole)
     with jax.named_scope("reduce_xy"):
-        summed = jnp.sum(exchange(partial.reshape(16, 16, KVW), ("x", "y")), axis=0)
+        parts = exchange(partial.astype(jnp.float16), ("x", "y")).astype(jnp.float32)
+        summed = jnp.sum(parts[:, :8] * jnp.exp2(parts[:, 8:]), axis=0).transpose(1, 0, 2)
     with jax.named_scope("reduce_z"):
-        parts = exchange(summed.reshape(16, 8, 128), Z)
+        parts = exchange(summed, Z)
     with jax.named_scope("adam"):
         new_first, new_second, normalized = adam(parts, first_moment, second_moment)
     with jax.named_scope("spread_z"):

time: 160 us -> 154 us (0.963)
  blocking collectives: 106 us -> 101 us
    all_to_all x6, blocking collectives: 106 us -> 101 us  [exchange(): return lax.all_to_all(blocks, axes, 0, 0, tiled=True)]
  transfers between devices with their start and end apart: 6 -> 6, of which waited for: 3 -> 3; matrix products, arithmetic and copies ran while one was open for 1% -> 0% of each run, Pallas kernels for 0% -> 0%
where the time goes in v10:
time: 154 us
  blocking collectives  101 us (66%)
  starting transfers between devices  33.7 us (22%)
  waiting for transfers between devices  7.22 us (5%)
  Pallas kernels  6.76 us (4%)
  local copies, waits for them, and re-layouts  2.78 us (2%)
    all_to_all x6, blocking collectives, exchange(): return lax.all_to_all(blocks, axes, 0, 0, tiled=True)  101 us
    ppermute x3, starting transfers between devices, local(): lax.ppermute(packed[k], 'x', [(i, (i + k) % 4) for i in range(4)])  10.8 us
    ppermute x1, starting transfers between devices, local(): held = [held, lax.ppermute(held, 'core', swap)]  8.6 us
    ppermute x1, starting transfers between devices, local(): other = lax.ppermute(own, 'core', swap)  7.39 us
    ppermute x1, starting transfers between devices, gather(): theirs = lax.ppermute(jnp.where(core_at == 0, high, low), 'core', swap)  7 us
    ppermute x1, waiting for transfers between devices, local(): held = [held, lax.ppermute(held, 'core', swap)]  5.26 us
  transfers between devices with their start and end apart: 6, of which 3 were waited for; matrix products, arithmetic and copies ran while one was open for 0% of the time, Pallas kernels for 0%

profile of v10, /device:TPU:1, one launch (start us, length us, event | category | flops | bytes accessed | tf_op | source)
XLA Modules:
  0.0 153.7 jit_solution(5006554152253274608)
XLA Ops:
  0.7 1.6 %copy-done.1 = bf16[128,8192]{1,0:T(8,128)(2,1)S(1)} copy-done((bf16[128,8192]{1,0:T(8,128)(2,1)S(1)}, bf16[128,8192]{1,0:T(8,128)(2,1)}, u32[]{:S(2)}) %copy-start.1) | copy-done | bytes 2097176
  2.3 0.9 copy-done.2
  3.2 2.1 %pack.1 = (bf16[128,3072]{1,0:T(8,128)(2,1)S(1)}, bf16[128,3072]{1,0:T(8,128)(2,1)}, bf16[128,3072]{1,0:T(8,128)(2,1)}, bf16[128,3072]{1,0:T(8,128)(2,1)}) custom-call(s32[1]{0:T(128)} %bitcast.2.x_ref, bf16[128,8192]{1,0:T(8,128)(2,1)S(1)} %copy-done.1, bf16[128,1024]{1,0:T(8,128)(2,1)S(1)} %copy-done.2), custom_call_target="tpu_custom_call" | custom-call | bytes 6291456 | tf_op jit(solution)/shard_map/tokens_x/pack/pallas_call | solution.py:58
  5.3 3.9 %collective-permute-start.1 = (bf16[128,3072]{1,0:T(8,128)(2,1)}, bf16[128,3072]{1,0:T(8,128)(2,1)S(1)}, u32[]{:S(2)}, u32[]{:S(2)}) collective-permute-start(bf16[128,3072]{1,0:T(8,128)(2,1)} %get-tuple-element.23.refs_1_), channel_id=1, source_target_pairs={{0,32},{32,64},{64,96},{96,0},{1,33},{33,65},{65,97},{97,1},{2,34}... | collective-permute-start | bytes 2359304 | tf_op jit(solution)/shard_map/tokens_x/ppermute | solution.py:219
  9.3 3.2 %collective-permute-start.2 = (bf16[128,3072]{1,0:T(8,128)(2,1)}, bf16[128,3072]{1,0:T(8,128)(2,1)S(1)}, u32[]{:S(2)}, u32[]{:S(2)}) collective-permute-start(bf16[128,3072]{1,0:T(8,128)(2,1)} %get-tuple-element.24), channel_id=1, source_target_pairs={{0,96},{32,0},{64,32},{96,64},{1,97},{33,1},{65,33},{97,65},{2,98}... | collective-permute-start | bytes 2359304 | tf_op jit(solution)/shard_map/tokens_x/ppermute | solution.py:219
  12.5 3.6 %collective-permute-start.3 = (bf16[128,3072]{1,0:T(8,128)(2,1)}, bf16[128,3072]{1,0:T(8,128)(2,1)S(1)}, u32[]{:S(2)}, u32[]{:S(2)}) collective-permute-start(bf16[128,3072]{1,0:T(8,128)(2,1)} %get-tuple-element.25), channel_id=1, source_target_pairs={{0,64},{32,96},{64,0},{96,32},{1,65},{33,97},{65,1},{97,33},{2,66}... | collective-permute-start | bytes 2359304 | tf_op jit(solution)/shard_map/tokens_x/ppermute | solution.py:219
  16.1 0.3 convolution_convert_fusion.1.refs_0_
  16.4 47.0 %conditional.1 = (bf16[2048,256]{1,0:T(8,128)(2,1)}) conditional(s32[]{:T(128)} %convert_element_type.19, () %tuple.14, (s32[]{:T(128)}, s32[]{:T(128)}, bf16[32,512]{1,0:T(8,128)(2,1)S(1)}) %tuple.15), branch_computations={%region_0.0_spmd, %region_1.2_spmd} | conditional | flops 24579 | bytes 4390993 | solution.py:234
  16.5 7.0 %collective-permute-start = (bf16[32,256]{1,0:T(8,128)(2,1)S(1)}, bf16[32,256]{1,0:T(8,128)(2,1)S(1)}, u32[]{:S(2)}, u32[]{:S(2)}) collective-permute-start(bf16[32,256]{1,0:T(8,128)(2,1)S(1)} %broadcast_select_fusion), channel_id=1, source_target_pairs={{0,1},{1,0},{2,3},{3,2},{4,5},{5,4},{6,7},{7,6},{8,9},{9,8},{10,11... | collective-permute-start | bytes 49160 | tf_op jit(solution)/shard_map/gather/cond/branch_1_fun/gather_core/ppermute | solution.py:224
  23.5 0.8 collective-permute-done
  24.3 25.2 %all_to_all.28 = bf16[16,32,256]{2,1,0:T(8,128)(2,1)S(1)} all-to-all(bf16[16,32,256]{2,1,0:T(8,128)(2,1)S(1)} %broadcast_in_dim.7), channel_id=1, replica_groups=mesh['z_lo'=4,'x'=4,'y'=4,'z_hi'=4,'core'=2] {'z_hi','z_lo'}, dimensions={0} | all-to-all | bytes 524288 | tf_op jit(solution)/shard_map/gather/cond/branch_1_fun/gather_z/all_to_all | solution.py:38
  49.6 13.8 %all_to_all.29 = bf16[4,512,256]{2,1,0:T(8,128)(2,1)} all-to-all(bf16[4,512,256]{2,1,0:T(8,128)(2,1)S(1)} %broadcast_in_dim.17), channel_id=1, replica_groups=mesh['z_lo'=4,'x'=4,'y'=4,'z_hi'=4,'core'=2] {'y'}, dimensions={0} | all-to-all | bytes 2097152 | tf_op jit(solution)/shard_map/gather/cond/branch_1_fun/gather_y/all_to_all | solution.py:38
  63.7 8.6 %collective-permute-start.4 = (bf16[512,3072]{1,0:T(8,128)(2,1)S(1)}, bf16[512,3072]{1,0:T(8,128)(2,1)S(1)}, u32[]{:S(2)}, u32[]{:S(2)}) collective-permute-start(bf16[512,3072]{1,0:T(8,128)(2,1)S(1)} %join.3.refs_0_), channel_id=1, source_target_pairs={{0,1},{1,0},{2,3},{3,2},{4,5},{5,4},{6,7},{7,6},{8,9},{9,8},{10,11... | collective-permute-start | bytes 9437192 | tf_op jit(solution)/shard_map/tokens_core/ppermute | solution.py:240
  72.3 5.3 %collective-permute-done.4.refs_1_ = bf16[512,3072]{1,0:T(8,128)(2,1)S(1)} collective-permute-done((bf16[512,3072]{1,0:T(8,128)(2,1)S(1)}, bf16[512,3072]{1,0:T(8,128)(2,1)S(1)}, u32[]{:S(2)}, u32[]{:S(2)}) %collective-permute-start.4) | collective-permute-done | bytes 3145760 | tf_op jit(solution)/shard_map/tokens_core/ppermute | solution.py:240
  77.5 2.6 %project.1 = f32[16,9,16,128]{3,2,1,0:T(8,128)S(1)} custom-call(bf16[512,3072]{1,0:T(8,128)(2,1)S(1)} %join.3.refs_0_, bf16[512,3072]{1,0:T(8,128)(2,1)S(1)} %collective-permute-done.4.refs_1_, bf16[2048,256]{1,0:T(8,128)(2,1)S(1)} %copy-done.5), custom_call_target="tpu_custom_call" | custom-call | flops 2147483648 | bytes 8388608 | tf_op jit(solution)/shard_map/project/project/pallas_call | solution.py:126
  80.2 14.7 %all_to_all.30 = f16[16,9,16,128]{3,2,1,0:T(8,128)(2,1)S(1)} all-to-all(f16[16,9,16,128]{3,2,1,0:T(8,128)(2,1)S(1)} %convert_element_type.21), channel_id=1, replica_groups=mesh['z_lo'=4,'x'=4,'y'=4,'z_hi'=4,'core'=2] {'x','y'}, dimensions={0} | all-to-all | bytes 1179648 | tf_op jit(solution)/shard_map/reduce_xy/all_to_all | solution.py:38
  95.2 21.3 %all_to_all.31.parts_ref = f32[16,8,128]{2,1,0:T(8,128)S(1)} all-to-all(f32[16,8,128]{2,1,0:T(8,128)S(1)} %bitcast.21), channel_id=1, replica_groups=mesh['z_lo'=4,'x'=4,'y'=4,'z_hi'=4,'core'=2] {'z_hi','z_lo'}, dimensions={0} | all-to-all | bytes 131072 | tf_op jit(solution)/shard_map/reduce_z/all_to_all | solution.py:38
  116.5 0.7 adam.1
  117.2 14.3 %all_to_all.32 = bf16[16,8,128]{2,1,0:T(8,128)(2,1)S(1)} all-to-all(bf16[16,8,128]{2,1,0:T(8,128)(2,1)S(1)} %broadcast_in_dim.34), channel_id=1, replica_groups=mesh['z_lo'=4,'x'=4,'y'=4,'z_hi'=4,'core'=2] {'z_hi','z_lo'}, dimensions={0} | all-to-all | bytes 65536 | tf_op jit(solution)/shard_map/spread_z/all_to_all | solution.py:38
  131.5 12.1 %all_to_all.33 = bf16[16,16,1024]{2,1,0:T(8,128)(2,1)S(1)} all-to-all(bf16[16,16,1024]{2,1,0:T(8,128)(2,1)S(1)} %broadcast_in_dim.36), channel_id=1, replica_groups=mesh['z_lo'=4,'x'=4,'y'=4,'z_hi'=4,'core'=2] {'x','y'}, dimensions={0} | all-to-all | bytes 1048576 | tf_op jit(solution)/shard_map/spread_xy/all_to_all | solution.py:38
  143.6 7.4 %collective-permute-start.5 = (bf16[256,1024]{1,0:T(8,128)(2,1)S(1)}, bf16[256,1024]{1,0:T(8,128)(2,1)S(1)}, u32[]{:S(2)}, u32[]{:S(2)}) collective-permute-start(bf16[256,1024]{1,0:T(8,128)(2,1)S(1)} %bitcast.17), channel_id=1, source_target_pairs={{0,1},{1,0},{2,3},{3,2},{4,5},{5,4},{6,7},{7,6},{8,9},{9,8},{10,11... | collective-permute-start | bytes 1572872 | tf_op jit(solution)/shard_map/spread_core/ppermute | solution.py:255
  151.0 0.4 fusion.basis_ref
  151.4 1.1 collective-permute-done.5.other_ref
  152.5 1.2 decode.1
  (29 shorter events, 0.7 us)
Async XLA Ops:
  0.6 15.5 %copy-start = (bf16[256,512]{1,0:T(8,128)(2,1)S(1)}, bf16[256,512]{1,0:T(8,128)(2,1)}, u32[]{:S(2)}) copy-start(bf16[256,512]{1,0:T(8,128)(2,1)} %param.11) | copy-start | bytes 786436
  0.7 1.6 %copy-start.1 = (bf16[128,8192]{1,0:T(8,128)(2,1)S(1)}, bf16[128,8192]{1,0:T(8,128)(2,1)}, u32[]{:S(2)}) copy-start(bf16[128,8192]{1,0:T(8,128)(2,1)} %tokens_ref.1) | copy-start | bytes 6291460
  2.3 0.9 copy-start.2
  3.2 12.9 %copy-start.6 = (s32[512]{0:T(512)S(1)}, s32[512]{0:T(512)}, u32[]{:S(2)}) copy-start(s32[512]{0:T(512)} %constant.43) | copy-start | bytes 6148
  5.3 58.1 %collective-permute-start.1 = (bf16[128,3072]{1,0:T(8,128)(2,1)}, bf16[128,3072]{1,0:T(8,128)(2,1)S(1)}, u32[]{:S(2)}, u32[]{:S(2)}) collective-permute-start(bf16[128,3072]{1,0:T(8,128)(2,1)} %get-tuple-element.23.refs_1_), channel_id=1, source_target_pairs={{0,32},{32,64},{64,96},{96,0},{1,33},{33,65},{65,97},{97,1},{2,34}... | collective-permute-start | bytes 2359304 | tf_op jit(solution)/shard_map/tokens_x/ppermute | solution.py:219
  9.3 54.1 %collective-permute-start.2 = (bf16[128,3072]{1,0:T(8,128)(2,1)}, bf16[128,3072]{1,0:T(8,128)(2,1)S(1)}, u32[]{:S(2)}, u32[]{:S(2)}) collective-permute-start(bf16[128,3072]{1,0:T(8,128)(2,1)} %get-tuple-element.24), channel_id=1, source_target_pairs={{0,96},{32,0},{64,32},{96,64},{1,97},{33,1},{65,33},{97,65},{2,98}... | collective-permute-start | bytes 2359304 | tf_op jit(solution)/shard_map/tokens_x/ppermute | solution.py:219
  12.5 50.9 %collective-permute-start.3 = (bf16[128,3072]{1,0:T(8,128)(2,1)}, bf16[128,3072]{1,0:T(8,128)(2,1)S(1)}, u32[]{:S(2)}, u32[]{:S(2)}) collective-permute-start(bf16[128,3072]{1,0:T(8,128)(2,1)} %get-tuple-element.25), channel_id=1, source_target_pairs={{0,64},{32,96},{64,0},{96,32},{1,65},{33,97},{65,1},{97,33},{2,66}... | collective-permute-start | bytes 2359304 | tf_op jit(solution)/shard_map/tokens_x/ppermute | solution.py:219
  16.5 7.8 %collective-permute-start = (bf16[32,256]{1,0:T(8,128)(2,1)S(1)}, bf16[32,256]{1,0:T(8,128)(2,1)S(1)}, u32[]{:S(2)}, u32[]{:S(2)}) collective-permute-start(bf16[32,256]{1,0:T(8,128)(2,1)S(1)} %broadcast_select_fusion), channel_id=1, source_target_pairs={{0,1},{1,0},{2,3},{3,2},{4,5},{5,4},{6,7},{7,6},{8,9},{9,8},{10,11... | collective-permute-start | bytes 49160 | tf_op jit(solution)/shard_map/gather/cond/branch_1_fun/gather_core/ppermute | solution.py:224
  63.4 14.1 %copy-start.5 = (bf16[2048,256]{1,0:T(8,128)(2,1)S(1)}, bf16[2048,256]{1,0:T(8,128)(2,1)}, u32[]{:S(2)}) copy-start(bf16[2048,256]{1,0:T(8,128)(2,1)} %get-tuple-element.29.refs_4_.refs_2_) | copy-start | bytes 3145732
  63.7 13.9 %collective-permute-start.4 = (bf16[512,3072]{1,0:T(8,128)(2,1)S(1)}, bf16[512,3072]{1,0:T(8,128)(2,1)S(1)}, u32[]{:S(2)}, u32[]{:S(2)}) collective-permute-start(bf16[512,3072]{1,0:T(8,128)(2,1)S(1)} %join.3.refs_0_), channel_id=1, source_target_pairs={{0,1},{1,0},{2,3},{3,2},{4,5},{5,4},{6,7},{7,6},{8,9},{9,8},{10,11... | collective-permute-start | bytes 9437192 | tf_op jit(solution)/shard_map/tokens_core/ppermute | solution.py:240
  95.0 21.5 %copy-start.3 = (f32[1,1024]{1,0:T(1,128)S(1)}, f32[1,1024]{1,0:T(1,128)}, u32[]{:S(2)}) copy-start(f32[1,1024]{1,0:T(1,128)} %first_hbm.1) | copy-start | bytes 12292
  95.0 21.5 %copy-start.4 = (f32[1,1024]{1,0:T(1,128)S(1)}, f32[1,1024]{1,0:T(1,128)}, u32[]{:S(2)}) copy-start(f32[1,1024]{1,0:T(1,128)} %second_hbm.1) | copy-start | bytes 12292
  143.6 8.9 %collective-permute-start.5 = (bf16[256,1024]{1,0:T(8,128)(2,1)S(1)}, bf16[256,1024]{1,0:T(8,128)(2,1)S(1)}, u32[]{:S(2)}, u32[]{:S(2)}) collective-permute-start(bf16[256,1024]{1,0:T(8,128)(2,1)S(1)} %bitcast.17), channel_id=1, source_target_pairs={{0,1},{1,0},{2,3},{3,2},{4,5},{5,4},{6,7},{7,6},{8,9},{9,8},{10,11... | collective-permute-start | bytes 1572872 | tf_op jit(solution)/shard_map/spread_core/ppermute | solution.py:255

commit v11 on v10

--- a/solution.py
+++ b/solution.py
@@ -224,19 +224,19 @@
             theirs = lax.ppermute(jnp.where(core_at == 0, high, low), "core", swap)
             chunk = jnp.where(core_at == (x_at & 1), jnp.where(core_at == 0, low, high), theirs)
         with jax.named_scope("gather_z"):
-            line = spread(chunk, Z, 16).reshape(512, 256)
-        with jax.named_scope("gather_y"):
-            return spread(line, "y", 4).reshape(QUARTER, 256)
+            return spread(chunk, Z, 16).reshape(512, 256)
 
     with jax.named_scope("gather"):
         rows = lax.dynamic_slice_in_dim(basis, (x_at >> 1) * 128 + z_lo_at * 32, 32, 0)
         rows = reorder(rows, by_core)
-        whole = lax.cond(
-            x_at < 4, gather, lambda rows: jnp.zeros((QUARTER, 256), jnp.bfloat16),
+        line = lax.cond(
+            x_at < 4, gather, lambda rows: jnp.zeros((512, 256), jnp.bfloat16),
             join([rows], packed[1]),
         )
+    with jax.named_scope("gather_y"):
+        whole = spread(line, "y", 4).reshape(QUARTER, 256)
     with jax.named_scope("tokens_core"):
-        held = join(pieces, whole)
+        held = join(pieces, line)
         held = [held, lax.ppermute(held, "core", swap)]
     with jax.named_scope("project"):
         partial = project(held, whole)

time: 154 us -> 152 us (0.987)
  waiting for transfers between devices: 7.22 us -> 1.96 us
  blocking collectives: 101 us -> 105 us
    ppermute x1, waiting for transfers between devices: 5.26 us -> 0.01 us  [local(): held = [held, lax.ppermute(held, 'core', swap)]]
    all_to_all x6, blocking collectives: 101 us -> 105 us  [exchange(): return lax.all_to_all(blocks, axes, 0, 0, tiled=True)]
    ppermute x1, starting transfers between devices: 8.6 us -> 7.04 us  [local(): held = [held, lax.ppermute(held, 'core', swap)]]
  transfers between devices with their start and end apart: 6 -> 6, of which waited for: 3 -> 2; matrix products, arithmetic and copies ran while one was open for 0% -> 1% of each run, Pallas kernels for 0% -> 0%
where the time goes in v11:
time: 152 us
  blocking collectives  105 us (69%)
  starting transfers between devices  33 us (22%)
  Pallas kernels  6.73 us (4%)
  local copies, waits for them, and re-layouts  2.79 us (2%)
  waiting for transfers between devices  1.96 us (1%)
    all_to_all x6, blocking collectives, exchange(): return lax.all_to_all(blocks, axes, 0, 0, tiled=True)  105 us
    ppermute x3, starting transfers between devices, local(): lax.ppermute(packed[k], 'x', [(i, (i + k) % 4) for i in range(4)])  10.8 us
    ppermute x1, starting transfers between devices, local(): other = lax.ppermute(own, 'core', swap)  8.2 us
    ppermute x1, starting transfers between devices, local(): held = [held, lax.ppermute(held, 'core', swap)]  7.04 us
    ppermute x1, starting transfers between devices, gather(): theirs = lax.ppermute(jnp.where(core_at == 0, high, low), 'core', swap)  7 us
  transfers between devices with their start and end apart: 6, of which 2 were waited for; matrix products, arithmetic and copies ran while one was open for 1% of the time, Pallas kernels for 0%

profile of v11, /device:TPU:1, one launch (start us, length us, event | category | flops | bytes accessed | tf_op | source)
XLA Modules:
  0.0 151.8 jit_solution(1589915212719511642)
XLA Ops:
  0.7 1.6 %copy-done.1 = bf16[128,8192]{1,0:T(8,128)(2,1)S(1)} copy-done((bf16[128,8192]{1,0:T(8,128)(2,1)S(1)}, bf16[128,8192]{1,0:T(8,128)(2,1)}, u32[]{:S(2)}) %copy-start.1) | copy-done | bytes 2097176
  2.3 0.9 copy-done.2
  3.2 2.1 %pack.1 = (bf16[128,3072]{1,0:T(8,128)(2,1)S(1)}, bf16[128,3072]{1,0:T(8,128)(2,1)}, bf16[128,3072]{1,0:T(8,128)(2,1)}, bf16[128,3072]{1,0:T(8,128)(2,1)}) custom-call(s32[1]{0:T(128)} %bitcast.1.x_ref, bf16[128,8192]{1,0:T(8,128)(2,1)S(1)} %copy-done.1, bf16[128,1024]{1,0:T(8,128)(2,1)S(1)} %copy-done.2), custom_call_target="tpu_custom_call" | custom-call | bytes 6291456 | tf_op jit(solution)/shard_map/tokens_x/pack/pallas_call | solution.py:58
  5.3 3.9 %collective-permute-start.1 = (bf16[128,3072]{1,0:T(8,128)(2,1)}, bf16[128,3072]{1,0:T(8,128)(2,1)S(1)}, u32[]{:S(2)}, u32[]{:S(2)}) collective-permute-start(bf16[128,3072]{1,0:T(8,128)(2,1)} %get-tuple-element.23.refs_1_), channel_id=1, source_target_pairs={{0,32},{32,64},{64,96},{96,0},{1,33},{33,65},{65,97},{97,1},{2,34}... | collective-permute-start | bytes 2359304 | tf_op jit(solution)/shard_map/tokens_x/ppermute | solution.py:219
  9.3 3.2 %collective-permute-start.2 = (bf16[128,3072]{1,0:T(8,128)(2,1)}, bf16[128,3072]{1,0:T(8,128)(2,1)S(1)}, u32[]{:S(2)}, u32[]{:S(2)}) collective-permute-start(bf16[128,3072]{1,0:T(8,128)(2,1)} %get-tuple-element.24), channel_id=1, source_target_pairs={{0,96},{32,0},{64,32},{96,64},{1,97},{33,1},{65,33},{97,65},{2,98}... | collective-permute-start | bytes 2359304 | tf_op jit(solution)/shard_map/tokens_x/ppermute | solution.py:219
  12.5 3.6 %collective-permute-start.3 = (bf16[128,3072]{1,0:T(8,128)(2,1)}, bf16[128,3072]{1,0:T(8,128)(2,1)S(1)}, u32[]{:S(2)}, u32[]{:S(2)}) collective-permute-start(bf16[128,3072]{1,0:T(8,128)(2,1)} %get-tuple-element.25), channel_id=1, source_target_pairs={{0,64},{32,96},{64,0},{96,32},{1,65},{33,97},{65,1},{97,33},{2,66}... | collective-permute-start | bytes 2359304 | tf_op jit(solution)/shard_map/tokens_x/ppermute | solution.py:219
  16.1 0.3 convolution_convert_fusion.1.refs_0_
  16.4 33.2 %conditional.1 = (bf16[512,256]{1,0:T(8,128)(2,1)}) conditional(s32[]{:T(128)} %convert_element_type.19, () %tuple.14, (s32[]{:T(128)}, s32[]{:T(128)}, bf16[32,512]{1,0:T(8,128)(2,1)S(1)}) %tuple.15), branch_computations={%region_0.0_spmd, %region_1.2_spmd} | conditional | flops 24579 | bytes 983121 | solution.py:232
  16.4 7.0 %collective-permute-start = (bf16[32,256]{1,0:T(8,128)(2,1)S(1)}, bf16[32,256]{1,0:T(8,128)(2,1)S(1)}, u32[]{:S(2)}, u32[]{:S(2)}) collective-permute-start(bf16[32,256]{1,0:T(8,128)(2,1)S(1)} %broadcast_select_fusion), channel_id=1, source_target_pairs={{0,1},{1,0},{2,3},{3,2},{4,5},{5,4},{6,7},{7,6},{8,9},{9,8},{10,11... | collective-permute-start | bytes 49160 | tf_op jit(solution)/shard_map/gather/cond/branch_1_fun/gather_core/ppermute | solution.py:224
  23.5 0.8 collective-permute-done
  24.3 25.3 %all_to_all.29 = bf16[16,32,256]{2,1,0:T(8,128)(2,1)} all-to-all(bf16[16,32,256]{2,1,0:T(8,128)(2,1)S(1)} %broadcast_in_dim.1), channel_id=1, replica_groups=mesh['z_lo'=4,'x'=4,'y'=4,'z_hi'=4,'core'=2] {'z_hi','z_lo'}, dimensions={0} | all-to-all | bytes 524288 | tf_op jit(solution)/shard_map/gather/cond/branch_1_fun/gather_z/all_to_all | solution.py:38
  49.6 0.2 join.3.refs_0_
  49.8 7.0 %collective-permute-start.4 = (bf16[512,3072]{1,0:T(8,128)(2,1)S(1)}, bf16[512,3072]{1,0:T(8,128)(2,1)S(1)}, u32[]{:S(2)}, u32[]{:S(2)}) collective-permute-start(bf16[512,3072]{1,0:T(8,128)(2,1)S(1)} %join.3.refs_0_), channel_id=1, source_target_pairs={{0,1},{1,0},{2,3},{3,2},{4,5},{5,4},{6,7},{7,6},{8,9},{9,8},{10,11... | collective-permute-start | bytes 9437192 | tf_op jit(solution)/shard_map/tokens_core/ppermute | solution.py:240
  57.0 18.9 %all_to_all.30 = bf16[4,512,256]{2,1,0:T(8,128)(2,1)S(1)} all-to-all(bf16[4,512,256]{2,1,0:T(8,128)(2,1)S(1)} %broadcast_in_dim.19), channel_id=1, replica_groups=mesh['z_lo'=4,'x'=4,'y'=4,'z_hi'=4,'core'=2] {'y'}, dimensions={0} | all-to-all | bytes 2097152 | tf_op jit(solution)/shard_map/gather_y/all_to_all | solution.py:38
  75.9 2.6 %project.1 = f32[16,9,16,128]{3,2,1,0:T(8,128)S(1)} custom-call(bf16[512,3072]{1,0:T(8,128)(2,1)S(1)} %join.3.refs_0_, bf16[512,3072]{1,0:T(8,128)(2,1)S(1)} %collective-permute-done.4.refs_1_, bf16[2048,256]{1,0:T(8,128)(2,1)S(1)} %bitcast.17), custom_call_target="tpu_custom_call" | custom-call | flops 2147483648 | bytes 8388608 | tf_op jit(solution)/shard_map/project/project/pallas_call | solution.py:126
  78.5 13.8 %all_to_all.31 = f16[16,9,16,128]{3,2,1,0:T(8,128)(2,1)S(1)} all-to-all(f16[16,9,16,128]{3,2,1,0:T(8,128)(2,1)S(1)} %convert_element_type.21), channel_id=1, replica_groups=mesh['z_lo'=4,'x'=4,'y'=4,'z_hi'=4,'core'=2] {'x','y'}, dimensions={0} | all-to-all | bytes 1179648 | tf_op jit(solution)/shard_map/reduce_xy/all_to_all | solution.py:38
  92.6 21.0 %all_to_all.32.parts_ref = f32[16,8,128]{2,1,0:T(8,128)S(1)} all-to-all(f32[16,8,128]{2,1,0:T(8,128)S(1)} %bitcast.21), channel_id=1, replica_groups=mesh['z_lo'=4,'x'=4,'y'=4,'z_hi'=4,'core'=2] {'z_hi','z_lo'}, dimensions={0} | all-to-all | bytes 131072 | tf_op jit(solution)/shard_map/reduce_z/all_to_all | solution.py:38
  113.6 0.7 adam.1
  114.2 14.3 %all_to_all.33 = bf16[16,8,128]{2,1,0:T(8,128)(2,1)S(1)} all-to-all(bf16[16,8,128]{2,1,0:T(8,128)(2,1)S(1)} %broadcast_in_dim.34), channel_id=1, replica_groups=mesh['z_lo'=4,'x'=4,'y'=4,'z_hi'=4,'core'=2] {'z_hi','z_lo'}, dimensions={0} | all-to-all | bytes 65536 | tf_op jit(solution)/shard_map/spread_z/all_to_all | solution.py:38
  128.6 12.2 %all_to_all.34 = bf16[16,16,1024]{2,1,0:T(8,128)(2,1)S(1)} all-to-all(bf16[16,16,1024]{2,1,0:T(8,128)(2,1)S(1)} %broadcast_in_dim.36), channel_id=1, replica_groups=mesh['z_lo'=4,'x'=4,'y'=4,'z_hi'=4,'core'=2] {'x','y'}, dimensions={0} | all-to-all | bytes 1048576 | tf_op jit(solution)/shard_map/spread_xy/all_to_all | solution.py:38
  140.8 8.2 %collective-permute-start.5 = (bf16[256,1024]{1,0:T(8,128)(2,1)S(1)}, bf16[256,1024]{1,0:T(8,128)(2,1)S(1)}, u32[]{:S(2)}, u32[]{:S(2)}) collective-permute-start(bf16[256,1024]{1,0:T(8,128)(2,1)S(1)} %bitcast.18), channel_id=1, source_target_pairs={{0,1},{1,0},{2,3},{3,2},{4,5},{5,4},{6,7},{7,6},{8,9},{9,8},{10,11... | collective-permute-start | bytes 1572872 | tf_op jit(solution)/shard_map/spread_core/ppermute | solution.py:255
  149.0 0.4 fusion.basis_ref
  149.4 1.1 collective-permute-done.5.other_ref
  150.5 1.2 decode.1
  (29 shorter events, 0.5 us)
Async XLA Ops:
  0.6 15.5 %copy-start = (bf16[256,512]{1,0:T(8,128)(2,1)S(1)}, bf16[256,512]{1,0:T(8,128)(2,1)}, u32[]{:S(2)}) copy-start(bf16[256,512]{1,0:T(8,128)(2,1)} %param.11) | copy-start | bytes 786436
  0.7 1.6 %copy-start.1 = (bf16[128,8192]{1,0:T(8,128)(2,1)S(1)}, bf16[128,8192]{1,0:T(8,128)(2,1)}, u32[]{:S(2)}) copy-start(bf16[128,8192]{1,0:T(8,128)(2,1)} %tokens_ref.1) | copy-start | bytes 6291460
  2.3 0.9 copy-start.2
  3.2 12.9 %copy-start.6 = (s32[512]{0:T(512)S(1)}, s32[512]{0:T(512)}, u32[]{:S(2)}) copy-start(s32[512]{0:T(512)} %constant.43) | copy-start | bytes 6148
  5.3 44.3 %collective-permute-start.1 = (bf16[128,3072]{1,0:T(8,128)(2,1)}, bf16[128,3072]{1,0:T(8,128)(2,1)S(1)}, u32[]{:S(2)}, u32[]{:S(2)}) collective-permute-start(bf16[128,3072]{1,0:T(8,128)(2,1)} %get-tuple-element.23.refs_1_), channel_id=1, source_target_pairs={{0,32},{32,64},{64,96},{96,0},{1,33},{33,65},{65,97},{97,1},{2,34}... | collective-permute-start | bytes 2359304 | tf_op jit(solution)/shard_map/tokens_x/ppermute | solution.py:219
  9.3 40.3 %collective-permute-start.2 = (bf16[128,3072]{1,0:T(8,128)(2,1)}, bf16[128,3072]{1,0:T(8,128)(2,1)S(1)}, u32[]{:S(2)}, u32[]{:S(2)}) collective-permute-start(bf16[128,3072]{1,0:T(8,128)(2,1)} %get-tuple-element.24), channel_id=1, source_target_pairs={{0,96},{32,0},{64,32},{96,64},{1,97},{33,1},{65,33},{97,65},{2,98}... | collective-permute-start | bytes 2359304 | tf_op jit(solution)/shard_map/tokens_x/ppermute | solution.py:219
  12.5 37.1 %collective-permute-start.3 = (bf16[128,3072]{1,0:T(8,128)(2,1)}, bf16[128,3072]{1,0:T(8,128)(2,1)S(1)}, u32[]{:S(2)}, u32[]{:S(2)}) collective-permute-start(bf16[128,3072]{1,0:T(8,128)(2,1)} %get-tuple-element.25), channel_id=1, source_target_pairs={{0,64},{32,96},{64,0},{96,32},{1,65},{33,97},{65,1},{97,33},{2,66}... | collective-permute-start | bytes 2359304 | tf_op jit(solution)/shard_map/tokens_x/ppermute | solution.py:219
  16.4 7.8 %collective-permute-start = (bf16[32,256]{1,0:T(8,128)(2,1)S(1)}, bf16[32,256]{1,0:T(8,128)(2,1)S(1)}, u32[]{:S(2)}, u32[]{:S(2)}) collective-permute-start(bf16[32,256]{1,0:T(8,128)(2,1)S(1)} %broadcast_select_fusion), channel_id=1, source_target_pairs={{0,1},{1,0},{2,3},{3,2},{4,5},{5,4},{6,7},{7,6},{8,9},{9,8},{10,11... | collective-permute-start | bytes 49160 | tf_op jit(solution)/shard_map/gather/cond/branch_1_fun/gather_core/ppermute | solution.py:224
  49.6 7.3 %copy-start.5 = (bf16[512,256]{1,0:T(8,128)(2,1)S(1)}, bf16[512,256]{1,0:T(8,128)(2,1)}, u32[]{:S(2)}) copy-start(bf16[512,256]{1,0:T(8,128)(2,1)} %get-tuple-element.29.refs_4_) | copy-start | bytes 786436
  49.8 26.1 %collective-permute-start.4 = (bf16[512,3072]{1,0:T(8,128)(2,1)S(1)}, bf16[512,3072]{1,0:T(8,128)(2,1)S(1)}, u32[]{:S(2)}, u32[]{:S(2)}) collective-permute-start(bf16[512,3072]{1,0:T(8,128)(2,1)S(1)} %join.3.refs_0_), channel_id=1, source_target_pairs={{0,1},{1,0},{2,3},{3,2},{4,5},{5,4},{6,7},{7,6},{8,9},{9,8},{10,11... | collective-permute-start | bytes 9437192 | tf_op jit(solution)/shard_map/tokens_core/ppermute | solution.py:240
  92.4 21.1 %copy-start.3 = (f32[1,1024]{1,0:T(1,128)S(1)}, f32[1,1024]{1,0:T(1,128)}, u32[]{:S(2)}) copy-start(f32[1,1024]{1,0:T(1,128)} %first_hbm.1) | copy-start | bytes 12292
  92.4 21.1 %copy-start.4 = (f32[1,1024]{1,0:T(1,128)S(1)}, f32[1,1024]{1,0:T(1,128)}, u32[]{:S(2)}) copy-start(f32[1,1024]{1,0:T(1,128)} %second_hbm.1) | copy-start | bytes 12292
  140.8 9.7 %collective-permute-start.5 = (bf16[256,1024]{1,0:T(8,128)(2,1)S(1)}, bf16[256,1024]{1,0:T(8,128)(2,1)S(1)}, u32[]{:S(2)}, u32[]{:S(2)}) collective-permute-start(bf16[256,1024]{1,0:T(8,128)(2,1)S(1)} %bitcast.18), channel_id=1, source_target_pairs={{0,1},{1,0},{2,3},{3,2},{4,5},{5,4},{6,7},{7,6},{8,9},{9,8},{10,11... | collective-permute-start | bytes 1572872 | tf_op jit(solution)/shard_map/spread_core/ppermute | solution.py:255

commit v12 on v11

--- a/solution.py
+++ b/solution.py
@@ -209,7 +209,7 @@
 
 
 def local(normed_input, value_cotangent, basis, first_moment, second_moment):
-    x_at, z_lo_at, core_at = (lax.axis_index(a) for a in ("x", "z_lo", "core"))
+    x_at, core_at = (lax.axis_index(a) for a in ("x", "core"))
     swap = [(0, 1), (1, 0)]
     place = np.arange(RANK, dtype=np.int32)
     by_core = owner_row(place >> 8, place >> 4 & 15, place & 15)
@@ -224,10 +224,10 @@
             theirs = lax.ppermute(jnp.where(core_at == 0, high, low), "core", swap)
             chunk = jnp.where(core_at == (x_at & 1), jnp.where(core_at == 0, low, high), theirs)
         with jax.named_scope("gather_z"):
-            return spread(chunk, Z, 16).reshape(512, 256)
+            return spread(chunk, "z_hi", 4).reshape(512, 256)
 
     with jax.named_scope("gather"):
-        rows = lax.dynamic_slice_in_dim(basis, (x_at >> 1) * 128 + z_lo_at * 32, 32, 0)
+        rows = lax.dynamic_slice_in_dim(basis, (x_at >> 1) * 128, 128, 0)
         rows = reorder(rows, by_core)
         line = lax.cond(
             x_at < 4, gather, lambda rows: jnp.zeros((512, 256), jnp.bfloat16),

time: 152 us -> 152 us (level)
  starting transfers between devices: 33 us -> 28.3 us
  blocking collectives: 105 us -> 108 us
    ppermute x1, starting transfers between devices: 7.04 us -> 2.35 us  [local(): held = [held, lax.ppermute(held, 'core', swap)]]
    all_to_all x6, blocking collectives: 105 us -> 108 us  [exchange(): return lax.all_to_all(blocks, axes, 0, 0, tiled=True)]
  transfers between devices with their start and end apart: 6 -> 6, of which waited for: 2 -> 2; matrix products, arithmetic and copies ran while one was open for 1% -> 2% of each run, Pallas kernels for 0% -> 0%
where the time goes in v12:
time: 152 us
  blocking collectives  108 us (71%)
  starting transfers between devices  28.3 us (19%)
  Pallas kernels  6.73 us (4%)
  local copies, waits for them, and re-layouts  2.78 us (2%)
  waiting for transfers between devices  2.36 us (2%)
  other arithmetic  1.78 us (1%)
    all_to_all x6, blocking collectives, exchange(): return lax.all_to_all(blocks, axes, 0, 0, tiled=True)  108 us
    ppermute x3, starting transfers between devices, local(): lax.ppermute(packed[k], 'x', [(i, (i + k) % 4) for i in range(4)])  10.8 us
    ppermute x1, starting transfers between devices, local(): other = lax.ppermute(own, 'core', swap)  8.2 us
    ppermute x1, starting transfers between devices, gather(): theirs = lax.ppermute(jnp.where(core_at == 0, high, low), 'core', swap)  6.99 us
  transfers between devices with their start and end apart: 6, of which 2 were waited for; matrix products, arithmetic and copies ran while one was open for 2% of the time, Pallas kernels for 0%

profile of v12, /device:TPU:1, one launch (start us, length us, event | category | flops | bytes accessed | tf_op | source)
XLA Modules:
  0.0 151.8 jit_solution(5654083657020313823)
XLA Ops:
  0.7 1.6 %copy-done.1 = bf16[128,8192]{1,0:T(8,128)(2,1)S(1)} copy-done((bf16[128,8192]{1,0:T(8,128)(2,1)S(1)}, bf16[128,8192]{1,0:T(8,128)(2,1)}, u32[]{:S(2)}) %copy-start.1) | copy-done | bytes 2097176
  2.3 0.9 copy-done.2
  3.2 2.1 %pack.1 = (bf16[128,3072]{1,0:T(8,128)(2,1)S(1)}, bf16[128,3072]{1,0:T(8,128)(2,1)}, bf16[128,3072]{1,0:T(8,128)(2,1)}, bf16[128,3072]{1,0:T(8,128)(2,1)}) custom-call(s32[1]{0:T(128)} %bitcast.1.x_ref, bf16[128,8192]{1,0:T(8,128)(2,1)S(1)} %copy-done.1, bf16[128,1024]{1,0:T(8,128)(2,1)S(1)} %copy-done.2), custom_call_target="tpu_custom_call" | custom-call | bytes 6291456 | tf_op jit(solution)/shard_map/tokens_x/pack/pallas_call | solution.py:58
  5.3 3.9 %collective-permute-start.1 = (bf16[128,3072]{1,0:T(8,128)(2,1)}, bf16[128,3072]{1,0:T(8,128)(2,1)S(1)}, u32[]{:S(2)}, u32[]{:S(2)}) collective-permute-start(bf16[128,3072]{1,0:T(8,128)(2,1)} %get-tuple-element.23.refs_1_), channel_id=1, source_target_pairs={{0,32},{32,64},{64,96},{96,0},{1,33},{33,65},{65,97},{97,1},{2,34}... | collective-permute-start | bytes 2359304 | tf_op jit(solution)/shard_map/tokens_x/ppermute | solution.py:219
  9.3 3.2 %collective-permute-start.2 = (bf16[128,3072]{1,0:T(8,128)(2,1)}, bf16[128,3072]{1,0:T(8,128)(2,1)S(1)}, u32[]{:S(2)}, u32[]{:S(2)}) collective-permute-start(bf16[128,3072]{1,0:T(8,128)(2,1)} %get-tuple-element.24), channel_id=1, source_target_pairs={{0,96},{32,0},{64,32},{96,64},{1,97},{33,1},{65,33},{97,65},{2,98}... | collective-permute-start | bytes 2359304 | tf_op jit(solution)/shard_map/tokens_x/ppermute | solution.py:219
  12.5 3.6 %collective-permute-start.3 = (bf16[128,3072]{1,0:T(8,128)(2,1)}, bf16[128,3072]{1,0:T(8,128)(2,1)S(1)}, u32[]{:S(2)}, u32[]{:S(2)}) collective-permute-start(bf16[128,3072]{1,0:T(8,128)(2,1)} %get-tuple-element.25), channel_id=1, source_target_pairs={{0,64},{32,96},{64,0},{96,32},{1,65},{33,97},{65,1},{97,33},{2,66}... | collective-permute-start | bytes 2359304 | tf_op jit(solution)/shard_map/tokens_x/ppermute | solution.py:219
  16.5 40.2 %conditional.1 = (bf16[512,256]{1,0:T(8,128)(2,1)}) conditional(s32[]{:T(128)} %convert_element_type.19, () %tuple.14, (s32[]{:T(128)}, s32[]{:T(128)}, bf16[128,512]{1,0:T(8,128)(2,1)S(1)}) %tuple.15), branch_computations={%region_0.0_spmd, %region_1.2_spmd} | conditional | flops 98307 | bytes 1572945 | solution.py:232
  16.5 0.6 broadcast_select_fusion
  17.1 7.0 %collective-permute-start = (bf16[128,256]{1,0:T(8,128)(2,1)}, bf16[128,256]{1,0:T(8,128)(2,1)}, u32[]{:S(2)}, u32[]{:S(2)}) collective-permute-start(bf16[128,256]{1,0:T(8,128)(2,1)} %broadcast_select_fusion), channel_id=1, source_target_pairs={{0,1},{1,0},{2,3},{3,2},{4,5},{5,4},{6,7},{7,6},{8,9},{9,8},{10,11... | collective-permute-start | bytes 196616 | tf_op jit(solution)/shard_map/gather/cond/branch_1_fun/gather_core/ppermute | solution.py:224
  24.1 1.2 collective-permute-done
  25.3 0.9 select_select_fusion
  26.2 30.4 %all_to_all.29 = bf16[4,128,256]{2,1,0:T(8,128)(2,1)} all-to-all(bf16[4,128,256]{2,1,0:T(8,128)(2,1)S(1)} %broadcast_in_dim.1), channel_id=1, replica_groups=mesh['z_lo'=4,'x'=4,'y'=4,'z_hi'=4,'core'=2] {'z_hi'}, dimensions={0} | all-to-all | bytes 524288 | tf_op jit(solution)/shard_map/gather/cond/branch_1_fun/gather_z/all_to_all | solution.py:38
  56.9 2.3 %collective-permute-start.4 = (bf16[512,3072]{1,0:T(8,128)(2,1)S(1)}, bf16[512,3072]{1,0:T(8,128)(2,1)S(1)}, u32[]{:S(2)}, u32[]{:S(2)}) collective-permute-start(bf16[512,3072]{1,0:T(8,128)(2,1)S(1)} %join.3.refs_0_), channel_id=1, source_target_pairs={{0,1},{1,0},{2,3},{3,2},{4,5},{5,4},{6,7},{7,6},{8,9},{9,8},{10,11... | collective-permute-start | bytes 9437192 | tf_op jit(solution)/shard_map/tokens_core/ppermute | solution.py:240
  59.3 18.9 %all_to_all.30 = bf16[4,512,256]{2,1,0:T(8,128)(2,1)S(1)} all-to-all(bf16[4,512,256]{2,1,0:T(8,128)(2,1)S(1)} %broadcast_in_dim.19), channel_id=1, replica_groups=mesh['z_lo'=4,'x'=4,'y'=4,'z_hi'=4,'core'=2] {'y'}, dimensions={0} | all-to-all | bytes 2097152 | tf_op jit(solution)/shard_map/gather_y/all_to_all | solution.py:38
  78.2 2.6 %project.1 = f32[16,9,16,128]{3,2,1,0:T(8,128)S(1)} custom-call(bf16[512,3072]{1,0:T(8,128)(2,1)S(1)} %join.3.refs_0_, bf16[512,3072]{1,0:T(8,128)(2,1)S(1)} %collective-permute-done.4.refs_1_, bf16[2048,256]{1,0:T(8,128)(2,1)S(1)} %bitcast.17), custom_call_target="tpu_custom_call" | custom-call | flops 2147483648 | bytes 8388608 | tf_op jit(solution)/shard_map/project/project/pallas_call | solution.py:126
  80.8 13.7 %all_to_all.31 = f16[16,9,16,128]{3,2,1,0:T(8,128)(2,1)S(1)} all-to-all(f16[16,9,16,128]{3,2,1,0:T(8,128)(2,1)S(1)} %convert_element_type.21), channel_id=1, replica_groups=mesh['z_lo'=4,'x'=4,'y'=4,'z_hi'=4,'core'=2] {'x','y'}, dimensions={0} | all-to-all | bytes 1179648 | tf_op jit(solution)/shard_map/reduce_xy/all_to_all | solution.py:38
  94.9 18.7 %all_to_all.32.parts_ref = f32[16,8,128]{2,1,0:T(8,128)S(1)} all-to-all(f32[16,8,128]{2,1,0:T(8,128)S(1)} %bitcast.21), channel_id=1, replica_groups=mesh['z_lo'=4,'x'=4,'y'=4,'z_hi'=4,'core'=2] {'z_hi','z_lo'}, dimensions={0} | all-to-all | bytes 131072 | tf_op jit(solution)/shard_map/reduce_z/all_to_all | solution.py:38
  113.6 0.7 adam.1
  114.2 14.3 %all_to_all.33 = bf16[16,8,128]{2,1,0:T(8,128)(2,1)S(1)} all-to-all(bf16[16,8,128]{2,1,0:T(8,128)(2,1)S(1)} %broadcast_in_dim.34), channel_id=1, replica_groups=mesh['z_lo'=4,'x'=4,'y'=4,'z_hi'=4,'core'=2] {'z_hi','z_lo'}, dimensions={0} | all-to-all | bytes 65536 | tf_op jit(solution)/shard_map/spread_z/all_to_all | solution.py:38
  128.6 12.2 %all_to_all.34 = bf16[16,16,1024]{2,1,0:T(8,128)(2,1)S(1)} all-to-all(bf16[16,16,1024]{2,1,0:T(8,128)(2,1)S(1)} %broadcast_in_dim.36), channel_id=1, replica_groups=mesh['z_lo'=4,'x'=4,'y'=4,'z_hi'=4,'core'=2] {'x','y'}, dimensions={0} | all-to-all | bytes 1048576 | tf_op jit(solution)/shard_map/spread_xy/all_to_all | solution.py:38
  140.8 8.2 %collective-permute-start.5 = (bf16[256,1024]{1,0:T(8,128)(2,1)S(1)}, bf16[256,1024]{1,0:T(8,128)(2,1)S(1)}, u32[]{:S(2)}, u32[]{:S(2)}) collective-permute-start(bf16[256,1024]{1,0:T(8,128)(2,1)S(1)} %bitcast.18), channel_id=1, source_target_pairs={{0,1},{1,0},{2,3},{3,2},{4,5},{5,4},{6,7},{7,6},{8,9},{9,8},{10,11... | collective-permute-start | bytes 1572872 | tf_op jit(solution)/shard_map/spread_core/ppermute | solution.py:255
  149.0 0.4 fusion.basis_ref
  149.4 1.1 collective-permute-done.5.other_ref
  150.5 1.2 decode.1
  (29 shorter events, 1.1 us)
Async XLA Ops:
  0.6 15.5 %copy-start = (bf16[256,512]{1,0:T(8,128)(2,1)S(1)}, bf16[256,512]{1,0:T(8,128)(2,1)}, u32[]{:S(2)}) copy-start(bf16[256,512]{1,0:T(8,128)(2,1)} %param.11) | copy-start | bytes 786436
  0.7 1.6 %copy-start.1 = (bf16[128,8192]{1,0:T(8,128)(2,1)S(1)}, bf16[128,8192]{1,0:T(8,128)(2,1)}, u32[]{:S(2)}) copy-start(bf16[128,8192]{1,0:T(8,128)(2,1)} %tokens_ref.1) | copy-start | bytes 6291460
  2.3 0.9 copy-start.2
  3.2 12.9 %copy-start.6 = (s32[512]{0:T(512)S(1)}, s32[512]{0:T(512)}, u32[]{:S(2)}) copy-start(s32[512]{0:T(512)} %constant.37) | copy-start | bytes 6148
  5.3 51.3 %collective-permute-start.1 = (bf16[128,3072]{1,0:T(8,128)(2,1)}, bf16[128,3072]{1,0:T(8,128)(2,1)S(1)}, u32[]{:S(2)}, u32[]{:S(2)}) collective-permute-start(bf16[128,3072]{1,0:T(8,128)(2,1)} %get-tuple-element.23.refs_1_), channel_id=1, source_target_pairs={{0,32},{32,64},{64,96},{96,0},{1,33},{33,65},{65,97},{97,1},{2,34}... | collective-permute-start | bytes 2359304 | tf_op jit(solution)/shard_map/tokens_x/ppermute | solution.py:219
  9.3 47.4 %collective-permute-start.2 = (bf16[128,3072]{1,0:T(8,128)(2,1)}, bf16[128,3072]{1,0:T(8,128)(2,1)S(1)}, u32[]{:S(2)}, u32[]{:S(2)}) collective-permute-start(bf16[128,3072]{1,0:T(8,128)(2,1)} %get-tuple-element.24), channel_id=1, source_target_pairs={{0,96},{32,0},{64,32},{96,64},{1,97},{33,1},{65,33},{97,65},{2,98}... | collective-permute-start | bytes 2359304 | tf_op jit(solution)/shard_map/tokens_x/ppermute | solution.py:219
  12.5 44.2 %collective-permute-start.3 = (bf16[128,3072]{1,0:T(8,128)(2,1)}, bf16[128,3072]{1,0:T(8,128)(2,1)S(1)}, u32[]{:S(2)}, u32[]{:S(2)}) collective-permute-start(bf16[128,3072]{1,0:T(8,128)(2,1)} %get-tuple-element.25), channel_id=1, source_target_pairs={{0,64},{32,96},{64,0},{96,32},{1,65},{33,97},{65,1},{97,33},{2,66}... | collective-permute-start | bytes 2359304 | tf_op jit(solution)/shard_map/tokens_x/ppermute | solution.py:219
  17.1 8.2 %collective-permute-start = (bf16[128,256]{1,0:T(8,128)(2,1)}, bf16[128,256]{1,0:T(8,128)(2,1)}, u32[]{:S(2)}, u32[]{:S(2)}) collective-permute-start(bf16[128,256]{1,0:T(8,128)(2,1)} %broadcast_select_fusion), channel_id=1, source_target_pairs={{0,1},{1,0},{2,3},{3,2},{4,5},{5,4},{6,7},{7,6},{8,9},{9,8},{10,11... | collective-permute-start | bytes 196616 | tf_op jit(solution)/shard_map/gather/cond/branch_1_fun/gather_core/ppermute | solution.py:224
  56.7 2.6 %copy-start.5 = (bf16[512,256]{1,0:T(8,128)(2,1)S(1)}, bf16[512,256]{1,0:T(8,128)(2,1)}, u32[]{:S(2)}) copy-start(bf16[512,256]{1,0:T(8,128)(2,1)} %get-tuple-element.29.refs_4_) | copy-start | bytes 786436
  56.9 21.3 %collective-permute-start.4 = (bf16[512,3072]{1,0:T(8,128)(2,1)S(1)}, bf16[512,3072]{1,0:T(8,128)(2,1)S(1)}, u32[]{:S(2)}, u32[]{:S(2)}) collective-permute-start(bf16[512,3072]{1,0:T(8,128)(2,1)S(1)} %join.3.refs_0_), channel_id=1, source_target_pairs={{0,1},{1,0},{2,3},{3,2},{4,5},{5,4},{6,7},{7,6},{8,9},{9,8},{10,11... | collective-permute-start | bytes 9437192 | tf_op jit(solution)/shard_map/tokens_core/ppermute | solution.py:240
  94.7 18.9 %copy-start.3 = (f32[1,1024]{1,0:T(1,128)S(1)}, f32[1,1024]{1,0:T(1,128)}, u32[]{:S(2)}) copy-start(f32[1,1024]{1,0:T(1,128)} %first_hbm.1) | copy-start | bytes 12292
  94.7 18.9 %copy-start.4 = (f32[1,1024]{1,0:T(1,128)S(1)}, f32[1,1024]{1,0:T(1,128)}, u32[]{:S(2)}) copy-start(f32[1,1024]{1,0:T(1,128)} %second_hbm.1) | copy-start | bytes 12292
  140.8 9.7 %collective-permute-start.5 = (bf16[256,1024]{1,0:T(8,128)(2,1)S(1)}, bf16[256,1024]{1,0:T(8,128)(2,1)S(1)}, u32[]{:S(2)}, u32[]{:S(2)}) collective-permute-start(bf16[256,1024]{1,0:T(8,128)(2,1)S(1)} %bitcast.18), channel_id=1, source_target_pairs={{0,1},{1,0},{2,3},{3,2},{4,5},{5,4},{6,7},{7,6},{8,9},{9,8},{10,11... | collective-permute-start | bytes 1572872 | tf_op jit(solution)/shard_map/spread_core/ppermute | solution.py:255

commit v13 on v11

--- a/solution.py
+++ b/solution.py
@@ -65,7 +65,7 @@
         ],
         out_specs=[pl.BlockSpec((rows, QUARTER + KVW), lambda i: (i, 0))] * 4,
         out_shape=[jax.ShapeDtypeStruct((128, QUARTER + KVW), jnp.bfloat16)] * 4,
-        compiler_params=pltpu.CompilerParams(vmem_limit_bytes=32 * 2**20),
+        compiler_params=pltpu.CompilerParams(vmem_limit_bytes=60 * 2**20),
         cost_estimate=pl.CostEstimate(flops=0, bytes_accessed=6 * 2**20, transcendentals=0),
         name="pack",
     )(x_at[None], tokens, cotangent)
@@ -218,20 +218,20 @@
         pieces = [packed[0]] + [
             lax.ppermute(packed[k], "x", [(i, (i + k) % 4) for i in range(4)]) for k in (1, 3, 2)
         ]
-    def gather(rows):
-        with jax.named_scope("gather_core"):
-            low, high = rows[:, :256], rows[:, 256:]
-            theirs = lax.ppermute(jnp.where(core_at == 0, high, low), "core", swap)
-            chunk = jnp.where(core_at == (x_at & 1), jnp.where(core_at == 0, low, high), theirs)
+    with jax.named_scope("gather_core"):
+        rows = lax.dynamic_slice_in_dim(basis, (x_at >> 1) * 128 + z_lo_at * 32, 32, 0)
+        rows = reorder(rows, by_core)
+        low, high = rows[:, :256], rows[:, 256:]
+        theirs = lax.ppermute(jnp.where(core_at == 0, high, low), "core", swap)
+        chunk = jnp.where(core_at == (x_at & 1), jnp.where(core_at == 0, low, high), theirs)
+
+    def gather(chunk):
         with jax.named_scope("gather_z"):
             return spread(chunk, Z, 16).reshape(512, 256)
 
     with jax.named_scope("gather"):
-        rows = lax.dynamic_slice_in_dim(basis, (x_at >> 1) * 128 + z_lo_at * 32, 32, 0)
-        rows = reorder(rows, by_core)
         line = lax.cond(
-            x_at < 4, gather, lambda rows: jnp.zeros((512, 256), jnp.bfloat16),
-            join([rows], packed[1]),
+            x_at < 4, gather, lambda chunk: jnp.zeros((512, 256), jnp.bfloat16), chunk
         )
     with jax.named_scope("gather_y"):
         whole = spread(line, "y", 4).reshape(QUARTER, 256)

time: 152 us -> 152 us (level)
  local copies, waits for them, and re-layouts: 2.79 us -> 0.22 us
  Pallas kernels: 6.73 us -> 8.93 us
    unnamed x15 -> x13, local copies, waits for them, and re-layouts: 2.61 us -> 0.04 us
    pallas_call x1, Pallas kernels: 2.07 us -> 4.27 us  [pack(): pl.pallas_call(pack_kernel, grid=(128 // rows,), in_specs=[pl.BlockSpec(m...]
where the time goes in v13:
time: 152 us
  blocking collectives  105 us (69%)
  starting transfers between devices  33.1 us (22%)
  Pallas kernels  8.93 us (6%)
  waiting for transfers between devices  1.97 us (1%)
    all_to_all x6, blocking collectives, exchange(): return lax.all_to_all(blocks, axes, 0, 0, tiled=True)  105 us
    ppermute x3, starting transfers between devices, local(): lax.ppermute(packed[k], 'x', [(i, (i + k) % 4) for i in range(4)])  10.9 us
    ppermute x1, starting transfers between devices, local(): other = lax.ppermute(own, 'core', swap)  8.21 us
    ppermute x1, starting transfers between devices, local(): held = [held, lax.ppermute(held, 'core', swap)]  7.04 us
    ppermute x1, starting transfers between devices, local(): theirs = lax.ppermute(jnp.where(core_at == 0, high, low), 'core', swap)  7 us
    pallas_call x1, Pallas kernels, pack(): pl.pallas_call(pack_kernel, grid=(128 // rows,), in_specs=[pl.BlockSpec(m...  4.27 us
  transfers between devices with their start and end apart: 6, of which 2 were waited for; matrix products, arithmetic and copies ran while one was open for 1% of the time, Pallas kernels for 0%

profile of v13, /device:TPU:1, one launch (start us, length us, event | category | flops | bytes accessed | tf_op | source)
XLA Modules:
  0.0 151.5 jit_solution(9159796072153546377)
XLA Ops:
  0.7 4.3 %pack.1 = (bf16[128,3072]{1,0:T(8,128)(2,1)}, bf16[128,3072]{1,0:T(8,128)(2,1)}, bf16[128,3072]{1,0:T(8,128)(2,1)}, bf16[128,3072]{1,0:T(8,128)(2,1)}) custom-call(s32[1]{0:T(128)} %bitcast.1.x_ref, bf16[128,8192]{1,0:T(8,128)(2,1)} %tokens_ref.1, bf16[128,1024]{1,0:T(8,128)(2,1)} %cotangent_ref.1), custom_call_target="tpu_custom_call" | custom-call | bytes 6291456 | tf_op jit(solution)/shard_map/tokens_x/pack/pallas_call | solution.py:58
  4.9 4.1 %collective-permute-start = (bf16[128,3072]{1,0:T(8,128)(2,1)}, bf16[128,3072]{1,0:T(8,128)(2,1)S(1)}, u32[]{:S(2)}, u32[]{:S(2)}) collective-permute-start(bf16[128,3072]{1,0:T(8,128)(2,1)} %get-tuple-element.38), channel_id=1, source_target_pairs={{0,32},{32,64},{64,96},{96,0},{1,33},{33,65},{65,97},{97,1},{2,34}... | collective-permute-start | bytes 2359304 | tf_op jit(solution)/shard_map/tokens_x/ppermute | solution.py:219
  9.0 3.2 %collective-permute-start.1 = (bf16[128,3072]{1,0:T(8,128)(2,1)}, bf16[128,3072]{1,0:T(8,128)(2,1)S(1)}, u32[]{:S(2)}, u32[]{:S(2)}) collective-permute-start(bf16[128,3072]{1,0:T(8,128)(2,1)} %get-tuple-element.39), channel_id=1, source_target_pairs={{0,96},{32,0},{64,32},{96,64},{1,97},{33,1},{65,33},{97,65},{2,98}... | collective-permute-start | bytes 2359304 | tf_op jit(solution)/shard_map/tokens_x/ppermute | solution.py:219
  12.2 3.6 %collective-permute-start.2 = (bf16[128,3072]{1,0:T(8,128)(2,1)}, bf16[128,3072]{1,0:T(8,128)(2,1)S(1)}, u32[]{:S(2)}, u32[]{:S(2)}) collective-permute-start(bf16[128,3072]{1,0:T(8,128)(2,1)} %get-tuple-element.40), channel_id=1, source_target_pairs={{0,64},{32,96},{64,0},{96,32},{1,65},{33,97},{65,1},{97,33},{2,66}... | collective-permute-start | bytes 2359304 | tf_op jit(solution)/shard_map/tokens_x/ppermute | solution.py:219
  15.9 0.3 convolution_convert_fusion.1
  16.2 7.0 %collective-permute-start.3 = (bf16[32,256]{1,0:T(8,128)(2,1)S(1)}, bf16[32,256]{1,0:T(8,128)(2,1)S(1)}, u32[]{:S(2)}, u32[]{:S(2)}) collective-permute-start(bf16[32,256]{1,0:T(8,128)(2,1)S(1)} %get-tuple-element.44), channel_id=1, source_target_pairs={{0,1},{1,0},{2,3},{3,2},{4,5},{5,4},{6,7},{7,6},{8,9},{9,8},{10,11... | collective-permute-start | bytes 49160 | tf_op jit(solution)/shard_map/gather_core/ppermute | solution.py:225
  23.2 0.8 collective-permute-done.3
  24.0 25.3 %conditional.1 = (bf16[512,256]{1,0:T(8,128)(2,1)}) conditional(s32[]{:T(128)} %convert_element_type.19, () %tuple.15, (s32[]{:T(128)}, s32[]{:T(128)}, pred[32,256]{1,0:T(8,128)(4,1)S(1)}, bf16[32,256]{1,0:T(8,128)(2,1)S(1)}, bf16[32,256]{1,0:T(8,128)(2,1)S(1)}, /*index=5*/bf16[32,256]{1,0:T(8,128)(2,1)S(1)}) %tuple.16), branch_computations={%region_0.1_spmd, %region_1.2_spmd} | conditional | flops 16386 | bytes 876574 | solution.py:233
  24.1 25.3 %all_to_all.29 = bf16[16,32,256]{2,1,0:T(8,128)(2,1)} all-to-all(bf16[16,32,256]{2,1,0:T(8,128)(2,1)S(1)} %broadcast_in_dim.1), channel_id=1, replica_groups=mesh['z_lo'=4,'x'=4,'y'=4,'z_hi'=4,'core'=2] {'z_hi','z_lo'}, dimensions={0} | all-to-all | bytes 524288 | tf_op jit(solution)/shard_map/gather/cond/branch_1_fun/gather_z/all_to_all | solution.py:38
  49.4 0.2 join.1.refs_0_
  49.6 7.0 %collective-permute-start.4 = (bf16[512,3072]{1,0:T(8,128)(2,1)S(1)}, bf16[512,3072]{1,0:T(8,128)(2,1)S(1)}, u32[]{:S(2)}, u32[]{:S(2)}) collective-permute-start(bf16[512,3072]{1,0:T(8,128)(2,1)S(1)} %join.1.refs_0_), channel_id=1, source_target_pairs={{0,1},{1,0},{2,3},{3,2},{4,5},{5,4},{6,7},{7,6},{8,9},{9,8},{10,11... | collective-permute-start | bytes 9437192 | tf_op jit(solution)/shard_map/tokens_core/ppermute | solution.py:240
  56.7 18.9 %all_to_all.30 = bf16[4,512,256]{2,1,0:T(8,128)(2,1)S(1)} all-to-all(bf16[4,512,256]{2,1,0:T(8,128)(2,1)S(1)} %broadcast_in_dim.19), channel_id=1, replica_groups=mesh['z_lo'=4,'x'=4,'y'=4,'z_hi'=4,'core'=2] {'y'}, dimensions={0} | all-to-all | bytes 2097152 | tf_op jit(solution)/shard_map/gather_y/all_to_all | solution.py:38
  75.6 2.6 %project.1 = f32[16,9,16,128]{3,2,1,0:T(8,128)S(1)} custom-call(bf16[512,3072]{1,0:T(8,128)(2,1)S(1)} %join.1.refs_0_, bf16[512,3072]{1,0:T(8,128)(2,1)S(1)} %collective-permute-done.4.refs_1_, bf16[2048,256]{1,0:T(8,128)(2,1)S(1)} %bitcast.17), custom_call_target="tpu_custom_call" | custom-call | flops 2147483648 | bytes 8388608 | tf_op jit(solution)/shard_map/project/project/pallas_call | solution.py:126
  78.3 13.8 %all_to_all.31 = f16[16,9,16,128]{3,2,1,0:T(8,128)(2,1)S(1)} all-to-all(f16[16,9,16,128]{3,2,1,0:T(8,128)(2,1)S(1)} %convert_element_type.21), channel_id=1, replica_groups=mesh['z_lo'=4,'x'=4,'y'=4,'z_hi'=4,'core'=2] {'x','y'}, dimensions={0} | all-to-all | bytes 1179648 | tf_op jit(solution)/shard_map/reduce_xy/all_to_all | solution.py:38
  92.1 0.1 convert_element_type.22
  92.2 0.1 fusion.1
  92.4 21.0 %all_to_all.32.parts_ref = f32[16,8,128]{2,1,0:T(8,128)S(1)} all-to-all(f32[16,8,128]{2,1,0:T(8,128)S(1)} %bitcast.21), channel_id=1, replica_groups=mesh['z_lo'=4,'x'=4,'y'=4,'z_hi'=4,'core'=2] {'z_hi','z_lo'}, dimensions={0} | all-to-all | bytes 131072 | tf_op jit(solution)/shard_map/reduce_z/all_to_all | solution.py:38
  113.3 0.7 adam.1
  114.0 14.3 %all_to_all.33 = bf16[16,8,128]{2,1,0:T(8,128)(2,1)S(1)} all-to-all(bf16[16,8,128]{2,1,0:T(8,128)(2,1)S(1)} %broadcast_in_dim.34), channel_id=1, replica_groups=mesh['z_lo'=4,'x'=4,'y'=4,'z_hi'=4,'core'=2] {'z_hi','z_lo'}, dimensions={0} | all-to-all | bytes 65536 | tf_op jit(solution)/shard_map/spread_z/all_to_all | solution.py:38
  128.4 12.2 %all_to_all.34 = bf16[16,16,1024]{2,1,0:T(8,128)(2,1)S(1)} all-to-all(bf16[16,16,1024]{2,1,0:T(8,128)(2,1)S(1)} %broadcast_in_dim.36), channel_id=1, replica_groups=mesh['z_lo'=4,'x'=4,'y'=4,'z_hi'=4,'core'=2] {'x','y'}, dimensions={0} | all-to-all | bytes 1048576 | tf_op jit(solution)/shard_map/spread_xy/all_to_all | solution.py:38
  140.6 8.2 %collective-permute-start.5 = (bf16[256,1024]{1,0:T(8,128)(2,1)S(1)}, bf16[256,1024]{1,0:T(8,128)(2,1)S(1)}, u32[]{:S(2)}, u32[]{:S(2)}) collective-permute-start(bf16[256,1024]{1,0:T(8,128)(2,1)S(1)} %bitcast.18), channel_id=1, source_target_pairs={{0,1},{1,0},{2,3},{3,2},{4,5},{5,4},{6,7},{7,6},{8,9},{9,8},{10,11... | collective-permute-start | bytes 1572872 | tf_op jit(solution)/shard_map/spread_core/ppermute | solution.py:255
  148.8 0.4 fusion.basis_ref
  149.2 1.1 collective-permute-done.5.other_ref
  150.3 1.2 decode.1
  (27 shorter events, 0.4 us)
Async XLA Ops:
  0.6 15.2 %copy-start = (bf16[256,512]{1,0:T(8,128)(2,1)S(1)}, bf16[256,512]{1,0:T(8,128)(2,1)}, u32[]{:S(2)}) copy-start(bf16[256,512]{1,0:T(8,128)(2,1)} %param.11) | copy-start | bytes 786436
  0.7 15.2 %copy-start.5 = (s32[512]{0:T(512)S(1)}, s32[512]{0:T(512)}, u32[]{:S(2)}) copy-start(s32[512]{0:T(512)} %constant.40) | copy-start | bytes 6148
  4.9 44.4 %copy-start.1 = (bf16[128,3072]{1,0:T(8,128)(2,1)S(1)}, bf16[128,3072]{1,0:T(8,128)(2,1)}, u32[]{:S(2)}) copy-start(bf16[128,3072]{1,0:T(8,128)(2,1)} %get-tuple-element.37.refs_0_) | copy-start | bytes 2359300
  4.9 44.4 %collective-permute-start = (bf16[128,3072]{1,0:T(8,128)(2,1)}, bf16[128,3072]{1,0:T(8,128)(2,1)S(1)}, u32[]{:S(2)}, u32[]{:S(2)}) collective-permute-start(bf16[128,3072]{1,0:T(8,128)(2,1)} %get-tuple-element.38), channel_id=1, source_target_pairs={{0,32},{32,64},{64,96},{96,0},{1,33},{33,65},{65,97},{97,1},{2,34}... | collective-permute-start | bytes 2359304 | tf_op jit(solution)/shard_map/tokens_x/ppermute | solution.py:219
  9.0 40.3 %collective-permute-start.1 = (bf16[128,3072]{1,0:T(8,128)(2,1)}, bf16[128,3072]{1,0:T(8,128)(2,1)S(1)}, u32[]{:S(2)}, u32[]{:S(2)}) collective-permute-start(bf16[128,3072]{1,0:T(8,128)(2,1)} %get-tuple-element.39), channel_id=1, source_target_pairs={{0,96},{32,0},{64,32},{96,64},{1,97},{33,1},{65,33},{97,65},{2,98}... | collective-permute-start | bytes 2359304 | tf_op jit(solution)/shard_map/tokens_x/ppermute | solution.py:219
  12.2 37.1 %collective-permute-start.2 = (bf16[128,3072]{1,0:T(8,128)(2,1)}, bf16[128,3072]{1,0:T(8,128)(2,1)S(1)}, u32[]{:S(2)}, u32[]{:S(2)}) collective-permute-start(bf16[128,3072]{1,0:T(8,128)(2,1)} %get-tuple-element.40), channel_id=1, source_target_pairs={{0,64},{32,96},{64,0},{96,32},{1,65},{33,97},{65,1},{97,33},{2,66}... | collective-permute-start | bytes 2359304 | tf_op jit(solution)/shard_map/tokens_x/ppermute | solution.py:219
  16.2 7.8 %collective-permute-start.3 = (bf16[32,256]{1,0:T(8,128)(2,1)S(1)}, bf16[32,256]{1,0:T(8,128)(2,1)S(1)}, u32[]{:S(2)}, u32[]{:S(2)}) collective-permute-start(bf16[32,256]{1,0:T(8,128)(2,1)S(1)} %get-tuple-element.44), channel_id=1, source_target_pairs={{0,1},{1,0},{2,3},{3,2},{4,5},{5,4},{6,7},{7,6},{8,9},{9,8},{10,11... | collective-permute-start | bytes 49160 | tf_op jit(solution)/shard_map/gather_core/ppermute | solution.py:225
  49.4 7.3 %copy-start.4 = (bf16[512,256]{1,0:T(8,128)(2,1)S(1)}, bf16[512,256]{1,0:T(8,128)(2,1)}, u32[]{:S(2)}) copy-start(bf16[512,256]{1,0:T(8,128)(2,1)} %get-tuple-element.47.refs_4_) | copy-start | bytes 786436
  49.6 26.1 %collective-permute-start.4 = (bf16[512,3072]{1,0:T(8,128)(2,1)S(1)}, bf16[512,3072]{1,0:T(8,128)(2,1)S(1)}, u32[]{:S(2)}, u32[]{:S(2)}) collective-permute-start(bf16[512,3072]{1,0:T(8,128)(2,1)S(1)} %join.1.refs_0_), channel_id=1, source_target_pairs={{0,1},{1,0},{2,3},{3,2},{4,5},{5,4},{6,7},{7,6},{8,9},{9,8},{10,11... | collective-permute-start | bytes 9437192 | tf_op jit(solution)/shard_map/tokens_core/ppermute | solution.py:240
  92.2 21.2 %copy-start.2 = (f32[1,1024]{1,0:T(1,128)S(1)}, f32[1,1024]{1,0:T(1,128)}, u32[]{:S(2)}) copy-start(f32[1,1024]{1,0:T(1,128)} %first_hbm.1) | copy-start | bytes 12292
  92.2 21.2 %copy-start.3 = (f32[1,1024]{1,0:T(1,128)S(1)}, f32[1,1024]{1,0:T(1,128)}, u32[]{:S(2)}) copy-start(f32[1,1024]{1,0:T(1,128)} %second_hbm.1) | copy-start | bytes 12292
  140.6 9.7 %collective-permute-start.5 = (bf16[256,1024]{1,0:T(8,128)(2,1)S(1)}, bf16[256,1024]{1,0:T(8,128)(2,1)S(1)}, u32[]{:S(2)}, u32[]{:S(2)}) collective-permute-start(bf16[256,1024]{1,0:T(8,128)(2,1)S(1)} %bitcast.18), channel_id=1, source_target_pairs={{0,1},{1,0},{2,3},{3,2},{4,5},{5,4},{6,7},{7,6},{8,9},{9,8},{10,11... | collective-permute-start | bytes 1572872 | tf_op jit(solution)/shard_map/spread_core/ppermute | solution.py:255
